TPU v7x, 256 devices: a whole 4x4x8 slice. The times are simulated.
256 devices in a mesh: ctx: 32 (over z, x_hi, core), tp: 8 (over x_lo, y).
Axes of the slice: x: 4 (x_hi: 2, x_lo: 2; x = x_hi * 2 + x_lo), y: 4, z: 8, core: 2. Of those that a mesh axis runs over, the one named last changes fastest.
Arguments:
- query_proj: bfloat16 [16384, 4096], P('ctx', 'tp'), may hold values from -6 to 6
- key_proj: bfloat16 [16384, 4096], P('ctx', 'tp'), may hold values from -6 to 6
- value_proj: bfloat16 [16384, 4096], P('ctx', 'tp'), may hold values from -6 to 6
- cotangent: bfloat16 [16384, 4096], P('ctx', 'tp'), may hold values from -6 to 6
- out_weight: bfloat16 [4096, 4096], P('tp'), may hold values from -0.09375 to 0.09375
- decay_rates: float32 [4096, 16], P('tp'), may hold values from 3.0517578e-05 to 0.1
- residues: float32 [4096, 16], P('tp'), may hold values from -1.8 to 1.8
- skip_gain: float32 [4096], P('tp'), may hold values from 0.5 to 1.5
Outputs:
- mixed: bfloat16 [16384, 4096], P('ctx', 'tp')
- grad_query: bfloat16 [16384, 4096], P('ctx', 'tp')
- grad_key: bfloat16 [16384, 4096], P('ctx', 'tp')
- grad_value: bfloat16 [16384, 4096], P('ctx', 'tp')
All inputs are finite; a program needn't handle non-finite values.
Results may differ from a plain program's by a relative error of at most 0.023.
Values may be sent and summed in bfloat16 or wider, within the bound.
No kernel may reach another device: no remote copies, remote signals or barrier semaphores. Data moves between devices by JAX's collectives and lax.ppermute only.
A program may use at most 64 MiB of HBM per device.

v0:
```python
import jax
import jax.numpy as jnp
from jax import lax
from jax.experimental import pallas as pl
from jax.experimental.pallas import tpu as pltpu
from jax.sharding import PartitionSpec as P

F32, BF16 = jnp.float32, jnp.bfloat16
ROWS, COLS, MODES, LANES = 512, 512, 16, 128
HALF = ROWS // 2
TILES = COLS // LANES
PARTS = 8
STEP = ROWS // PARTS
VMEM = pl.BlockSpec(memory_space=pltpu.VMEM)
SMEM = pl.BlockSpec(memory_space=pltpu.SMEM)


def tile_of(tile):
    return slice(tile * LANES, (tile + 1) * LANES)


def spread(ref, tile, mode):
    return jnp.broadcast_to(ref[tile, mode : mode + 1, :], (PARTS, LANES))


def ends_of(signal, ends, keep, tile, flipped):
    decay = [spread(keep, tile, m) for m in range(MODES)]

    def step(i, states):
        at = STEP - 1 - i if flipped else i
        u = signal[tile, pl.ds(at, PARTS, stride=STEP), :]
        return tuple(decay[m] * states[m] + u for m in range(MODES))

    zero = jnp.zeros((PARTS, LANES), F32)
    states = lax.fori_loop(0, STEP, step, (zero,) * MODES, unroll=4)
    for m in range(MODES):
        ends[tile, pl.ds(m, PARTS, stride=MODES), :] = states[m]


def chain(ends, starts, total, keep_piece, tile, flipped):
    state = jnp.zeros((MODES, LANES), F32)
    factor = keep_piece[tile]
    order = range(PARTS - 1, -1, -1) if flipped else range(PARTS)
    for piece in order:
        rows = slice(piece * MODES, (piece + 1) * MODES)
        starts[tile, rows, :] = state
        state = factor * state + ends[tile, rows, :]
    total[tile] = state


def whole_starts(starts, initial, begin, keep_piece, tile, flipped):
    carried = initial[tile]
    factor = keep_piece[tile]
    order = range(PARTS - 1, -1, -1) if flipped else range(PARTS)
    for piece in order:
        rows = slice(piece * MODES, (piece + 1) * MODES)
        begin[tile, rows, :] = starts[tile, rows, :] + carried
        carried = factor * carried


def responses(signal, begin, result, keep, gain, tile, flipped):
    decay = [spread(keep, tile, m) for m in range(MODES)]
    gains = [spread(gain, tile, m) for m in range(MODES)]

    def step(i, states):
        at = STEP - 1 - i if flipped else i
        u = signal[tile, pl.ds(at, PARTS, stride=STEP), :]
        states = tuple(decay[m] * states[m] + u for m in range(MODES))
        terms = [gains[m] * states[m] for m in range(MODES)]
        while len(terms) > 1:
            terms = [terms[i] + terms[i + 1] for i in range(0, len(terms), 2)]
        result[tile, pl.ds(at, PARTS, stride=STEP), :] = terms[0]
        return states

    states = tuple(begin[tile, pl.ds(m, PARTS, stride=MODES), :] for m in range(MODES))
    lax.fori_loop(0, STEP, step, states, unroll=4)


def columns(weight, place, which):
    return weight[:, pl.ds(pl.multiple_of(place[which] * COLS, COLS), COLS)]


def dot(a, b):
    return jnp.dot(a, b, preferred_element_type=F32)


def wide(value):
    return value.astype(F32)


NEAR = [(0, 0), (1, 0), (0, -1), (0, 1), (1, -1), (1, 1), (0, 2), (1, 2)]
OWN, ACROSS, BELOW, ABOVE, ACROSS_BELOW, ACROSS_ABOVE, FAR, ACROSS_FAR = range(8)
TOP, BOTTOM = slice(0, HALF), slice(HALF, ROWS)


def gate_kernel(key, value, keep, keep_piece, gated, starts, total, signal, ends):
    for tile in range(TILES):
        lanes = tile_of(tile)
        product = (wide(key[:, lanes]) * wide(value[:, lanes])).astype(BF16)
        gated[:, lanes] = product
        signal[tile] = wide(product)
        ends_of(signal, ends, keep, tile, False)
        chain(ends, starts, total, keep_piece, tile, False)


def mix_kernel(
    place, gated, starts, initial, keep, keep_piece, gain, skip, query, weight,
    summed, mixed_in, far_t, far_b, above_b, below_t, two_t, two_b,
    signal, begin, result,
):
    for tile in range(TILES):
        lanes = tile_of(tile)
        signal[tile] = wide(gated[:, lanes])
        whole_starts(starts, initial, begin, keep_piece, tile, False)
        responses(signal, begin, result, keep, gain, tile, False)
        conv = wide(result[tile].astype(BF16))
        total = conv + skip[0:1, lanes] * signal[tile]
        summed[:, lanes] = total
        mixed_in[:, lanes] = (wide(query[:, lanes]) * total).astype(BF16)
    sends = (
        (far_t, ACROSS_FAR, TOP), (far_b, ACROSS_FAR, BOTTOM),
        (above_b, ACROSS_ABOVE, BOTTOM), (below_t, ACROSS_BELOW, TOP),
        (two_t, FAR, TOP), (two_b, FAR, BOTTOM),
    )
    for out, which, rows in sends:
        out[...] = dot(mixed_in[rows, :], columns(weight, place, which)).astype(BF16)


def second_kernel(place, mixed_in, weight, got_t, got_b, out_t, out_b):
    top = dot(mixed_in[TOP, :], columns(weight, place, ACROSS_ABOVE))
    out_t[...] = (top + wide(got_t[...])).astype(BF16)
    bottom = dot(mixed_in[BOTTOM, :], columns(weight, place, ACROSS_BELOW))
    out_b[...] = (bottom + wide(got_b[...])).astype(BF16)


def third_kernel(place, mixed_in, weight, x_t, x_b, p_t, p_b, m_t, m_b, out_x, out_p, out_m):
    trios = ((out_x, ACROSS, x_t, x_b), (out_p, ABOVE, p_t, p_b), (out_m, BELOW, m_t, m_b))
    for out, which, got_t, got_b in trios:
        for rows, got in ((TOP, got_t), (BOTTOM, got_b)):
            part = dot(mixed_in[rows, :], columns(weight, place, which))
            out[rows, :] = (part + wide(got[...])).astype(BF16)


def last_kernel(place, mixed_in, weight, x, p, m, out):
    for rows in (TOP, BOTTOM):
        part = dot(mixed_in[rows, :], columns(weight, place, OWN))
        part = part + wide(x[rows, :]) + (wide(p[rows, :]) + wide(m[rows, :]))
        out[rows, :] = part.astype(BF16)


def grad_kernel(
    place, weight, own, across, below, above, ab_t, ab_b, aa_t, aa_b, far_t, far_b, af_t, af_b,
    summed, query, keep, keep_piece,
    grad_query, grad_conv, starts, total,
    acc, signal, ends,
):
    wholes = ((own, OWN), (across, ACROSS), (below, BELOW), (above, ABOVE))
    halves = {
        TOP.start: ((ab_t, ACROSS_BELOW), (aa_t, ACROSS_ABOVE), (far_t, FAR), (af_t, ACROSS_FAR)),
        BOTTOM.start: ((ab_b, ACROSS_BELOW), (aa_b, ACROSS_ABOVE), (far_b, FAR), (af_b, ACROSS_FAR)),
    }
    turned = (((1,), (1,)), ((), ()))
    for rows in (TOP, BOTTOM):
        grad = jnp.zeros((HALF, COLS), F32)
        for ref, which in wholes:
            grad += lax.dot_general(
                ref[rows, :], columns(weight, place, which), turned, preferred_element_type=F32
            )
        for ref, which in halves[rows.start]:
            grad += lax.dot_general(
                ref[...], columns(weight, place, which), turned, preferred_element_type=F32
            )
        acc[rows, :] = grad
    for tile in range(TILES):
        lanes = tile_of(tile)
        grad = acc[:, lanes]
        grad_query[:, lanes] = (grad * summed[:, lanes]).astype(BF16)
        conv = (grad * wide(query[:, lanes])).astype(BF16)
        grad_conv[:, lanes] = conv
        signal[tile] = wide(conv)
        ends_of(signal, ends, keep, tile, True)
        chain(ends, starts, total, keep_piece, tile, True)


def back_kernel(
    grad_conv, starts, initial, keep, keep_piece, gain, skip, key, value,
    grad_key, grad_value,
    signal, begin, result,
):
    for tile in range(TILES):
        lanes = tile_of(tile)
        signal[tile] = wide(grad_conv[:, lanes])
        whole_starts(starts, initial, begin, keep_piece, tile, True)
        responses(signal, begin, result, keep, gain, tile, True)
        back = wide(result[tile].astype(BF16))
        total = back + skip[0:1, lanes] * signal[tile]
        grad_key[:, lanes] = (total * wide(value[:, lanes])).astype(BF16)
        grad_value[:, lanes] = (total * wide(key[:, lanes])).astype(BF16)


def call(kernel, outs, scratch, specs, flops, moved, *args):
    return pl.pallas_call(
        kernel,
        out_shape=[jax.ShapeDtypeStruct(shape, kind) for shape, kind in outs],
        in_specs=specs,
        out_specs=[VMEM] * len(outs),
        scratch_shapes=scratch,
        cost_estimate=pl.CostEstimate(flops=flops, bytes_accessed=moved, transcendentals=0),
        compiler_params=pltpu.CompilerParams(vmem_limit_bytes=24 * 1024 * 1024),
    )(*args)


def tp_perm(move):
    return [(x * 4 + y, move(x, y)[0] % 2 * 4 + move(x, y)[1] % 4) for x in range(2) for y in range(4)]


def ctx_perm(move):
    pairs = []
    for z in range(8):
        for h in range(2):
            for c in range(2):
                to = move(z, h, c)
                pairs.append((z * 4 + h * 2 + c, to[0] % 8 * 4 + to[1] % 2 * 2 + to[2] % 2))
    return pairs


def shift_x(value):
    return lax.ppermute(value, "tp", tp_perm(lambda x, y: (x + 1, y)))


def shift_up(value):
    return lax.ppermute(value, "tp", tp_perm(lambda x, y: (x, y + 1)))


def shift_down(value):
    return lax.ppermute(value, "tp", tp_perm(lambda x, y: (x, y + 3)))


def carried_in(own, rates, flipped):
    place = lax.axis_index("ctx")
    core, high, z = place % 2, place // 2 % 2, place // 4
    if flipped:
        core, high, z = 1 - core, 1 - high, 7 - z

    def power(n):
        return jnp.exp(rates * (-float(ROWS) * n.astype(F32)))

    other = lax.ppermute(own, "ctx", ctx_perm(lambda z, h, c: (z, h, c + 1)))
    pair = power(1 - core) * own + power(core) * other
    before = jnp.where(core == 1, other, 0.0)
    other = lax.ppermute(pair, "ctx", ctx_perm(lambda z, h, c: (z, h + 1, c)))
    group = power(2 - 2 * high) * pair + power(2 * high) * other
    before = before + jnp.where(high == 1, power(core) * other, 0.0)
    window, over = group, None
    for k in (1, 2, 4):
        move = -k if flipped else k
        other = lax.ppermute(window, "ctx", ctx_perm(lambda z, h, c: (z + move, h, c)))
        other = jnp.where(z >= k, other, 0.0)
        term = power(jnp.asarray(4 * (k - 1))) * other
        over = other if over is None else over + term
        if k < 4:
            window = window + power(jnp.asarray(4 * k)) * other
    return before + power(2 * high + core) * over


def per_device(query, key, value, cotangent, weight, decay_rates, residues, skip_gain):
    at = lax.axis_index("tp")
    x, y = at // 4, at % 4
    place = jnp.stack([(x + dx) % 2 * 4 + (y + dy + 4) % 4 for dx, dy in NEAR]).astype(jnp.int32)

    def by_tile(table):
        return table.reshape(TILES, LANES, MODES).transpose(0, 2, 1)

    rates = by_tile(decay_rates)
    keep, keep_piece = jnp.exp(-rates), jnp.exp(rates * -float(STEP))
    gain = by_tile(residues) * jnp.sqrt(-jnp.expm1(-2.0 * rates))
    skip = skip_gain.reshape(1, COLS)

    across = shift_x(cotangent)
    below = shift_up(cotangent)
    above = shift_down(cotangent)
    ab_t = shift_up(across[TOP])
    aa_b = shift_down(across[BOTTOM])
    ab_b = shift_x(below[BOTTOM])
    aa_t = shift_x(above[TOP])
    far_t = shift_up(below[TOP])
    far_b = shift_down(above[BOTTOM])
    af_t = shift_up(ab_t)
    af_b = shift_down(aa_b)

    state, block, half = (TILES, MODES, LANES), (ROWS, COLS), (HALF, COLS)
    table = (TILES, PARTS * MODES, LANES)
    deep = pltpu.VMEM((TILES, ROWS, LANES), F32)
    ends = pltpu.VMEM(table, F32)
    elements = ROWS * COLS
    local, product = 40 * elements, 2 * ROWS * COLS * COLS
    gated, starts, total = call(
        gate_kernel,
        [(block, BF16), (table, F32), (state, F32)],
        [deep, ends],
        [VMEM] * 4,
        local,
        6 * elements,
        key,
        value,
        keep,
        keep_piece,
    )
    initial = carried_in(total, rates, False)
    summed, mixed_in, s_far_t, s_far_b, s_above_b, s_below_t, s_two_t, s_two_b = call(
        mix_kernel,
        [(block, F32), (block, BF16)] + [(half, BF16)] * 6,
        [deep, ends, deep],
        [SMEM] + [VMEM] * 9,
        2 * local + 3 * product,
        16 * elements,
        place,
        gated,
        starts,
        initial,
        keep,
        keep_piece,
        gain,
        skip,
        query,
        weight,
    )
    g_above_t, g_below_b = shift_up(s_far_t), shift_down(s_far_b)
    g_p_b, g_m_t = shift_x(s_above_b), shift_x(s_below_t)
    g_p_t, g_m_b = shift_up(s_two_t), shift_down(s_two_b)

    grad_query, grad_conv, back_starts, back_total = call(
        grad_kernel,
        [(block, BF16), (block, BF16), (table, F32), (state, F32)],
        [pltpu.VMEM(block, F32), deep, ends],
        [SMEM] + [VMEM] * 17,
        local + 8 * product,
        32 * elements,
        place,
        weight,
        cotangent,
        across,
        below,
        above,
        ab_t,
        ab_b,
        aa_t,
        aa_b,
        far_t,
        far_b,
        af_t,
        af_b,
        summed,
        query,
        keep,
        keep_piece,
    )
    back_initial = carried_in(back_total, rates, True)

    s_x_t, s_x_b = call(
        second_kernel,
        [(half, BF16)] * 2,
        [],
        [SMEM] + [VMEM] * 4,
        product,
        6 * elements,
        place,
        mixed_in,
        weight,
        g_above_t,
        g_below_b,
    )
    g_x_t, g_x_b = shift_up(s_x_t), shift_down(s_x_b)
    s_x, s_p, s_m = call(
        third_kernel,
        [(block, BF16)] * 3,
        [],
        [SMEM] + [VMEM] * 8,
        3 * product,
        10 * elements,
        place,
        mixed_in,
        weight,
        g_x_t,
        g_x_b,
        g_p_t,
        g_p_b,
        g_m_t,
        g_m_b,
    )
    (mixed,) = call(
        last_kernel,
        [(block, BF16)],
        [],
        [SMEM] + [VMEM] * 5,
        product,
        8 * elements,
        place,
        mixed_in,
        weight,
        shift_x(s_x),
        shift_up(s_p),
        shift_down(s_m),
    )
    grad_key, grad_value = call(
        back_kernel,
        [(block, BF16), (block, BF16)],
        [deep, ends, deep],
        [VMEM] * 9,
        2 * local,
        12 * elements,
        grad_conv,
        back_starts,
        back_initial,
        keep,
        keep_piece,
        gain,
        skip,
        key,
        value,
    )
    return mixed, grad_query, grad_key, grad_value


def solution(mesh):
    split, rows = P("ctx", "tp"), P("tp", None)
    return jax.shard_map(
        per_device,
        mesh=mesh,
        in_specs=(split, split, split, split, rows, rows, rows, P("tp")),
        out_specs=(split, split, split, split),
        check_vma=False,
    )
```

profile of v0, /device:TPU:2, one launch (start us, length us, event | category | flops | bytes accessed | tf_op | source)
XLA Modules:
  0.0 120.7 jit_solution(9833165774331492815)
XLA Ops:
  4.4 2.4 %shard_map.111 = (bf16[512,512]{1,0:T(8,128)(2,1)S(1)}, f32[4,128,128]{2,1,0:T(8,128)S(1)}, f32[4,16,128]{2,1,0:T(8,128)S(1)}) custom-call(bf16[512,512]{1,0:T(8,128)(2,1)S(1)} %copy-done.3, bf16[512,512]{1,0:T(8,128)(2,1)S(1)} %copy-done.5, f32[4,16,128]{2,1,0:T(8,128)S(1)} %get-tuple-element.69.keep, f32[4,16,128]{2,1,0:T(8,128)S(1)} %get-tuple-element.68.keep_piece), custom_call_target="tpu_custom_call" | custom-call | flops 10485760 | bytes 1572864 | tf_op jit(solution)/shard_map/pallas_call | solution.py:202
  6.8 2.4 %collective-permute-start.16 = (bf16[512,512]{1,0:T(8,128)(2,1)}, bf16[512,512]{1,0:T(8,128)(2,1)S(1)}, u32[]{:S(2)}, u32[]{:S(2)}) collective-permute-start(bf16[512,512]{1,0:T(8,128)(2,1)} %own.1), channel_id=1, source_target_pairs={{0,4},{1,5},{2,6},{3,7},{4,0},{5,1},{6,2},{7,3},{8,12},{9,13},{10,... | collective-permute-start | bytes 1572872 | tf_op jit(solution)/shard_map/ppermute | solution.py:228
  11.8 11.2 %collective-permute-done.1 = f32[4,16,128]{2,1,0:T(8,128)S(1)} collective-permute-done((f32[4,16,128]{2,1,0:T(8,128)S(1)}, f32[4,16,128]{2,1,0:T(8,128)S(1)}, u32[]{:S(2)}, u32[]{:S(2)}) %collective-permute-start.1) | collective-permute-done | bytes 32800 | tf_op jit(solution)/shard_map/ppermute | solution.py:251
  23.0 2.0 %collective-permute-start.2 = (f32[4,16,128]{2,1,0:T(8,128)S(1)}, f32[4,16,128]{2,1,0:T(8,128)S(1)}, u32[]{:S(2)}, u32[]{:S(2)}) collective-permute-start(f32[4,16,128]{2,1,0:T(8,128)S(1)} %fusion.24), channel_id=1, source_target_pairs={{0,32},{8,40},{16,48},{24,56},{32,64},{40,72},{48,80},{56,88},{64,... | collective-permute-start | bytes 98312 | tf_op jit(solution)/shard_map/ppermute | solution.py:257
  25.0 3.0 %collective-permute-start.18 = (bf16[512,512]{1,0:T(8,128)(2,1)}, bf16[512,512]{1,0:T(8,128)(2,1)S(1)}, u32[]{:S(2)}, u32[]{:S(2)}) collective-permute-start(bf16[512,512]{1,0:T(8,128)(2,1)} %own.1), channel_id=1, source_target_pairs={{0,3},{1,0},{2,1},{3,2},{4,7},{5,4},{6,5},{7,6},{8,11},{9,8},{10,9... | collective-permute-start | bytes 1572872 | tf_op jit(solution)/shard_map/ppermute | solution.py:236
  28.1 2.7 %collective-permute-done.2 = f32[4,16,128]{2,1,0:T(8,128)S(1)} collective-permute-done((f32[4,16,128]{2,1,0:T(8,128)S(1)}, f32[4,16,128]{2,1,0:T(8,128)S(1)}, u32[]{:S(2)}, u32[]{:S(2)}) %collective-permute-start.2) | collective-permute-done | bytes 32800 | tf_op jit(solution)/shard_map/ppermute | solution.py:257
  34.6 2.2 %collective-permute-start.22 = (bf16[256,512]{1,0:T(8,128)(2,1)S(1)}, bf16[256,512]{1,0:T(8,128)(2,1)S(1)}, u32[]{:S(2)}, u32[]{:S(2)}) collective-permute-start(bf16[256,512]{1,0:T(8,128)(2,1)S(1)} %get-tuple-element.52), channel_id=1, source_target_pairs={{0,3},{1,0},{2,1},{3,2},{4,7},{5,4},{6,5},{7,6},{8,11},{9,8},{10,9... | collective-permute-start | bytes 786440 | tf_op jit(solution)/shard_map/ppermute | solution.py:236
  37.3 4.3 %collective-permute-start.4 = (f32[4,16,128]{2,1,0:T(8,128)S(1)}, f32[4,16,128]{2,1,0:T(8,128)S(1)}, u32[]{:S(2)}, u32[]{:S(2)}) collective-permute-start(f32[4,16,128]{2,1,0:T(8,128)S(1)} %fusion.7), channel_id=1, source_target_pairs={{0,128},{8,136},{16,144},{24,152},{32,160},{40,168},{48,176},{56,1... | collective-permute-start | bytes 98312 | tf_op jit(solution)/shard_map/ppermute | solution.py:257
  48.9 2.9 %collective-permute-start.26 = (bf16[256,512]{1,0:T(8,128)(2,1)S(1)}, bf16[256,512]{1,0:T(8,128)(2,1)S(1)}, u32[]{:S(2)}, u32[]{:S(2)}) collective-permute-start(bf16[256,512]{1,0:T(8,128)(2,1)S(1)} %collective-permute-done.22.aa_b), channel_id=1, source_target_pairs={{0,3},{1,0},{2,1},{3,2},{4,7},{5,4},{6,5},{7,6},{8,11},{9,8},{10,9... | collective-permute-start | bytes 786440 | tf_op jit(solution)/shard_map/ppermute | solution.py:236
  51.8 2.2 %copy-done = bf16[512,4096]{1,0:T(8,128)(2,1)S(1)} copy-done((bf16[512,4096]{1,0:T(8,128)(2,1)S(1)}, bf16[512,4096]{1,0:T(8,128)(2,1)}, u32[]{:S(2)}) %copy-start) | copy-done | bytes 4194328
  54.0 5.2 %shard_map.112 = (f32[512,512]{1,0:T(8,128)S(1)}, bf16[512,512]{1,0:T(8,128)(2,1)S(1)}, bf16[256,512]{1,0:T(8,128)(2,1)S(1)}, bf16[256,512]{1,0:T(8,128)(2,1)S(1...) custom-call(s32[8]{0:T(128)S(1)} %stack.35.place, ...), custom_call_target="tpu_custom_call" | custom-call | flops 826277888 | bytes 4194304 | tf_op jit(solution)/shard_map/pallas_call | solution.py:202
  59.3 6.3 %shard_map.116 = (bf16[512,512]{1,0:T(8,128)(2,1)}, bf16[512,512]{1,0:T(8,128)(2,1)S(1)}, f32[4,128,128]{2,1,0:T(8,128)S(1)}, f32[4,16,128]{2,1,0:T(8,128)S(1)}) custom-call(s32[8]{0:T(128)S(1)} %stack.35.place, bf16[512,4096]{1,0:T(8,128)(2,1)S(1)} %copy-done.1, bf16[512,512]{1,0:T(8,128)(2,1)S(1)} %copy-done.8, ...), custom_call_target="tpu_custom_call" | custom-call | flops 2157969408 | bytes 8388608 | tf_op jit(solution)/shard_map/pallas_call | solution.py:202
  65.7 3.2 %collective-permute-start.6 = (bf16[256,512]{1,0:T(8,128)(2,1)S(1)}, bf16[256,512]{1,0:T(8,128)(2,1)S(1)}, u32[]{:S(2)}, u32[]{:S(2)}) collective-permute-start(bf16[256,512]{1,0:T(8,128)(2,1)S(1)} %get-tuple-element.31), channel_id=1, source_target_pairs={{0,3},{1,0},{2,1},{3,2},{4,7},{5,4},{6,5},{7,6},{8,11},{9,8},{10,9... | collective-permute-start | bytes 786440 | tf_op jit(solution)/shard_map/ppermute | solution.py:236
  71.7 4.3 %collective-permute-done.5.got_t = bf16[256,512]{1,0:T(8,128)(2,1)S(1)} collective-permute-done((bf16[256,512]{1,0:T(8,128)(2,1)S(1)}, bf16[256,512]{1,0:T(8,128)(2,1)S(1)}, u32[]{:S(2)}, u32[]{:S(2)}) %collective-permute-start.5) | collective-permute-done | bytes 262176 | tf_op jit(solution)/shard_map/ppermute | solution.py:232
  81.2 3.2 %collective-permute-start.8 = (bf16[256,512]{1,0:T(8,128)(2,1)S(1)}, bf16[256,512]{1,0:T(8,128)(2,1)S(1)}, u32[]{:S(2)}, u32[]{:S(2)}) collective-permute-start(bf16[256,512]{1,0:T(8,128)(2,1)S(1)} %get-tuple-element.33), channel_id=1, source_target_pairs={{0,3},{1,0},{2,1},{3,2},{4,7},{5,4},{6,5},{7,6},{8,11},{9,8},{10,9... | collective-permute-start | bytes 786440 | tf_op jit(solution)/shard_map/ppermute | solution.py:236
  85.1 2.1 %collective-permute-start.29 = (f32[4,16,128]{2,1,0:T(8,128)}, f32[4,16,128]{2,1,0:T(8,128)}, u32[]{:S(2)}, u32[]{:S(2)}) collective-permute-start(f32[4,16,128]{2,1,0:T(8,128)} %fusion.1), channel_id=1, source_target_pairs={{0,224},{8,232},{16,240},{24,248},{32,0},{40,8},{48,16},{56,24},{6... | collective-permute-start | bytes 98312 | tf_op jit(solution)/shard_map/ppermute | solution.py:257
  87.2 3.1 %collective-permute-done.7.x_t = bf16[256,512]{1,0:T(8,128)(2,1)S(1)} collective-permute-done((bf16[256,512]{1,0:T(8,128)(2,1)S(1)}, bf16[256,512]{1,0:T(8,128)(2,1)S(1)}, u32[]{:S(2)}, u32[]{:S(2)}) %collective-permute-start.7) | collective-permute-done | bytes 262176 | tf_op jit(solution)/shard_map/ppermute | solution.py:232
  90.6 2.4 %shard_map.114 = (bf16[512,512]{1,0:T(8,128)(2,1)}, bf16[512,512]{1,0:T(8,128)(2,1)}, bf16[512,512]{1,0:T(8,128)(2,1)}) custom-call(s32[8]{0:T(128)S(1)} %stack.35.place, bf16[512,512]{1,0:T(8,128)(2,1)S(1)} %get-tuple-element.29.mixed_in, bf16[512,4096]{1,0:T(8,128)(2,1)S(1)} %copy-done.1, bf16[256,512]{1,0:T(8,128)(2,1)S(1)} %collective-permute-done.7.x_t, ...), custom_call_target="tpu_custom_call" | custom-call | flops 805306368 | bytes 2621440 | tf_op jit(solution)/shard_map/pallas_call | solution.py:202
  94.5 3.2 %collective-permute-start.15 = (bf16[512,512]{1,0:T(8,128)(2,1)}, bf16[512,512]{1,0:T(8,128)(2,1)}, u32[]{:S(2)}, u32[]{:S(2)}) collective-permute-start(bf16[512,512]{1,0:T(8,128)(2,1)} %get-tuple-element.40), channel_id=1, source_target_pairs={{0,3},{1,0},{2,1},{3,2},{4,7},{5,4},{6,5},{7,6},{8,11},{9,8},{10,9... | collective-permute-start | bytes 1572872 | tf_op jit(solution)/shard_map/ppermute | solution.py:236
  99.2 3.6 %collective-permute-start.30 = (f32[4,16,128]{2,1,0:T(8,128)}, f32[4,16,128]{2,1,0:T(8,128)}, u32[]{:S(2)}, u32[]{:S(2)}) collective-permute-start(f32[4,16,128]{2,1,0:T(8,128)} %fusion.21), channel_id=1, source_target_pairs={{0,192},{8,200},{16,208},{24,216},{32,224},{40,232},{48,240},{56,2... | collective-permute-start | bytes 98312 | tf_op jit(solution)/shard_map/ppermute | solution.py:257
  106.1 4.0 %collective-permute-start.31 = (f32[4,16,128]{2,1,0:T(8,128)}, f32[4,16,128]{2,1,0:T(8,128)}, u32[]{:S(2)}, u32[]{:S(2)}) collective-permute-start(f32[4,16,128]{2,1,0:T(8,128)} %fusion.8), channel_id=1, source_target_pairs={{0,128},{8,136},{16,144},{24,152},{32,160},{40,168},{48,176},{56,1... | collective-permute-start | bytes 98312 | tf_op jit(solution)/shard_map/ppermute | solution.py:257
  110.1 2.2 %copy-done.2 = bf16[512,4096]{1,0:T(8,128)(2,1)S(1)} copy-done((bf16[512,4096]{1,0:T(8,128)(2,1)S(1)}, bf16[512,4096]{1,0:T(8,128)(2,1)}, u32[]{:S(2)}) %copy-start.2) | copy-done | bytes 4194328
  112.3 2.4 %shard_map.115 = bf16[512,512]{1,0:T(8,128)(2,1)} custom-call(s32[8]{0:T(128)S(1)} %stack.35.place, bf16[512,512]{1,0:T(8,128)(2,1)S(1)} %get-tuple-element.29.mixed_in, bf16[512,4096]{1,0:T(8,128)(2,1)S(1)} %copy-done.2, bf16[512,512]{1,0:T(8,128)(2,1)S(1)} %collective-permute-done.13.x, bf16[512,512]{1,0:T(8,128)(2,1)S(1)} %collective-permute-done.14.p, ...), custom_call_target="tpu_custom_call" | custom-call | flops 268435456 | bytes 2097152 | tf_op jit(solution)/shard_map/pallas_call | solution.py:202
  115.5 5.2 %shard_map.117 = (bf16[512,512]{1,0:T(8,128)(2,1)}, bf16[512,512]{1,0:T(8,128)(2,1)}) custom-call(bf16[512,512]{1,0:T(8,128)(2,1)S(1)} %get-tuple-element.43.grad_conv, f32[4,128,128]{2,1,0:T(8,128)S(1)} %get-tuple-element.44.starts, f32[4,16,128]{2,1,0:T(8,128)S(1)} %fusion.4.initial, f32[4,16,128]{2,1,0:T(8,128)S(1)} %get-tuple-element.69.keep, ...), custom_call_target="tpu_custom_call" | custom-call | flops 20971520 | bytes 3145728 | tf_op jit(solution)/shard_map/pallas_call | solution.py:202
  (114 shorter events, 34.0 us)
Async XLA Ops:
  6.8 24.7 %collective-permute-start.16 = (bf16[512,512]{1,0:T(8,128)(2,1)}, bf16[512,512]{1,0:T(8,128)(2,1)S(1)}, u32[]{:S(2)}, u32[]{:S(2)}) collective-permute-start(bf16[512,512]{1,0:T(8,128)(2,1)} %own.1), channel_id=1, source_target_pairs={{0,4},{1,5},{2,6},{3,7},{4,0},{5,1},{6,2},{7,3},{8,12},{9,13},{10,... | collective-permute-start | bytes 1572872 | tf_op jit(solution)/shard_map/ppermute | solution.py:228
  9.2 13.8 %collective-permute-start.1 = (f32[4,16,128]{2,1,0:T(8,128)S(1)}, f32[4,16,128]{2,1,0:T(8,128)S(1)}, u32[]{:S(2)}, u32[]{:S(2)}) collective-permute-start(f32[4,16,128]{2,1,0:T(8,128)S(1)} %fusion.29), channel_id=1, source_target_pairs={{0,16},{8,24},{16,0},{24,8},{32,48},{40,56},{48,32},{56,40},{64,80... | collective-permute-start | bytes 98312 | tf_op jit(solution)/shard_map/ppermute | solution.py:251
  10.3 22.4 %collective-permute-start.17 = (bf16[512,512]{1,0:T(8,128)(2,1)}, bf16[512,512]{1,0:T(8,128)(2,1)S(1)}, u32[]{:S(2)}, u32[]{:S(2)}) collective-permute-start(bf16[512,512]{1,0:T(8,128)(2,1)} %own.1), channel_id=1, source_target_pairs={{0,1},{1,2},{2,3},{3,0},{4,5},{5,6},{6,7},{7,4},{8,9},{9,10},{10,1... | collective-permute-start | bytes 1572872 | tf_op jit(solution)/shard_map/ppermute | solution.py:232
  25.0 16.6 %collective-permute-start.18 = (bf16[512,512]{1,0:T(8,128)(2,1)}, bf16[512,512]{1,0:T(8,128)(2,1)S(1)}, u32[]{:S(2)}, u32[]{:S(2)}) collective-permute-start(bf16[512,512]{1,0:T(8,128)(2,1)} %own.1), channel_id=1, source_target_pairs={{0,3},{1,0},{2,1},{3,2},{4,7},{5,4},{6,5},{7,6},{8,11},{9,8},{10,9... | collective-permute-start | bytes 1572872 | tf_op jit(solution)/shard_map/ppermute | solution.py:236
  31.6 15.3 %collective-permute-start.19 = (bf16[256,512]{1,0:T(8,128)(2,1)S(1)}, bf16[256,512]{1,0:T(8,128)(2,1)S(1)}, u32[]{:S(2)}, u32[]{:S(2)}) collective-permute-start(bf16[256,512]{1,0:T(8,128)(2,1)S(1)} %get-tuple-element.53), channel_id=1, source_target_pairs={{0,1},{1,2},{2,3},{3,0},{4,5},{5,6},{6,7},{7,4},{8,9},{9,10},{10,1... | collective-permute-start | bytes 786440 | tf_op jit(solution)/shard_map/ppermute | solution.py:232
  32.7 15.8 %collective-permute-start.20 = (bf16[256,512]{1,0:T(8,128)(2,1)S(1)}, bf16[256,512]{1,0:T(8,128)(2,1)S(1)}, u32[]{:S(2)}, u32[]{:S(2)}) collective-permute-start(bf16[256,512]{1,0:T(8,128)(2,1)S(1)} %get-tuple-element.51), channel_id=1, source_target_pairs={{0,4},{1,5},{2,6},{3,7},{4,0},{5,1},{6,2},{7,3},{8,12},{9,13},{10,... | collective-permute-start | bytes 786440 | tf_op jit(solution)/shard_map/ppermute | solution.py:228
  34.6 14.2 %collective-permute-start.22 = (bf16[256,512]{1,0:T(8,128)(2,1)S(1)}, bf16[256,512]{1,0:T(8,128)(2,1)S(1)}, u32[]{:S(2)}, u32[]{:S(2)}) collective-permute-start(bf16[256,512]{1,0:T(8,128)(2,1)S(1)} %get-tuple-element.52), channel_id=1, source_target_pairs={{0,3},{1,0},{2,1},{3,2},{4,7},{5,4},{6,5},{7,6},{8,11},{9,8},{10,9... | collective-permute-start | bytes 786440 | tf_op jit(solution)/shard_map/ppermute | solution.py:236
  41.7 17.6 %collective-permute-start.21 = (bf16[256,512]{1,0:T(8,128)(2,1)S(1)}, bf16[256,512]{1,0:T(8,128)(2,1)S(1)}, u32[]{:S(2)}, u32[]{:S(2)}) collective-permute-start(bf16[256,512]{1,0:T(8,128)(2,1)S(1)} %get-tuple-element.49), channel_id=1, source_target_pairs={{0,4},{1,5},{2,6},{3,7},{4,0},{5,1},{6,2},{7,3},{8,12},{9,13},{10,... | collective-permute-start | bytes 786440 | tf_op jit(solution)/shard_map/ppermute | solution.py:228
  45.3 14.0 %collective-permute-start.23 = (bf16[256,512]{1,0:T(8,128)(2,1)S(1)}, bf16[256,512]{1,0:T(8,128)(2,1)S(1)}, u32[]{:S(2)}, u32[]{:S(2)}) collective-permute-start(bf16[256,512]{1,0:T(8,128)(2,1)S(1)} %get-tuple-element.50), channel_id=1, source_target_pairs={{0,1},{1,2},{2,3},{3,0},{4,5},{5,6},{6,7},{7,4},{8,9},{9,10},{10,1... | collective-permute-start | bytes 786440 | tf_op jit(solution)/shard_map/ppermute | solution.py:232
  46.8 12.4 %collective-permute-start.24 = (bf16[256,512]{1,0:T(8,128)(2,1)S(1)}, bf16[256,512]{1,0:T(8,128)(2,1)S(1)}, u32[]{:S(2)}, u32[]{:S(2)}) collective-permute-start(bf16[256,512]{1,0:T(8,128)(2,1)S(1)} %get-tuple-element.48), channel_id=1, source_target_pairs={{0,3},{1,0},{2,1},{3,2},{4,7},{5,4},{6,5},{7,6},{8,11},{9,8},{10,9... | collective-permute-start | bytes 786440 | tf_op jit(solution)/shard_map/ppermute | solution.py:236
  48.5 10.8 %collective-permute-start.25 = (bf16[256,512]{1,0:T(8,128)(2,1)S(1)}, bf16[256,512]{1,0:T(8,128)(2,1)S(1)}, u32[]{:S(2)}, u32[]{:S(2)}) collective-permute-start(bf16[256,512]{1,0:T(8,128)(2,1)S(1)} %collective-permute-done.19.ab_t), channel_id=1, source_target_pairs={{0,1},{1,2},{2,3},{3,0},{4,5},{5,6},{6,7},{7,4},{8,9},{9,10},{10,1... | collective-permute-start | bytes 786440 | tf_op jit(solution)/shard_map/ppermute | solution.py:232
  48.9 10.4 %collective-permute-start.26 = (bf16[256,512]{1,0:T(8,128)(2,1)S(1)}, bf16[256,512]{1,0:T(8,128)(2,1)S(1)}, u32[]{:S(2)}, u32[]{:S(2)}) collective-permute-start(bf16[256,512]{1,0:T(8,128)(2,1)S(1)} %collective-permute-done.22.aa_b), channel_id=1, source_target_pairs={{0,3},{1,0},{2,1},{3,2},{4,7},{5,4},{6,5},{7,6},{8,11},{9,8},{10,9... | collective-permute-start | bytes 786440 | tf_op jit(solution)/shard_map/ppermute | solution.py:236
  65.7 10.4 %collective-permute-start.5 = (bf16[256,512]{1,0:T(8,128)(2,1)S(1)}, bf16[256,512]{1,0:T(8,128)(2,1)S(1)}, u32[]{:S(2)}, u32[]{:S(2)}) collective-permute-start(bf16[256,512]{1,0:T(8,128)(2,1)S(1)} %get-tuple-element.30), channel_id=1, source_target_pairs={{0,1},{1,2},{2,3},{3,0},{4,5},{5,6},{6,7},{7,4},{8,9},{9,10},{10,1... | collective-permute-start | bytes 786440 | tf_op jit(solution)/shard_map/ppermute | solution.py:232
  65.7 12.1 %collective-permute-start.6 = (bf16[256,512]{1,0:T(8,128)(2,1)S(1)}, bf16[256,512]{1,0:T(8,128)(2,1)S(1)}, u32[]{:S(2)}, u32[]{:S(2)}) collective-permute-start(bf16[256,512]{1,0:T(8,128)(2,1)S(1)} %get-tuple-element.31), channel_id=1, source_target_pairs={{0,3},{1,0},{2,1},{3,2},{4,7},{5,4},{6,5},{7,6},{8,11},{9,8},{10,9... | collective-permute-start | bytes 786440 | tf_op jit(solution)/shard_map/ppermute | solution.py:236
  69.0 12.2 %collective-permute-start.9 = (bf16[256,512]{1,0:T(8,128)(2,1)S(1)}, bf16[256,512]{1,0:T(8,128)(2,1)S(1)}, u32[]{:S(2)}, u32[]{:S(2)}) collective-permute-start(bf16[256,512]{1,0:T(8,128)(2,1)S(1)} %get-tuple-element.34), channel_id=1, source_target_pairs={{0,1},{1,2},{2,3},{3,0},{4,5},{5,6},{6,7},{7,4},{8,9},{9,10},{10,1... | collective-permute-start | bytes 786440 | tf_op jit(solution)/shard_map/ppermute | solution.py:232
  69.0 12.2 %collective-permute-start.28 = (f32[4,16,128]{2,1,0:T(8,128)S(1)}, f32[4,16,128]{2,1,0:T(8,128)S(1)}, u32[]{:S(2)}, u32[]{:S(2)}) collective-permute-start(f32[4,16,128]{2,1,0:T(8,128)S(1)} %fusion.30), channel_id=1, source_target_pairs={{0,16},{8,24},{16,0},{24,8},{32,48},{40,56},{48,32},{56,40},{64,80... | collective-permute-start | bytes 98312 | tf_op jit(solution)/shard_map/ppermute | solution.py:251
  70.2 14.8 %collective-permute-start.10 = (bf16[256,512]{1,0:T(8,128)(2,1)S(1)}, bf16[256,512]{1,0:T(8,128)(2,1)S(1)}, u32[]{:S(2)}, u32[]{:S(2)}) collective-permute-start(bf16[256,512]{1,0:T(8,128)(2,1)S(1)} %get-tuple-element.35), channel_id=1, source_target_pairs={{0,4},{1,5},{2,6},{3,7},{4,0},{5,1},{6,2},{7,3},{8,12},{9,13},{10,... | collective-permute-start | bytes 786440 | tf_op jit(solution)/shard_map/ppermute | solution.py:228
  76.0 11.2 %collective-permute-start.11 = (bf16[256,512]{1,0:T(8,128)(2,1)S(1)}, bf16[256,512]{1,0:T(8,128)(2,1)S(1)}, u32[]{:S(2)}, u32[]{:S(2)}) collective-permute-start(bf16[256,512]{1,0:T(8,128)(2,1)S(1)} %get-tuple-element.36), channel_id=1, source_target_pairs={{0,4},{1,5},{2,6},{3,7},{4,0},{5,1},{6,2},{7,3},{8,12},{9,13},{10,... | collective-permute-start | bytes 786440 | tf_op jit(solution)/shard_map/ppermute | solution.py:228
  77.9 9.3 %collective-permute-start.12 = (bf16[256,512]{1,0:T(8,128)(2,1)S(1)}, bf16[256,512]{1,0:T(8,128)(2,1)S(1)}, u32[]{:S(2)}, u32[]{:S(2)}) collective-permute-start(bf16[256,512]{1,0:T(8,128)(2,1)S(1)} %get-tuple-element.37), channel_id=1, source_target_pairs={{0,3},{1,0},{2,1},{3,2},{4,7},{5,4},{6,5},{7,6},{8,11},{9,8},{10,9... | collective-permute-start | bytes 786440 | tf_op jit(solution)/shard_map/ppermute | solution.py:236
  81.2 9.4 %collective-permute-start.8 = (bf16[256,512]{1,0:T(8,128)(2,1)S(1)}, bf16[256,512]{1,0:T(8,128)(2,1)S(1)}, u32[]{:S(2)}, u32[]{:S(2)}) collective-permute-start(bf16[256,512]{1,0:T(8,128)(2,1)S(1)} %get-tuple-element.33), channel_id=1, source_target_pairs={{0,3},{1,0},{2,1},{3,2},{4,7},{5,4},{6,5},{7,6},{8,11},{9,8},{10,9... | collective-permute-start | bytes 786440 | tf_op jit(solution)/shard_map/ppermute | solution.py:236
  85.1 12.7 %collective-permute-start.29 = (f32[4,16,128]{2,1,0:T(8,128)}, f32[4,16,128]{2,1,0:T(8,128)}, u32[]{:S(2)}, u32[]{:S(2)}) collective-permute-start(f32[4,16,128]{2,1,0:T(8,128)} %fusion.1), channel_id=1, source_target_pairs={{0,224},{8,232},{16,240},{24,248},{32,0},{40,8},{48,16},{56,24},{6... | collective-permute-start | bytes 98312 | tf_op jit(solution)/shard_map/ppermute | solution.py:257
  93.0 17.0 %collective-permute-start.13 = (bf16[512,512]{1,0:T(8,128)(2,1)}, bf16[512,512]{1,0:T(8,128)(2,1)S(1)}, u32[]{:S(2)}, u32[]{:S(2)}) collective-permute-start(bf16[512,512]{1,0:T(8,128)(2,1)} %get-tuple-element.38), channel_id=1, source_target_pairs={{0,4},{1,5},{2,6},{3,7},{4,0},{5,1},{6,2},{7,3},{8,12},{9,13},{10,... | collective-permute-start | bytes 1572872 | tf_op jit(solution)/shard_map/ppermute | solution.py:228
  94.5 15.5 %collective-permute-start.14 = (bf16[512,512]{1,0:T(8,128)(2,1)}, bf16[512,512]{1,0:T(8,128)(2,1)S(1)}, u32[]{:S(2)}, u32[]{:S(2)}) collective-permute-start(bf16[512,512]{1,0:T(8,128)(2,1)} %get-tuple-element.39), channel_id=1, source_target_pairs={{0,1},{1,2},{2,3},{3,0},{4,5},{5,6},{6,7},{7,4},{8,9},{9,10},{10,1... | collective-permute-start | bytes 1572872 | tf_op jit(solution)/shard_map/ppermute | solution.py:232
  94.5 15.5 %collective-permute-start.15 = (bf16[512,512]{1,0:T(8,128)(2,1)}, bf16[512,512]{1,0:T(8,128)(2,1)}, u32[]{:S(2)}, u32[]{:S(2)}) collective-permute-start(bf16[512,512]{1,0:T(8,128)(2,1)} %get-tuple-element.40), channel_id=1, source_target_pairs={{0,3},{1,0},{2,1},{3,2},{4,7},{5,4},{6,5},{7,6},{8,11},{9,8},{10,9... | collective-permute-start | bytes 1572872 | tf_op jit(solution)/shard_map/ppermute | solution.py:236
  (33 other events, 486.0 us)
where the time goes:
time: 122 us; the launch traced here: 121 us
  starting transfers between devices  54.7 us (45%)
  waiting for transfers between devices  27.5 us (23%)
  Pallas kernels  24.8 us (20%)
  local copies, waits for them, and re-layouts  6.76 us (6%)
  other arithmetic  5.82 us (5%)
    pallas_call x7, Pallas kernels, call(): pl.pallas_call(kernel, out_shape=[jax.ShapeDtypeStruct(shape, kind) for s...  24.8 us
    ppermute x8, starting transfers between devices, shift_down(): return lax.ppermute(value, 'tp', tp_perm(lambda x, y: (x, y + 3)))  20.1 us
    ppermute x6, starting transfers between devices, carried_in(): lax.ppermute(window, 'ctx', ctx_perm(lambda z, h, c: (z + move, h, c)))  16.6 us
    ppermute x2, waiting for transfers between devices, carried_in(): other = lax.ppermute(pair, 'ctx', ctx_perm(lambda z, h, c: (z, h + 1, c)))  11.2 us
    ppermute x6, starting transfers between devices, shift_x(): return lax.ppermute(value, 'tp', tp_perm(lambda x, y: (x + 1, y)))  10.9 us
    ppermute x8, waiting for transfers between devices, shift_up(): return lax.ppermute(value, 'tp', tp_perm(lambda x, y: (x, y + 1)))  9.07 us
    ppermute x6, waiting for transfers between devices, carried_in(): lax.ppermute(window, 'ctx', ctx_perm(lambda z, h, c: (z + move, h, c)))  6.85 us
    unnamed x50, local copies, waits for them, and re-layouts  6.57 us
  transfers between devices with their start and end apart: 32, of which 9 were waited for; matrix products, arithmetic and copies ran while one was open for 3% of the time, Pallas kernels for 9%

commit v1 on v0

v1 whole, which is shorter than its diff:
```python
import functools

import jax
import jax.numpy as jnp
from jax import lax
from jax.experimental import pallas as pl
from jax.experimental.pallas import tpu as pltpu
from jax.sharding import PartitionSpec as P

F32, BF16 = jnp.float32, jnp.bfloat16
ROWS, COLS, MODES, LANES = 512, 512, 16, 128
HALF = ROWS // 2
TILES = COLS // LANES
PARTS = 8
STEP = ROWS // PARTS
VMEM = pl.BlockSpec(memory_space=pltpu.VMEM)
SMEM = pl.BlockSpec(memory_space=pltpu.SMEM)


def tile_of(tile):
    return slice(tile * LANES, (tile + 1) * LANES)


def spread(ref, tile, mode):
    return jnp.broadcast_to(ref[tile, mode : mode + 1, :], (PARTS, LANES))


def ends_of(signal, ends, keep, tile, flipped):
    decay = [spread(keep, tile, m) for m in range(MODES)]

    def step(i, states):
        at = STEP - 1 - i if flipped else i
        u = signal[tile, pl.ds(at, PARTS, stride=STEP), :]
        return tuple(decay[m] * states[m] + u for m in range(MODES))

    zero = jnp.zeros((PARTS, LANES), F32)
    states = lax.fori_loop(0, STEP, step, (zero,) * MODES, unroll=4)
    for m in range(MODES):
        ends[tile, pl.ds(m, PARTS, stride=MODES), :] = states[m]


def chain(ends, starts, total, keep_piece, tile, flipped):
    state = jnp.zeros((MODES, LANES), F32)
    factor = keep_piece[tile]
    order = range(PARTS - 1, -1, -1) if flipped else range(PARTS)
    for piece in order:
        rows = slice(piece * MODES, (piece + 1) * MODES)
        starts[tile, rows, :] = state
        state = factor * state + ends[tile, rows, :]
    total[tile] = state


def whole_starts(starts, initial, begin, keep_piece, tile, flipped):
    carried = initial
    factor = keep_piece[tile]
    order = range(PARTS - 1, -1, -1) if flipped else range(PARTS)
    for piece in order:
        rows = slice(piece * MODES, (piece + 1) * MODES)
        begin[tile, rows, :] = starts[tile, rows, :] + carried
        carried = factor * carried


def responses(signal, begin, result, keep, gain, tile, flipped):
    decay = [spread(keep, tile, m) for m in range(MODES)]
    gains = [spread(gain, tile, m) for m in range(MODES)]

    def step(i, states):
        at = STEP - 1 - i if flipped else i
        u = signal[tile, pl.ds(at, PARTS, stride=STEP), :]
        states = tuple(decay[m] * states[m] + u for m in range(MODES))
        terms = [gains[m] * states[m] for m in range(MODES)]
        while len(terms) > 1:
            terms = [terms[i] + terms[i + 1] for i in range(0, len(terms), 2)]
        result[tile, pl.ds(at, PARTS, stride=STEP), :] = terms[0]
        return states

    states = tuple(begin[tile, pl.ds(m, PARTS, stride=MODES), :] for m in range(MODES))
    lax.fori_loop(0, STEP, step, states, unroll=4)


def dot(a, b):
    return jnp.dot(a, b, preferred_element_type=F32)


def turned(a, b):
    return lax.dot_general(a, b, (((1,), (1,)), ((), ())), preferred_element_type=F32)


def wide(value):
    return value.astype(F32)


def columns(weight, place, which):
    return weight[:, pl.ds(pl.multiple_of(place[which] * COLS, COLS), COLS)]


NEAR = [(0, 0), (1, 0), (0, -1), (0, 1), (1, -1), (1, 1), (0, 2), (1, 2)]
OWN, ACROSS, BELOW, ABOVE, ACROSS_BELOW, ACROSS_ABOVE, FAR, ACROSS_FAR = range(8)
TOP, BOTTOM = slice(0, HALF), slice(HALF, ROWS)
PER_TILE = range(TILES)


def gate_kernel(
    spot, place, gated, decay_rates, amplitude, rates, keep, keep_piece, gain, starts, total, signal, ends,
):
    for tile in PER_TILE:
        at = tile_of(tile)
        rates[tile] = decay_rates[:, at]
        gain[tile] = amplitude[:, at]
        keep[tile] = jnp.exp(-rates[tile])
        keep_piece[tile] = jnp.exp(rates[tile] * -float(STEP))
        signal[tile] = wide(gated[:, at])
        ends_of(signal, ends, keep, tile, False)
        chain(ends, starts, total, keep_piece, tile, False)


def power(rates, n):
    return jnp.exp(rates * (-float(ROWS) * jnp.asarray(n).astype(F32)))


def spot_of(spot, flipped):
    core, high, z = spot[0], spot[1], spot[2]
    return (1 - core, 1 - high, 7 - z) if flipped else (core, high, z)


def pair_kernel(flipped, spot, rates, own, other, pair, before):
    core, _, _ = spot_of(spot, flipped)
    pair[...] = power(rates[...], 1 - core) * own[...] + power(rates[...], core) * other[...]
    before[...] = core.astype(F32) * other[...]


def three_kernel(flipped, spot, rates, pair, one_off, two_off, two, three):
    _, _, z = spot_of(spot, flipped)
    here = (z >= 1).astype(F32) * one_off[...]
    here += (z >= 2).astype(F32) * (power(rates[...], 4) * two_off[...])
    two[...] = here
    three[...] = pair[...] + power(rates[...], 4) * here


def over_of(rates, z, two, three_off, six_off):
    here = two + (z >= 3).astype(F32) * (power(rates, 8) * three_off)
    return here + (z >= 6).astype(F32) * (power(rates, 20) * six_off)


def sent_kernel(flipped, spot, rates, pair, two, three_off, six_off, after, over, sent):
    _, high, z = spot_of(spot, flipped)
    here = over_of(rates[...], z, two[...], three_off[...], six_off[...])
    over[...] = here
    later = high.astype(F32)
    sent[...] = later * here + (1.0 - later) * (pair[...] + power(rates[...], 4) * here)


def group_kernel(flipped, spot, rates, pair, before, other, group, before_all):
    core, high, _ = spot_of(spot, flipped)
    early, late = power(rates[...], 2 - 2 * high), power(rates[...], 2 * high)
    group[...] = early * pair[...] + late * other[...]
    before_all[...] = before[...] + high.astype(F32) * (power(rates[...], core) * other[...])


def pack_kernel(across, below, above, after, up, down, over):
    up[TOP, :], up[BOTTOM, :] = across[TOP, :], below[TOP, :]
    down[TOP, :], down[BOTTOM, :] = across[BOTTOM, :], above[BOTTOM, :]
    over[TOP, :], over[BOTTOM, :] = below[BOTTOM, :], above[TOP, :]


def halve_kernel(up, down, after, far_t, far_b):
    far_t[...] = up[TOP, :]
    far_b[...] = down[TOP, :]


def mix_kernel(
    spot, rates, other, over, before,
    gated, starts, keep, keep_piece, gain, skip, query, after_t, after_b,
    summed, mixed_in,
    signal, result, begin,
):
    for tile in PER_TILE:
        at = tile_of(tile)
        signal[tile] = wide(gated[:, at])
        core, _, _ = spot_of(spot, False)
        initial = other[tile] + power(rates[tile], 2) * over[tile]
        initial = power(rates[tile], core) * initial + before[tile]
        whole_starts(starts, initial, begin, keep_piece, tile, False)
        responses(signal, begin, result, keep, gain, tile, False)
        conv = wide(result[tile].astype(BF16))
        total = conv + skip[0:1, at] * signal[tile]
        summed[:, at] = total
        mixed_in[:, at] = (wide(query[:, at]) * total).astype(BF16)


def first_kernel(place, mixed_in, weight, after_t, after_b, up, down, over):
    top, bottom = mixed_in[TOP, :], mixed_in[BOTTOM, :]
    up[TOP, :] = dot(top, columns(weight, place, ACROSS_FAR)).astype(BF16)
    down[TOP, :] = dot(bottom, columns(weight, place, ACROSS_FAR)).astype(BF16)
    up[BOTTOM, :] = dot(top, columns(weight, place, FAR)).astype(BF16)
    down[BOTTOM, :] = dot(bottom, columns(weight, place, FAR)).astype(BF16)
    over[TOP, :] = dot(bottom, columns(weight, place, ACROSS_ABOVE)).astype(BF16)
    over[BOTTOM, :] = dot(top, columns(weight, place, ACROSS_BELOW)).astype(BF16)


def rest_kernel(place, mixed_in, weight, after, side, above, below, across, own):
    top, bottom = mixed_in[TOP, :], mixed_in[BOTTOM, :]
    side[TOP, :] = dot(top, columns(weight, place, ACROSS_ABOVE)).astype(BF16)
    side[BOTTOM, :] = dot(bottom, columns(weight, place, ACROSS_BELOW)).astype(BF16)
    for out, which in ((above, ABOVE), (below, BELOW), (across, ACROSS), (own, OWN)):
        out[TOP, :] = dot(top, columns(weight, place, which)).astype(BF16)
        out[BOTTOM, :] = dot(bottom, columns(weight, place, which)).astype(BF16)


def second_kernel(up, down, over, side, above, below, after, top_out, bottom_out, above_out, below_out):
    top_out[...] = (wide(side[TOP, :]) + wide(up[TOP, :])).astype(BF16)
    bottom_out[...] = (wide(side[BOTTOM, :]) + wide(down[TOP, :])).astype(BF16)
    above_out[TOP, :] = (wide(above[TOP, :]) + wide(up[BOTTOM, :])).astype(BF16)
    above_out[BOTTOM, :] = (wide(above[BOTTOM, :]) + wide(over[TOP, :])).astype(BF16)
    below_out[TOP, :] = (wide(below[TOP, :]) + wide(over[BOTTOM, :])).astype(BF16)
    below_out[BOTTOM, :] = (wide(below[BOTTOM, :]) + wide(down[BOTTOM, :])).astype(BF16)


def third_kernel(across, got_t, got_b, after, out):
    out[TOP, :] = (wide(across[TOP, :]) + wide(got_t[...])).astype(BF16)
    out[BOTTOM, :] = (wide(across[BOTTOM, :]) + wide(got_b[...])).astype(BF16)


def last_kernel(own, above, below, across, out):
    inner = wide(own[...]) + wide(above[...])
    out[...] = (inner + (wide(below[...]) + wide(across[...]))).astype(BF16)


def grad_kernel(
    place, weight, own, across, below, above, up, down, over, far_t, far_b, query,
    summed, keep, keep_piece, after,
    grad_query, grad_conv, starts, total,
    full, signal, ends,
):
    halves = (
        (TOP, ((up, TOP, ACROSS_BELOW), (over, BOTTOM, ACROSS_ABOVE), (up, BOTTOM, FAR), (far_t, TOP, ACROSS_FAR))),
        (BOTTOM, ((over, TOP, ACROSS_BELOW), (down, TOP, ACROSS_ABOVE), (down, BOTTOM, FAR), (far_b, TOP, ACROSS_FAR))),
    )
    for rows, parts in halves:
        grad = turned(own[rows, :], columns(weight, place, OWN))
        for ref, which in ((across, ACROSS), (below, BELOW), (above, ABOVE)):
            grad += turned(ref[rows, :], columns(weight, place, which))
        for ref, part, which in parts:
            grad += turned(ref[part, :], columns(weight, place, which))
        full[rows, :] = grad
    for tile in PER_TILE:
        at = tile_of(tile)
        grad_query[:, at] = (full[:, at] * summed[:, at]).astype(BF16)
        conv = (full[:, at] * wide(query[:, at])).astype(BF16)
        grad_conv[:, at] = conv
        signal[tile] = wide(conv)
        ends_of(signal, ends, keep, tile, True)
        chain(ends, starts, total, keep_piece, tile, True)


def back_kernel(
    spot, rates, two, three_off, six_off, before,
    grad_conv, starts, keep, keep_piece, gain, skip, key, value,
    grad_key, grad_value,
    signal, result, begin,
):
    for tile in PER_TILE:
        at = tile_of(tile)
        signal[tile] = wide(grad_conv[:, at])
        core, high, z = spot_of(spot, True)
        over = over_of(rates[tile], z, two[tile], three_off[tile], six_off[tile])
        initial = power(rates[tile], 2 * high + core) * over + before[tile]
        whole_starts(starts, initial, begin, keep_piece, tile, True)
        responses(signal, begin, result, keep, gain, tile, True)
        back = wide(result[tile].astype(BF16))
        total = back + skip[0:1, at] * signal[tile]
        grad_key[:, at] = (total * wide(value[:, at])).astype(BF16)
        grad_value[:, at] = (total * wide(key[:, at])).astype(BF16)


STATE_SHAPE, BLOCK, HALVED = (TILES, MODES, LANES), (ROWS, COLS), (HALF, COLS)
TABLE, DEEP = (TILES, PARTS * MODES, LANES), (TILES, ROWS, LANES)


def call(kernel, outs, scratch, micros, mib, *args):
    return pl.pallas_call(
        kernel,
        out_shape=[jax.ShapeDtypeStruct(shape, kind) for shape, kind in outs],
        in_specs=[SMEM if arg.dtype == jnp.int32 else VMEM for arg in args],
        out_specs=[VMEM] * len(outs),
        scratch_shapes=[pltpu.VMEM(shape, kind) for shape, kind in scratch],
        cost_estimate=pl.CostEstimate(
            flops=int(micros * 1.1e9), bytes_accessed=int(micros * 3e6), transcendentals=0
        ),
        compiler_params=pltpu.CompilerParams(vmem_limit_bytes=mib * 1024 * 1024),
    )(*args)


def tp_perm(move):
    return [(x * 4 + y, move(x, y)[0] % 2 * 4 + move(x, y)[1] % 4) for x in range(2) for y in range(4)]


def ctx_perm(move):
    pairs = []
    for z in range(8):
        for h in range(2):
            for c in range(2):
                to = move(z, h, c)
                pairs.append((z * 4 + h * 2 + c, to[0] % 8 * 4 + to[1] % 2 * 2 + to[2] % 2))
    return pairs


def shift_x(value):
    return lax.ppermute(value, "tp", tp_perm(lambda x, y: (x + 1, y)))


def shift_up(value):
    return lax.ppermute(value, "tp", tp_perm(lambda x, y: (x, y + 1)))


def shift_down(value):
    return lax.ppermute(value, "tp", tp_perm(lambda x, y: (x, y + 3)))


def small(kernel, flipped, *args):
    both = [(STATE_SHAPE, F32)] * 2
    return call(functools.partial(kernel, flipped), both, [], 1.0, 4, *args)


def other_core(value):
    return lax.ppermute(value, "ctx", ctx_perm(lambda z, h, c: (z, h, c + 1)))


def other_half(value):
    return lax.ppermute(value, "ctx", ctx_perm(lambda z, h, c: (z, h + 1, c)))


def earlier(value, k, flipped):
    move = -k if flipped else k
    return lax.ppermute(value, "ctx", ctx_perm(lambda z, h, c: (z + move, h, c)))


def per_device(query, key, value, cotangent, weight, decay_rates, residues, skip_gain):
    at, line = lax.axis_index("tp"), lax.axis_index("ctx")
    x, y = at // 4, at % 4
    place = jnp.stack([(x + dx) % 2 * 4 + (y + dy + 4) % 4 for dx, dy in NEAR]).astype(jnp.int32)
    spot = jnp.stack([line % 2, line // 2 % 2, line // 4]).astype(jnp.int32)
    decay_rates, residues = decay_rates.T, residues.T
    amplitude = residues * jnp.sqrt(-jnp.expm1(-2.0 * decay_rates))
    skip = skip_gain.reshape(1, COLS)

    across = shift_x(cotangent)
    below = shift_up(cotangent)
    above = shift_down(cotangent)
    deep, table, state = (DEEP, F32), (TABLE, F32), (STATE_SHAPE, F32)
    gated = (key.astype(F32) * value.astype(F32)).astype(BF16)
    rates, keep, keep_piece, gain, starts, total = call(
        gate_kernel, [state] * 4 + [table, state], [deep, table], 2.4, 6, spot, place, gated, decay_rates, amplitude
    )
    pair, before = small(pair_kernel, False, spot, rates, total, other_core(total))
    s_up, s_down, s_over = call(
        pack_kernel, [(BLOCK, BF16)] * 3, [], 0.1, 4, across, below, above, pair
    )
    up, down, over = shift_up(s_up), shift_down(s_down), shift_x(s_over)
    packed = s_up
    s_far_t, s_far_b = call(halve_kernel, [(HALVED, BF16)] * 2, [], 0.1, 4, up, down, over)
    far_t, far_b = shift_up(s_far_t), shift_down(s_far_b)

    offs = earlier(pair, 1, False), earlier(pair, 2, False)
    two, three = small(three_kernel, False, spot, rates, pair, *offs)
    offs = earlier(three, 3, False), earlier(three, 6, False)
    over_state, sent = small(sent_kernel, False, spot, rates, pair, two, *offs, packed)
    carried = other_half(sent), over_state, before
    summed, mixed_in = call(
        mix_kernel,
        [(BLOCK, F32), (BLOCK, BF16)],
        [deep, deep, table],
        4.5,
        8,
        spot,
        rates,
        *carried,
        gated,
        starts,
        keep,
        keep_piece,
        gain,
        skip,
        query,
        s_far_t,
        s_far_b,
    )
    s_up, s_down, s_over = call(
        first_kernel, [(BLOCK, BF16)] * 3, [], 1.5, 6, place, mixed_in, weight, far_t, far_b
    )
    g_up, g_down, g_over = shift_up(s_up), shift_down(s_down), shift_x(s_over)
    grad_query, grad_conv, back_starts, back_total = call(
        grad_kernel,
        [(BLOCK, BF16), (BLOCK, BF16), table, state],
        [(BLOCK, F32), deep, table],
        6.0,
        8,
        place,
        weight,
        cotangent,
        across,
        below,
        above,
        up,
        down,
        over,
        far_t,
        far_b,
        query,
        summed,
        keep,
        keep_piece,
        s_up,
    )
    pair, before = small(pair_kernel, True, spot, rates, back_total, other_core(back_total))
    half_other = other_half(pair)
    side, above_part, below_part, across_part, own_part = call(
        rest_kernel, [(BLOCK, BF16)] * 5, [], 2.0, 6, place, mixed_in, weight, pair
    )
    group, before = small(group_kernel, True, spot, rates, pair, before, half_other)
    offs = earlier(group, 1, True), earlier(group, 2, True)
    two, three = small(three_kernel, True, spot, rates, group, *offs)
    offs = earlier(three, 3, True), earlier(three, 6, True)

    s_t, s_b, s_above, s_below = call(
        second_kernel,
        [(HALVED, BF16)] * 2 + [(BLOCK, BF16)] * 2,
        [],
        0.1,
        4,
        g_up,
        g_down,
        g_over,
        side,
        above_part,
        below_part,
        group,
    )
    g_t, g_b = shift_up(s_t), shift_down(s_b)
    g_above, g_below = shift_up(s_above), shift_down(s_below)
    (s_across,) = call(third_kernel, [(BLOCK, BF16)], [], 0.5, 4, across_part, g_t, g_b, three)
    (mixed,) = call(
        last_kernel, [(BLOCK, BF16)], [], 0.1, 4, own_part, g_above, g_below, shift_x(s_across)
    )
    grad_key, grad_value = call(
        back_kernel,
        [(BLOCK, BF16)] * 2,
        [deep, deep, table],
        4.5,
        8,
        spot,
        rates,
        two,
        *offs,
        before,
        grad_conv,
        back_starts,
        keep,
        keep_piece,
        gain,
        skip,
        key,
        value,
    )
    return mixed, grad_query, grad_key, grad_value


def solution(mesh):
    split, rows = P("ctx", "tp"), P("tp", None)
    return jax.shard_map(
        per_device,
        mesh=mesh,
        in_specs=(split, split, split, split, rows, rows, rows, P("tp")),
        out_specs=(split, split, split, split),
        check_vma=False,
    )
```

time: 122 us -> 102 us (0.84)
  starting transfers between devices: 54.7 us -> 47.3 us
  waiting for transfers between devices: 27.5 us -> 21.3 us
  local copies, waits for them, and re-layouts: 6.76 us -> 0.88 us
  other arithmetic: 5.82 us -> 2.21 us
  Pallas kernels: 24.8 us -> 27.8 us
    ppermute x8 -> x6, waiting for transfers between devices: 9.07 us -> 2 us  [shift_up(): return lax.ppermute(value, 'tp', tp_perm(lambda x, y: (x, y + 1)))]
    ppermute x6 -> x4, starting transfers between devices: 10.9 us -> 4.08 us  [shift_x(): return lax.ppermute(value, 'tp', tp_perm(lambda x, y: (x + 1, y)))]
    unnamed x50 -> x14, local copies, waits for them, and re-layouts: 6.57 us -> 0.8 us
    add x10 -> x0, other arithmetic: 4.3 us -> none  [the longest x4 2.8 us: carried_in(): window = window + power(jnp.asarray(4 * k)) * other]
    pallas_call x7 -> x17, Pallas kernels: 24.8 us -> 27.8 us  [call(): pl.pallas_call(kernel, out_shape=[jax.ShapeDtypeStruct(shape, kind) for s...]
    ppermute x8 -> x6, starting transfers between devices: 20.1 us -> 17.6 us  [shift_down(): return lax.ppermute(value, 'tp', tp_perm(lambda x, y: (x, y + 3)))]
    ppermute x10 -> x12, starting transfers between devices: 19 us -> 21 us  [the longest x8 17.7 us: earlier(): lax.ppermute(value, 'ctx', ctx_perm(lambda z, h, c: (z + move, h, c)))]
    unnamed x1 -> x0, other arithmetic: 1.52 us -> none
  transfers between devices with their start and end apart: 32 -> 28, of which waited for: 9 -> 14; matrix products, arithmetic and copies ran while one was open for 3% -> 2% of each run, Pallas kernels for 9% -> 25%
where the time goes in v1:
time: 102 us; the launch traced here: 100 us
  starting transfers between devices  47.3 us (46%)
  Pallas kernels  27.8 us (27%)
  waiting for transfers between devices  21.3 us (21%)
  other arithmetic  2.21 us (2%)
    pallas_call x17, Pallas kernels, call(): pl.pallas_call(kernel, out_shape=[jax.ShapeDtypeStruct(shape, kind) for s...  27.8 us
    ppermute x8, starting transfers between devices, earlier(): lax.ppermute(value, 'ctx', ctx_perm(lambda z, h, c: (z + move, h, c)))  17.7 us
    ppermute x6, starting transfers between devices, shift_down(): return lax.ppermute(value, 'tp', tp_perm(lambda x, y: (x, y + 3)))  17.6 us
    ppermute x8, waiting for transfers between devices, earlier(): lax.ppermute(value, 'ctx', ctx_perm(lambda z, h, c: (z + move, h, c)))  14.2 us
    ppermute x6, starting transfers between devices, shift_up(): return lax.ppermute(value, 'tp', tp_perm(lambda x, y: (x, y + 1)))  4.59 us
    ppermute x4, starting transfers between devices, shift_x(): return lax.ppermute(value, 'tp', tp_perm(lambda x, y: (x + 1, y)))  4.08 us
    ppermute x2, starting transfers between devices, other_half(): return lax.ppermute(value, 'ctx', ctx_perm(lambda z, h, c: (z, h + 1, c)))  3.21 us
    ppermute x2, waiting for transfers between devices, other_core(): return lax.ppermute(value, 'ctx', ctx_perm(lambda z, h, c: (z, h, c + 1)))  2.4 us
  transfers between devices with their start and end apart: 28, of which 14 were waited for; matrix products, arithmetic and copies ran while one was open for 2% of the time, Pallas kernels for 25%

profile of v1, /device:TPU:2, one launch (start us, length us, event | category | flops | bytes accessed | tf_op | source)
XLA Modules:
  0.0 100.4 jit_solution(15528131077923051710)
XLA Ops:
  0.6 1.7 %collective-permute-start.6 = (bf16[512,512]{1,0:T(8,128)(2,1)}, bf16[512,512]{1,0:T(8,128)(2,1)S(1)}, u32[]{:S(2)}, u32[]{:S(2)}) collective-permute-start(bf16[512,512]{1,0:T(8,128)(2,1)} %own.1), channel_id=1, source_target_pairs={{0,1},{1,2},{2,3},{3,0},{4,5},{5,6},{6,7},{7,4},{8,9},{9,10},{10,1... | collective-permute-start | bytes 1572872 | tf_op jit(solution)/shard_map/ppermute | solution.py:313
  3.1 3.1 %collective-permute-start.7 = (bf16[512,512]{1,0:T(8,128)(2,1)}, bf16[512,512]{1,0:T(8,128)(2,1)S(1)}, u32[]{:S(2)}, u32[]{:S(2)}) collective-permute-start(bf16[512,512]{1,0:T(8,128)(2,1)} %own.1), channel_id=1, source_target_pairs={{0,3},{1,0},{2,1},{3,2},{4,7},{5,4},{6,5},{7,6},{8,11},{9,8},{10,9... | collective-permute-start | bytes 1572872 | tf_op jit(solution)/shard_map/ppermute | solution.py:317
  9.4 2.6 %shard_map.111 = (f32[4,16,128]{2,1,0:T(8,128)S(1)}, f32[4,16,128]{2,1,0:T(8,128)S(1)}, f32[4,16,128]{2,1,0:T(8,128)S(1)}, f32[4,16,128]{2,1,0:T(8,128)S(1)}, f3...) custom-call(s32[3]{0:T(128)S(1)} %pad_add_fusion.spot, s32[8]{0:T(128)S(1)} %stack.47.place, ...), custom_call_target="tpu_custom_call" | custom-call | flops 2640000000 | bytes 7200000 | tf_op jit(solution)/shard_map/pallas_call | solution.py:281
  13.9 2.0 %collective-permute-done.6.below = bf16[512,512]{1,0:T(8,128)(2,1)S(1)} collective-permute-done((bf16[512,512]{1,0:T(8,128)(2,1)}, bf16[512,512]{1,0:T(8,128)(2,1)S(1)}, u32[]{:S(2)}, u32[]{:S(2)}) %collective-permute-start.6) | collective-permute-done | bytes 524320 | tf_op jit(solution)/shard_map/ppermute | solution.py:313
  16.2 3.1 %collective-permute-start.10 = (bf16[512,512]{1,0:T(8,128)(2,1)S(1)}, bf16[512,512]{1,0:T(8,128)(2,1)S(1)}, u32[]{:S(2)}, u32[]{:S(2)}) collective-permute-start(bf16[512,512]{1,0:T(8,128)(2,1)S(1)} %get-tuple-element.60), channel_id=1, source_target_pairs={{0,3},{1,0},{2,1},{3,2},{4,7},{5,4},{6,5},{7,6},{8,11},{9,8},{10,9... | collective-permute-start | bytes 1572872 | tf_op jit(solution)/shard_map/ppermute | solution.py:317
  20.8 3.3 %collective-permute-start.2 = (f32[4,16,128]{2,1,0:T(8,128)S(1)}, f32[4,16,128]{2,1,0:T(8,128)S(1)}, u32[]{:S(2)}, u32[]{:S(2)}) collective-permute-start(f32[4,16,128]{2,1,0:T(8,128)S(1)} %get-tuple-element.49.pair.after), channel_id=1, source_target_pairs={{0,64},{8,72},{16,80},{24,88},{32,96},{40,104},{48,112},{56,120},{... | collective-permute-start | bytes 98312 | tf_op jit(solution)/shard_map/ppermute | solution.py:335
  24.1 1.9 %collective-permute-start.1 = (f32[4,16,128]{2,1,0:T(8,128)S(1)}, f32[4,16,128]{2,1,0:T(8,128)S(1)}, u32[]{:S(2)}, u32[]{:S(2)}) collective-permute-start(f32[4,16,128]{2,1,0:T(8,128)S(1)} %get-tuple-element.49.pair.after), channel_id=1, source_target_pairs={{0,32},{8,40},{16,48},{24,56},{32,64},{40,72},{48,80},{56,88},{64,... | collective-permute-start | bytes 98312 | tf_op jit(solution)/shard_map/ppermute | solution.py:335
  26.0 3.0 %collective-permute-done.2.two_off = f32[4,16,128]{2,1,0:T(8,128)S(1)} collective-permute-done((f32[4,16,128]{2,1,0:T(8,128)S(1)}, f32[4,16,128]{2,1,0:T(8,128)S(1)}, u32[]{:S(2)}, u32[]{:S(2)}) %collective-permute-start.2) | collective-permute-done | bytes 32800 | tf_op jit(solution)/shard_map/ppermute | solution.py:335
  30.0 2.9 %collective-permute-start.4 = (f32[4,16,128]{2,1,0:T(8,128)S(1)}, f32[4,16,128]{2,1,0:T(8,128)S(1)}, u32[]{:S(2)}, u32[]{:S(2)}) collective-permute-start(f32[4,16,128]{2,1,0:T(8,128)S(1)} %get-tuple-element.51), channel_id=1, source_target_pairs={{0,192},{8,200},{16,208},{24,216},{32,224},{40,232},{48,240},{56,2... | collective-permute-start | bytes 98312 | tf_op jit(solution)/shard_map/ppermute | solution.py:335
  35.1 5.1 %collective-permute-done.3.three_off = f32[4,16,128]{2,1,0:T(8,128)S(1)} collective-permute-done((f32[4,16,128]{2,1,0:T(8,128)S(1)}, f32[4,16,128]{2,1,0:T(8,128)S(1)}, u32[]{:S(2)}, u32[]{:S(2)}) %collective-permute-start.3) | collective-permute-done | bytes 32800 | tf_op jit(solution)/shard_map/ppermute | solution.py:335
  40.7 2.2 %collective-permute-start.8 = (f32[4,16,128]{2,1,0:T(8,128)S(1)}, f32[4,16,128]{2,1,0:T(8,128)S(1)}, u32[]{:S(2)}, u32[]{:S(2)}) collective-permute-start(f32[4,16,128]{2,1,0:T(8,128)S(1)} %get-tuple-element.53), channel_id=1, source_target_pairs={{0,16},{8,24},{16,0},{24,8},{32,48},{40,56},{48,32},{56,40},{64,80... | collective-permute-start | bytes 98312 | tf_op jit(solution)/shard_map/ppermute | solution.py:330
  43.6 2.9 %collective-permute-start.13 = (bf16[256,512]{1,0:T(8,128)(2,1)S(1)}, bf16[256,512]{1,0:T(8,128)(2,1)S(1)}, u32[]{:S(2)}, u32[]{:S(2)}) collective-permute-start(bf16[256,512]{1,0:T(8,128)(2,1)S(1)} %get-tuple-element.63.after_b), channel_id=1, source_target_pairs={{0,3},{1,0},{2,1},{3,2},{4,7},{5,4},{6,5},{7,6},{8,11},{9,8},{10,9... | collective-permute-start | bytes 786440 | tf_op jit(solution)/shard_map/ppermute | solution.py:317
  46.6 4.3 %shard_map.117 = (f32[512,512]{1,0:T(8,128)S(1)}, bf16[512,512]{1,0:T(8,128)(2,1)S(1)}) custom-call(s32[3]{0:T(128)S(1)} %pad_add_fusion.spot, f32[4,16,128]{2,1,0:T(8,128)S(1)} %get-tuple-element.47.rates, f32[4,16,128]{2,1,0:T(8,128)S(1)} %collective-permute-done.8.other, f32[4,16,128]{2,1,0:T(8,128)S(1)} %get-tuple-element.54.over, ...), custom_call_target="tpu_custom_call" | custom-call | flops 4950000128 | bytes 13500000 | tf_op jit(solution)/shard_map/pallas_call | solution.py:281
  52.7 3.8 %collective-permute-start.16 = (bf16[512,512]{1,0:T(8,128)(2,1)S(1)}, bf16[512,512]{1,0:T(8,128)(2,1)S(1)}, u32[]{:S(2)}, u32[]{:S(2)}) collective-permute-start(bf16[512,512]{1,0:T(8,128)(2,1)S(1)} %get-tuple-element.70), channel_id=1, source_target_pairs={{0,3},{1,0},{2,1},{3,2},{4,7},{5,4},{6,5},{7,6},{8,11},{9,8},{10,9... | collective-permute-start | bytes 1572872 | tf_op jit(solution)/shard_map/ppermute | solution.py:317
  57.6 6.3 %shard_map.119 = (bf16[512,512]{1,0:T(8,128)(2,1)}, bf16[512,512]{1,0:T(8,128)(2,1)S(1)}, f32[4,128,128]{2,1,0:T(8,128)S(1)}, f32[4,16,128]{2,1,0:T(8,128)S(1)}) custom-call(s32[8]{0:T(128)S(1)} %stack.47.place, bf16[512,4096]{1,0:T(8,128)(2,1)S(1)} %copy-done.3, bf16[512,512]{1,0:T(8,128)(2,1)S(1)} %copy-done.4, ...), custom_call_target="tpu_custom_call" | custom-call | flops 6600000000 | bytes 18000000 | tf_op jit(solution)/shard_map/pallas_call | solution.py:281
  66.6 2.1 %shard_map.121 = (bf16[512,512]{1,0:T(8,128)(2,1)S(1)}, bf16[512,512]{1,0:T(8,128)(2,1)S(1)}, bf16[512,512]{1,0:T(8,128)(2,1)S(1)}, bf16[512,512]{1,0:T(8,128)(2,1)S(1)}, bf16[512,512]{1,0:T(8,128)(2,1)S(1)}) custom-call(s32[8]{0:T(128)S(1)} %stack.47.place, bf16[512,512]{1,0:T(8,128)(2,1)S(1)} %get-tuple-element.64.mixed_in, ...), custom_call_target="tpu_custom_call" | custom-call | flops 2200000000 | bytes 6000000 | tf_op jit(solution)/shard_map/pallas_call | solution.py:281
  68.8 2.4 %collective-permute-done.18.other = f32[4,16,128]{2,1,0:T(8,128)S(1)} collective-permute-done((f32[4,16,128]{2,1,0:T(8,128)S(1)}, f32[4,16,128]{2,1,0:T(8,128)S(1)}, u32[]{:S(2)}, u32[]{:S(2)}) %collective-permute-start.18) | collective-permute-done | bytes 32800 | tf_op jit(solution)/shard_map/ppermute | solution.py:330
  72.1 1.6 %collective-permute-start.21 = (bf16[256,512]{1,0:T(8,128)(2,1)S(1)}, bf16[256,512]{1,0:T(8,128)(2,1)S(1)}, u32[]{:S(2)}, u32[]{:S(2)}) collective-permute-start(bf16[256,512]{1,0:T(8,128)(2,1)S(1)} %get-tuple-element.80), channel_id=1, source_target_pairs={{0,1},{1,2},{2,3},{3,0},{4,5},{5,6},{6,7},{7,4},{8,9},{9,10},{10,1... | collective-permute-start | bytes 786440 | tf_op jit(solution)/shard_map/ppermute | solution.py:313
  73.8 1.8 %collective-permute-start.22 = (bf16[256,512]{1,0:T(8,128)(2,1)S(1)}, bf16[256,512]{1,0:T(8,128)(2,1)S(1)}, u32[]{:S(2)}, u32[]{:S(2)}) collective-permute-start(bf16[256,512]{1,0:T(8,128)(2,1)S(1)} %get-tuple-element.81), channel_id=1, source_target_pairs={{0,3},{1,0},{2,1},{3,2},{4,7},{5,4},{6,5},{7,6},{8,11},{9,8},{10,9... | collective-permute-start | bytes 786440 | tf_op jit(solution)/shard_map/ppermute | solution.py:317
  75.5 3.0 %collective-permute-start.24 = (f32[4,16,128]{2,1,0:T(8,128)S(1)}, f32[4,16,128]{2,1,0:T(8,128)S(1)}, u32[]{:S(2)}, u32[]{:S(2)}) collective-permute-start(f32[4,16,128]{2,1,0:T(8,128)S(1)} %get-tuple-element.76.after.pair), channel_id=1, source_target_pairs={{0,192},{8,200},{16,208},{24,216},{32,224},{40,232},{48,240},{56,2... | collective-permute-start | bytes 98312 | tf_op jit(solution)/shard_map/ppermute | solution.py:335
  80.5 2.0 %collective-permute-done.23.one_off = f32[4,16,128]{2,1,0:T(8,128)S(1)} collective-permute-done((f32[4,16,128]{2,1,0:T(8,128)S(1)}, f32[4,16,128]{2,1,0:T(8,128)S(1)}, u32[]{:S(2)}, u32[]{:S(2)}) %collective-permute-start.23) | collective-permute-done | bytes 32800 | tf_op jit(solution)/shard_map/ppermute | solution.py:335
  83.7 2.9 %collective-permute-start.20 = (bf16[512,512]{1,0:T(8,128)(2,1)S(1)}, bf16[512,512]{1,0:T(8,128)(2,1)S(1)}, u32[]{:S(2)}, u32[]{:S(2)}) collective-permute-start(bf16[512,512]{1,0:T(8,128)(2,1)S(1)} %get-tuple-element.78), channel_id=1, source_target_pairs={{0,3},{1,0},{2,1},{3,2},{4,7},{5,4},{6,5},{7,6},{8,11},{9,8},{10,9... | collective-permute-start | bytes 1572872 | tf_op jit(solution)/shard_map/ppermute | solution.py:317
  87.6 4.4 %collective-permute-start.26 = (f32[4,16,128]{2,1,0:T(8,128)S(1)}, f32[4,16,128]{2,1,0:T(8,128)S(1)}, u32[]{:S(2)}, u32[]{:S(2)}) collective-permute-start(f32[4,16,128]{2,1,0:T(8,128)S(1)} %get-tuple-element.82.after), channel_id=1, source_target_pairs={{0,160},{8,168},{16,176},{24,184},{32,192},{40,200},{48,208},{56,2... | collective-permute-start | bytes 98312 | tf_op jit(solution)/shard_map/ppermute | solution.py:335
  93.6 5.7 %shard_map.127 = (bf16[512,512]{1,0:T(8,128)(2,1)}, bf16[512,512]{1,0:T(8,128)(2,1)}) custom-call(s32[3]{0:T(128)S(1)} %pad_add_fusion.spot, f32[4,16,128]{2,1,0:T(8,128)S(1)} %get-tuple-element.47.rates, f32[4,16,128]{2,1,0:T(8,128)S(1)} %get-tuple-element.84.two, f32[4,16,128]{2,1,0:T(8,128)S(1)} %collective-permute-done.26.three_off, ...), custom_call_target="tpu_custom_call" | custom-call | flops 4950000128 | bytes 13500000 | tf_op jit(solution)/shard_map/pallas_call | solution.py:281
  (67 shorter events, 25.3 us)
Async XLA Ops:
  0.6 15.2 %collective-permute-start.6 = (bf16[512,512]{1,0:T(8,128)(2,1)}, bf16[512,512]{1,0:T(8,128)(2,1)S(1)}, u32[]{:S(2)}, u32[]{:S(2)}) collective-permute-start(bf16[512,512]{1,0:T(8,128)(2,1)} %own.1), channel_id=1, source_target_pairs={{0,1},{1,2},{2,3},{3,0},{4,5},{5,6},{6,7},{7,4},{8,9},{9,10},{10,1... | collective-permute-start | bytes 1572872 | tf_op jit(solution)/shard_map/ppermute | solution.py:313
  2.3 13.6 %collective-permute-start.5 = (bf16[512,512]{1,0:T(8,128)(2,1)}, bf16[512,512]{1,0:T(8,128)(2,1)S(1)}, u32[]{:S(2)}, u32[]{:S(2)}) collective-permute-start(bf16[512,512]{1,0:T(8,128)(2,1)} %own.1), channel_id=1, source_target_pairs={{0,4},{1,5},{2,6},{3,7},{4,0},{5,1},{6,2},{7,3},{8,12},{9,13},{10,... | collective-permute-start | bytes 1572872 | tf_op jit(solution)/shard_map/ppermute | solution.py:309
  3.1 13.1 %collective-permute-start.7 = (bf16[512,512]{1,0:T(8,128)(2,1)}, bf16[512,512]{1,0:T(8,128)(2,1)S(1)}, u32[]{:S(2)}, u32[]{:S(2)}) collective-permute-start(bf16[512,512]{1,0:T(8,128)(2,1)} %own.1), channel_id=1, source_target_pairs={{0,3},{1,0},{2,1},{3,2},{4,7},{5,4},{6,5},{7,6},{8,11},{9,8},{10,9... | collective-permute-start | bytes 1572872 | tf_op jit(solution)/shard_map/ppermute | solution.py:317
  16.2 26.7 %collective-permute-start.10 = (bf16[512,512]{1,0:T(8,128)(2,1)S(1)}, bf16[512,512]{1,0:T(8,128)(2,1)S(1)}, u32[]{:S(2)}, u32[]{:S(2)}) collective-permute-start(bf16[512,512]{1,0:T(8,128)(2,1)S(1)} %get-tuple-element.60), channel_id=1, source_target_pairs={{0,3},{1,0},{2,1},{3,2},{4,7},{5,4},{6,5},{7,6},{8,11},{9,8},{10,9... | collective-permute-start | bytes 1572872 | tf_op jit(solution)/shard_map/ppermute | solution.py:317
  19.3 23.6 %collective-permute-start.11 = (bf16[512,512]{1,0:T(8,128)(2,1)S(1)}, bf16[512,512]{1,0:T(8,128)(2,1)S(1)}, u32[]{:S(2)}, u32[]{:S(2)}) collective-permute-start(bf16[512,512]{1,0:T(8,128)(2,1)S(1)} %get-tuple-element.61), channel_id=1, source_target_pairs={{0,4},{1,5},{2,6},{3,7},{4,0},{5,1},{6,2},{7,3},{8,12},{9,13},{10,... | collective-permute-start | bytes 1572872 | tf_op jit(solution)/shard_map/ppermute | solution.py:309
  20.8 22.1 %collective-permute-start.9 = (bf16[512,512]{1,0:T(8,128)(2,1)S(1)}, bf16[512,512]{1,0:T(8,128)(2,1)S(1)}, u32[]{:S(2)}, u32[]{:S(2)}) collective-permute-start(bf16[512,512]{1,0:T(8,128)(2,1)S(1)} %get-tuple-element.52.after), channel_id=1, source_target_pairs={{0,1},{1,2},{2,3},{3,0},{4,5},{5,6},{6,7},{7,4},{8,9},{9,10},{10,1... | collective-permute-start | bytes 1572872 | tf_op jit(solution)/shard_map/ppermute | solution.py:313
  20.8 8.2 %collective-permute-start.2 = (f32[4,16,128]{2,1,0:T(8,128)S(1)}, f32[4,16,128]{2,1,0:T(8,128)S(1)}, u32[]{:S(2)}, u32[]{:S(2)}) collective-permute-start(f32[4,16,128]{2,1,0:T(8,128)S(1)} %get-tuple-element.49.pair.after), channel_id=1, source_target_pairs={{0,64},{8,72},{16,80},{24,88},{32,96},{40,104},{48,112},{56,120},{... | collective-permute-start | bytes 98312 | tf_op jit(solution)/shard_map/ppermute | solution.py:335
  24.1 5.3 %collective-permute-start.1 = (f32[4,16,128]{2,1,0:T(8,128)S(1)}, f32[4,16,128]{2,1,0:T(8,128)S(1)}, u32[]{:S(2)}, u32[]{:S(2)}) collective-permute-start(f32[4,16,128]{2,1,0:T(8,128)S(1)} %get-tuple-element.49.pair.after), channel_id=1, source_target_pairs={{0,32},{8,40},{16,48},{24,56},{32,64},{40,72},{48,80},{56,88},{64,... | collective-permute-start | bytes 98312 | tf_op jit(solution)/shard_map/ppermute | solution.py:335
  30.0 5.1 %collective-permute-start.4 = (f32[4,16,128]{2,1,0:T(8,128)S(1)}, f32[4,16,128]{2,1,0:T(8,128)S(1)}, u32[]{:S(2)}, u32[]{:S(2)}) collective-permute-start(f32[4,16,128]{2,1,0:T(8,128)S(1)} %get-tuple-element.51), channel_id=1, source_target_pairs={{0,192},{8,200},{16,208},{24,216},{32,224},{40,232},{48,240},{56,2... | collective-permute-start | bytes 98312 | tf_op jit(solution)/shard_map/ppermute | solution.py:335
  32.9 7.3 %collective-permute-start.3 = (f32[4,16,128]{2,1,0:T(8,128)S(1)}, f32[4,16,128]{2,1,0:T(8,128)S(1)}, u32[]{:S(2)}, u32[]{:S(2)}) collective-permute-start(f32[4,16,128]{2,1,0:T(8,128)S(1)} %get-tuple-element.51), channel_id=1, source_target_pairs={{0,96},{8,104},{16,112},{24,120},{32,128},{40,136},{48,144},{56,15... | collective-permute-start | bytes 98312 | tf_op jit(solution)/shard_map/ppermute | solution.py:335
  40.7 5.9 %collective-permute-start.8 = (f32[4,16,128]{2,1,0:T(8,128)S(1)}, f32[4,16,128]{2,1,0:T(8,128)S(1)}, u32[]{:S(2)}, u32[]{:S(2)}) collective-permute-start(f32[4,16,128]{2,1,0:T(8,128)S(1)} %get-tuple-element.53), channel_id=1, source_target_pairs={{0,16},{8,24},{16,0},{24,8},{32,48},{40,56},{48,32},{56,40},{64,80... | collective-permute-start | bytes 98312 | tf_op jit(solution)/shard_map/ppermute | solution.py:330
  43.0 8.0 %collective-permute-start.12 = (bf16[256,512]{1,0:T(8,128)(2,1)S(1)}, bf16[256,512]{1,0:T(8,128)(2,1)S(1)}, u32[]{:S(2)}, u32[]{:S(2)}) collective-permute-start(bf16[256,512]{1,0:T(8,128)(2,1)S(1)} %get-tuple-element.62.after_t), channel_id=1, source_target_pairs={{0,1},{1,2},{2,3},{3,0},{4,5},{5,6},{6,7},{7,4},{8,9},{9,10},{10,1... | collective-permute-start | bytes 786440 | tf_op jit(solution)/shard_map/ppermute | solution.py:313
  43.6 7.4 %collective-permute-start.13 = (bf16[256,512]{1,0:T(8,128)(2,1)S(1)}, bf16[256,512]{1,0:T(8,128)(2,1)S(1)}, u32[]{:S(2)}, u32[]{:S(2)}) collective-permute-start(bf16[256,512]{1,0:T(8,128)(2,1)S(1)} %get-tuple-element.63.after_b), channel_id=1, source_target_pairs={{0,3},{1,0},{2,1},{3,2},{4,7},{5,4},{6,5},{7,6},{8,11},{9,8},{10,9... | collective-permute-start | bytes 786440 | tf_op jit(solution)/shard_map/ppermute | solution.py:317
  52.7 19.0 %collective-permute-start.16 = (bf16[512,512]{1,0:T(8,128)(2,1)S(1)}, bf16[512,512]{1,0:T(8,128)(2,1)S(1)}, u32[]{:S(2)}, u32[]{:S(2)}) collective-permute-start(bf16[512,512]{1,0:T(8,128)(2,1)S(1)} %get-tuple-element.70), channel_id=1, source_target_pairs={{0,3},{1,0},{2,1},{3,2},{4,7},{5,4},{6,5},{7,6},{8,11},{9,8},{10,9... | collective-permute-start | bytes 1572872 | tf_op jit(solution)/shard_map/ppermute | solution.py:317
  56.4 15.3 %collective-permute-start.17 = (bf16[512,512]{1,0:T(8,128)(2,1)S(1)}, bf16[512,512]{1,0:T(8,128)(2,1)S(1)}, u32[]{:S(2)}, u32[]{:S(2)}) collective-permute-start(bf16[512,512]{1,0:T(8,128)(2,1)S(1)} %get-tuple-element.71), channel_id=1, source_target_pairs={{0,4},{1,5},{2,6},{3,7},{4,0},{5,1},{6,2},{7,3},{8,12},{9,13},{10,... | collective-permute-start | bytes 1572872 | tf_op jit(solution)/shard_map/ppermute | solution.py:309
  57.6 14.2 %collective-permute-start.15 = (bf16[512,512]{1,0:T(8,128)(2,1)S(1)}, bf16[512,512]{1,0:T(8,128)(2,1)S(1)}, u32[]{:S(2)}, u32[]{:S(2)}) collective-permute-start(bf16[512,512]{1,0:T(8,128)(2,1)S(1)} %get-tuple-element.66.after), channel_id=1, source_target_pairs={{0,1},{1,2},{2,3},{3,0},{4,5},{5,6},{6,7},{7,4},{8,9},{9,10},{10,1... | collective-permute-start | bytes 1572872 | tf_op jit(solution)/shard_map/ppermute | solution.py:313
  65.6 5.5 %collective-permute-start.18 = (f32[4,16,128]{2,1,0:T(8,128)S(1)}, f32[4,16,128]{2,1,0:T(8,128)S(1)}, u32[]{:S(2)}, u32[]{:S(2)}) collective-permute-start(f32[4,16,128]{2,1,0:T(8,128)S(1)} %get-tuple-element.68.after.pair), channel_id=1, source_target_pairs={{0,16},{8,24},{16,0},{24,8},{32,48},{40,56},{48,32},{56,40},{64,80... | collective-permute-start | bytes 98312 | tf_op jit(solution)/shard_map/ppermute | solution.py:330
  72.1 14.5 %collective-permute-start.21 = (bf16[256,512]{1,0:T(8,128)(2,1)S(1)}, bf16[256,512]{1,0:T(8,128)(2,1)S(1)}, u32[]{:S(2)}, u32[]{:S(2)}) collective-permute-start(bf16[256,512]{1,0:T(8,128)(2,1)S(1)} %get-tuple-element.80), channel_id=1, source_target_pairs={{0,1},{1,2},{2,3},{3,0},{4,5},{5,6},{6,7},{7,4},{8,9},{9,10},{10,1... | collective-permute-start | bytes 786440 | tf_op jit(solution)/shard_map/ppermute | solution.py:313
  73.8 12.8 %collective-permute-start.22 = (bf16[256,512]{1,0:T(8,128)(2,1)S(1)}, bf16[256,512]{1,0:T(8,128)(2,1)S(1)}, u32[]{:S(2)}, u32[]{:S(2)}) collective-permute-start(bf16[256,512]{1,0:T(8,128)(2,1)S(1)} %get-tuple-element.81), channel_id=1, source_target_pairs={{0,3},{1,0},{2,1},{3,2},{4,7},{5,4},{6,5},{7,6},{8,11},{9,8},{10,9... | collective-permute-start | bytes 786440 | tf_op jit(solution)/shard_map/ppermute | solution.py:317
  83.1 16.3 %collective-permute-start.19 = (bf16[512,512]{1,0:T(8,128)(2,1)S(1)}, bf16[512,512]{1,0:T(8,128)(2,1)S(1)}, u32[]{:S(2)}, u32[]{:S(2)}) collective-permute-start(bf16[512,512]{1,0:T(8,128)(2,1)S(1)} %get-tuple-element.77), channel_id=1, source_target_pairs={{0,1},{1,2},{2,3},{3,0},{4,5},{5,6},{6,7},{7,4},{8,9},{9,10},{10,1... | collective-permute-start | bytes 1572872 | tf_op jit(solution)/shard_map/ppermute | solution.py:313
  83.7 15.6 %collective-permute-start.20 = (bf16[512,512]{1,0:T(8,128)(2,1)S(1)}, bf16[512,512]{1,0:T(8,128)(2,1)S(1)}, u32[]{:S(2)}, u32[]{:S(2)}) collective-permute-start(bf16[512,512]{1,0:T(8,128)(2,1)S(1)} %get-tuple-element.78), channel_id=1, source_target_pairs={{0,3},{1,0},{2,1},{3,2},{4,7},{5,4},{6,5},{7,6},{8,11},{9,8},{10,9... | collective-permute-start | bytes 1572872 | tf_op jit(solution)/shard_map/ppermute | solution.py:317
  86.7 12.6 %collective-permute-start.25 = (bf16[512,512]{1,0:T(8,128)(2,1)S(1)}, bf16[512,512]{1,0:T(8,128)(2,1)S(1)}, u32[]{:S(2)}, u32[]{:S(2)}) collective-permute-start(bf16[512,512]{1,0:T(8,128)(2,1)S(1)} %shard_map.125), channel_id=1, source_target_pairs={{0,4},{1,5},{2,6},{3,7},{4,0},{5,1},{6,2},{7,3},{8,12},{9,13},{10,... | collective-permute-start | bytes 1572872 | tf_op jit(solution)/shard_map/ppermute | solution.py:309
  87.4 6.0 %collective-permute-start.27 = (f32[4,16,128]{2,1,0:T(8,128)S(1)}, f32[4,16,128]{2,1,0:T(8,128)S(1)}, u32[]{:S(2)}, u32[]{:S(2)}) collective-permute-start(f32[4,16,128]{2,1,0:T(8,128)S(1)} %get-tuple-element.82.after), channel_id=1, source_target_pairs={{0,64},{8,72},{16,80},{24,88},{32,96},{40,104},{48,112},{56,120},{... | collective-permute-start | bytes 98312 | tf_op jit(solution)/shard_map/ppermute | solution.py:335
  87.6 6.0 %collective-permute-start.26 = (f32[4,16,128]{2,1,0:T(8,128)S(1)}, f32[4,16,128]{2,1,0:T(8,128)S(1)}, u32[]{:S(2)}, u32[]{:S(2)}) collective-permute-start(f32[4,16,128]{2,1,0:T(8,128)S(1)} %get-tuple-element.82.after), channel_id=1, source_target_pairs={{0,160},{8,168},{16,176},{24,184},{32,192},{40,200},{48,208},{56,2... | collective-permute-start | bytes 98312 | tf_op jit(solution)/shard_map/ppermute | solution.py:335
  (11 other events, 118.5 us)

commit v2 on v1

v2 whole, which is shorter than its diff:
```python
import functools

import jax
import jax.numpy as jnp
from jax import lax
from jax.experimental import pallas as pl
from jax.experimental.pallas import tpu as pltpu
from jax.sharding import PartitionSpec as P

F32, BF16 = jnp.float32, jnp.bfloat16
ROWS, COLS, MODES, LANES = 512, 512, 16, 128
HALF = ROWS // 2
TILES = COLS // LANES
PARTS = 8
STEP = ROWS // PARTS
APART = STEP + 8
VMEM = pl.BlockSpec(memory_space=pltpu.VMEM)
SMEM = pl.BlockSpec(memory_space=pltpu.SMEM)


def tile_of(tile):
    return slice(tile * LANES, (tile + 1) * LANES)


def spread(ref, tile, mode):
    return jnp.broadcast_to(ref[tile, mode : mode + 1, :], (PARTS, LANES))


def lay(table, tile, values):
    for piece in range(PARTS):
        rows = slice(piece * APART, piece * APART + STEP)
        table[tile, rows, :] = values[piece * STEP : (piece + 1) * STEP, :]


def laid(table, tile):
    starts = range(0, PARTS * APART, APART)
    return jnp.concatenate([table[tile, start : start + STEP, :] for start in starts])


def ends_of(signal, ends, keep, tile, flipped):
    decay = [spread(keep, tile, m) for m in range(MODES)]

    def step(i, states):
        at = STEP - 1 - i if flipped else i
        u = signal[tile, pl.ds(at, PARTS, stride=APART), :]
        return tuple(decay[m] * states[m] + u for m in range(MODES))

    zero = jnp.zeros((PARTS, LANES), F32)
    states = lax.fori_loop(0, STEP, step, (zero,) * MODES, unroll=16)
    for m in range(MODES):
        ends[tile, pl.ds(m, PARTS, stride=MODES), :] = states[m]


def chain(ends, starts, total, keep_piece, tile, flipped):
    state = jnp.zeros((MODES, LANES), F32)
    factor = keep_piece[tile]
    order = range(PARTS - 1, -1, -1) if flipped else range(PARTS)
    for piece in order:
        rows = slice(piece * MODES, (piece + 1) * MODES)
        starts[tile, rows, :] = state
        state = factor * state + ends[tile, rows, :]
    total[tile] = state


def whole_starts(starts, initial, begin, keep_piece, tile, flipped):
    carried = initial
    factor = keep_piece[tile]
    order = range(PARTS - 1, -1, -1) if flipped else range(PARTS)
    for piece in order:
        rows = slice(piece * MODES, (piece + 1) * MODES)
        begin[tile, rows, :] = starts[tile, rows, :] + carried
        carried = factor * carried


def responses(signal, begin, result, keep, gain, tile, flipped):
    decay = [spread(keep, tile, m) for m in range(MODES)]
    gains = [spread(gain, tile, m) for m in range(MODES)]

    def step(i, states):
        at = STEP - 1 - i if flipped else i
        u = signal[tile, pl.ds(at, PARTS, stride=APART), :]
        states = tuple(decay[m] * states[m] + u for m in range(MODES))
        terms = [gains[m] * states[m] for m in range(MODES)]
        while len(terms) > 1:
            terms = [terms[i] + terms[i + 1] for i in range(0, len(terms), 2)]
        result[tile, pl.ds(at, PARTS, stride=APART), :] = terms[0]
        return states

    states = tuple(begin[tile, pl.ds(m, PARTS, stride=MODES), :] for m in range(MODES))
    lax.fori_loop(0, STEP, step, states, unroll=16)


def dot(a, b):
    return jnp.dot(a, b, preferred_element_type=F32)


def turned(a, b):
    return lax.dot_general(a, b, (((1,), (1,)), ((), ())), preferred_element_type=F32)


def wide(value):
    return value.astype(F32)


def columns(weight, place, which):
    return weight[:, pl.ds(pl.multiple_of(place[which] * COLS, COLS), COLS)]


NEAR = [(0, 0), (1, 0), (0, -1), (0, 1), (1, -1), (1, 1), (0, 2), (1, 2)]
OWN, ACROSS, BEHIND, AHEAD, ACROSS_BEHIND, ACROSS_AHEAD, FAR, ACROSS_FAR = range(8)
TOP, BOTTOM = slice(0, HALF), slice(HALF, ROWS)
FIRST, SECOND = slice(0, ROWS), slice(ROWS, 2 * ROWS)
PER_TILE = range(TILES)


def gate_kernel(
    spot, place, gated, decay_rates, amplitude, rates, keep, keep_piece, gain, starts, total, signal, ends,
):
    for tile in PER_TILE:
        at = tile_of(tile)
        rates[tile] = decay_rates[:, at]
        gain[tile] = amplitude[:, at]
        keep[tile] = jnp.exp(-rates[tile])
        keep_piece[tile] = jnp.exp(rates[tile] * -float(STEP))
        lay(signal, tile, wide(gated[:, at]))
        ends_of(signal, ends, keep, tile, False)
        chain(ends, starts, total, keep_piece, tile, False)


def power(rates, n):
    return jnp.exp(rates * (-float(ROWS) * jnp.asarray(n).astype(F32)))


def spot_of(spot, flipped):
    core, high, z = spot[0], spot[1], spot[2]
    return (1 - core, 1 - high, 7 - z) if flipped else (core, high, z)


def pair_kernel(flipped, spot, rates, own, other, pair, before):
    core, _, _ = spot_of(spot, flipped)
    pair[...] = power(rates[...], 1 - core) * own[...] + power(rates[...], core) * other[...]
    before[...] = core.astype(F32) * other[...]


def three_kernel(flipped, spot, rates, pair, one_off, two_off, two, three):
    _, _, z = spot_of(spot, flipped)
    here = (z >= 1).astype(F32) * one_off[...]
    here += (z >= 2).astype(F32) * (power(rates[...], 4) * two_off[...])
    two[...] = here
    three[...] = pair[...] + power(rates[...], 4) * here


def over_of(rates, z, two, three_off, six_off):
    here = two + (z >= 3).astype(F32) * (power(rates, 8) * three_off)
    return here + (z >= 6).astype(F32) * (power(rates, 20) * six_off)


def sent_kernel(flipped, spot, rates, pair, two, three_off, six_off, after, over, sent):
    _, high, z = spot_of(spot, flipped)
    here = over_of(rates[...], z, two[...], three_off[...], six_off[...])
    over[...] = here
    later = high.astype(F32)
    sent[...] = later * here + (1.0 - later) * (pair[...] + power(rates[...], 4) * here)


def group_kernel(flipped, spot, rates, pair, before, other, group, before_all):
    core, high, _ = spot_of(spot, flipped)
    early, late = power(rates[...], 2 - 2 * high), power(rates[...], 2 * high)
    group[...] = early * pair[...] + late * other[...]
    before_all[...] = before[...] + high.astype(F32) * (power(rates[...], core) * other[...])


def pack_kernel(across, behind, ahead, after, out):
    out[FIRST, :] = across[...]
    out[SECOND, :] = behind[...]


def halve_kernel(got, after, out):
    out[...] = got[FIRST, :]


def mix_kernel(
    spot, rates, other, over, before,
    gated, starts, keep, keep_piece, gain, skip, query, after,
    summed, mixed_in,
    signal, result, begin,
):
    for tile in PER_TILE:
        at = tile_of(tile)
        lay(signal, tile, wide(gated[:, at]))
        core, _, _ = spot_of(spot, False)
        initial = other[tile] + power(rates[tile], 2) * over[tile]
        initial = power(rates[tile], core) * initial + before[tile]
        whole_starts(starts, initial, begin, keep_piece, tile, False)
        responses(signal, begin, result, keep, gain, tile, False)
        conv = wide(laid(result, tile).astype(BF16))
        total = conv + skip[0:1, at] * wide(gated[:, at])
        summed[:, at] = total
        mixed_in[:, at] = (wide(query[:, at]) * total).astype(BF16)


def products(mixed_in, weight, place, outs):
    for out, start, which in outs:
        for rows in (TOP, BOTTOM):
            part = dot(mixed_in[rows, :], columns(weight, place, which))
            out[start + rows.start : start + rows.stop, :] = part.astype(BF16)


def first_kernel(place, mixed_in, weight, after, along, over):
    outs = ((along, 0, ACROSS_FAR), (along, ROWS, FAR), (over, 0, ACROSS_BEHIND))
    products(mixed_in, weight, place, outs)


def rest_kernel(place, mixed_in, weight, after, side, ahead, behind, across, own):
    outs = ((side, 0, ACROSS_AHEAD), (ahead, 0, AHEAD), (behind, 0, BEHIND))
    products(mixed_in, weight, place, outs + ((across, 0, ACROSS), (own, 0, OWN)))


def second_kernel(along, over, side, ahead, behind, after, side_out, ahead_out, behind_out):
    side_out[...] = (wide(side[...]) + wide(along[FIRST, :])).astype(BF16)
    ahead_out[...] = (wide(ahead[...]) + wide(along[SECOND, :])).astype(BF16)
    behind_out[...] = (wide(behind[...]) + wide(over[...])).astype(BF16)


def third_kernel(across, got, after, out):
    out[...] = (wide(across[...]) + wide(got[...])).astype(BF16)


def last_kernel(own, ahead, behind, across, out):
    inner = wide(own[...]) + wide(ahead[...])
    out[...] = (inner + (wide(behind[...]) + wide(across[...]))).astype(BF16)


def early_kernel(place, weight, own, across, behind, ahead, after, acc):
    blocks = ((own, OWN), (across, ACROSS), (behind, BEHIND), (ahead, AHEAD))
    for rows in (TOP, BOTTOM):
        grad = jnp.zeros((HALF, COLS), F32)
        for ref, which in blocks:
            grad += turned(ref[rows, :], columns(weight, place, which))
        acc[rows, :] = grad


def grad_kernel(
    place, weight, acc, got, over, far, query, summed, keep, keep_piece, after,
    grad_query, grad_conv, starts, total,
    full, signal, ends,
):
    parts = ((got, 0, ACROSS_BEHIND), (got, ROWS, FAR), (over, 0, ACROSS_AHEAD), (far, 0, ACROSS_FAR))
    for rows in (TOP, BOTTOM):
        grad = acc[rows, :]
        for ref, start, which in parts:
            block = ref[start + rows.start : start + rows.stop, :]
            grad += turned(block, columns(weight, place, which))
        full[rows, :] = grad
    for tile in PER_TILE:
        at = tile_of(tile)
        grad_query[:, at] = (full[:, at] * summed[:, at]).astype(BF16)
        conv = (full[:, at] * wide(query[:, at])).astype(BF16)
        grad_conv[:, at] = conv
        lay(signal, tile, wide(conv))
        ends_of(signal, ends, keep, tile, True)
        chain(ends, starts, total, keep_piece, tile, True)


def back_kernel(
    spot, rates, two, three_off, six_off, before,
    grad_conv, starts, keep, keep_piece, gain, skip, key, value,
    grad_key, grad_value,
    signal, result, begin,
):
    for tile in PER_TILE:
        at = tile_of(tile)
        lay(signal, tile, wide(grad_conv[:, at]))
        core, high, z = spot_of(spot, True)
        over = over_of(rates[tile], z, two[tile], three_off[tile], six_off[tile])
        initial = power(rates[tile], 2 * high + core) * over + before[tile]
        whole_starts(starts, initial, begin, keep_piece, tile, True)
        responses(signal, begin, result, keep, gain, tile, True)
        back = wide(laid(result, tile).astype(BF16))
        total = back + skip[0:1, at] * wide(grad_conv[:, at])
        grad_key[:, at] = (total * wide(value[:, at])).astype(BF16)
        grad_value[:, at] = (total * wide(key[:, at])).astype(BF16)


STATE_SHAPE, BLOCK, TWICE = (TILES, MODES, LANES), (ROWS, COLS), (2 * ROWS, COLS)
TABLE, DEEP = (TILES, PARTS * MODES, LANES), (TILES, PARTS * APART, LANES)


def call(kernel, outs, scratch, micros, mib, *args):
    return pl.pallas_call(
        kernel,
        out_shape=[jax.ShapeDtypeStruct(shape, kind) for shape, kind in outs],
        in_specs=[SMEM if arg.dtype == jnp.int32 else VMEM for arg in args],
        out_specs=[VMEM] * len(outs),
        scratch_shapes=[pltpu.VMEM(shape, kind) for shape, kind in scratch],
        cost_estimate=pl.CostEstimate(
            flops=int(micros * 1.1e9), bytes_accessed=int(micros * 3e6), transcendentals=0
        ),
        compiler_params=pltpu.CompilerParams(vmem_limit_bytes=mib * 1024 * 1024),
    )(*args)


def ctx_perm(move):
    pairs = []
    for z in range(8):
        for h in range(2):
            for c in range(2):
                to = move(z, h, c)
                pairs.append((z * 4 + h * 2 + c, to[0] % 8 * 4 + to[1] % 2 * 2 + to[2] % 2))
    return pairs


def shift_x(value):
    return lax.ppermute(value, "tp", [(at, (at + 4) % 8) for at in range(8)])


def along_y(value, turn):
    pairs = []
    for line in range(32):
        step = turn * (1 - 2 * (line % 2))
        for at in range(8):
            pairs.append((line * 8 + at, line * 8 + at // 4 * 4 + (at + step) % 4))
    return lax.ppermute(value, ("ctx", "tp"), pairs)


def small(kernel, flipped, *args):
    both = [(STATE_SHAPE, F32)] * 2
    return call(functools.partial(kernel, flipped), both, [], 1.0, 4, *args)


def other_core(value):
    return lax.ppermute(value, "ctx", ctx_perm(lambda z, h, c: (z, h, c + 1)))


def other_half(value):
    return lax.ppermute(value, "ctx", ctx_perm(lambda z, h, c: (z, h + 1, c)))


def earlier(value, k, flipped):
    move = -k if flipped else k
    return lax.ppermute(value, "ctx", ctx_perm(lambda z, h, c: (z + move, h, c)))


def per_device(query, key, value, cotangent, weight, decay_rates, residues, skip_gain):
    at, line = lax.axis_index("tp"), lax.axis_index("ctx")
    x, y = at // 4, at % 4
    step = 1 - 2 * (line % 2)
    place = [(x + dx) % 2 * 4 + (y + step * dy + 4) % 4 for dx, dy in NEAR]
    place = jnp.stack(place).astype(jnp.int32)
    spot = jnp.stack([line % 2, line // 2 % 2, line // 4]).astype(jnp.int32)
    decay_rates, residues = decay_rates.T, residues.T
    amplitude = residues * jnp.sqrt(-jnp.expm1(-2.0 * decay_rates))
    skip = skip_gain.reshape(1, COLS)

    across = shift_x(cotangent)
    behind = along_y(cotangent, 1)
    ahead = along_y(cotangent, -1)

    deep, table, state = (DEEP, F32), (TABLE, F32), (STATE_SHAPE, F32)
    gated = (key.astype(F32) * value.astype(F32)).astype(BF16)
    rates, keep, keep_piece, gain, starts, total = call(
        gate_kernel, [state] * 4 + [table, state], [deep, table], 2.4, 6, spot, place, gated, decay_rates, amplitude
    )
    pair, before = small(pair_kernel, False, spot, rates, total, other_core(total))
    offs = earlier(pair, 1, False), earlier(pair, 2, False)
    (packed,) = call(pack_kernel, [(TWICE, BF16)], [], 1.0, 4, across, behind, ahead, offs[0])
    got, over = along_y(packed, 1), shift_x(ahead)
    (s_far,) = call(halve_kernel, [(BLOCK, BF16)], [], 1.0, 4, got, over)
    far = along_y(s_far, 1)
    (acc,) = call(
        early_kernel,
        [(BLOCK, F32)],
        [],
        2.0,
        6,
        place,
        weight,
        cotangent,
        across,
        behind,
        ahead,
        packed,
    )

    two, three = small(three_kernel, False, spot, rates, pair, *offs)
    offs = earlier(three, 3, False), earlier(three, 6, False)
    over_state, sent = small(sent_kernel, False, spot, rates, pair, two, *offs, acc)
    carried = other_half(sent), over_state, before
    summed, mixed_in = call(
        mix_kernel,
        [(BLOCK, F32), (BLOCK, BF16)],
        [deep, deep, table],
        4.5,
        8,
        spot,
        rates,
        *carried,
        gated,
        starts,
        keep,
        keep_piece,
        gain,
        skip,
        query,
        s_far,
    )
    s_along, s_over = call(
        first_kernel,
        [(TWICE, BF16), (BLOCK, BF16)],
        [],
        1.5,
        6,
        place,
        mixed_in,
        weight,
        far,
    )
    g_along, g_over = along_y(s_along, 1), shift_x(s_over)
    grad_query, grad_conv, back_starts, back_total = call(
        grad_kernel,
        [(BLOCK, BF16), (BLOCK, BF16), table, state],
        [(BLOCK, F32), deep, table],
        6.0,
        8,
        place,
        weight,
        acc,
        got,
        over,
        far,
        query,
        summed,
        keep,
        keep_piece,
        s_along,
    )
    pair, before = small(pair_kernel, True, spot, rates, back_total, other_core(back_total))
    half_other = other_half(pair)
    side, ahead_part, behind_part, across_part, own_part = call(
        rest_kernel, [(BLOCK, BF16)] * 5, [], 2.0, 6, place, mixed_in, weight, pair
    )
    group, before = small(group_kernel, True, spot, rates, pair, before, half_other)
    offs = earlier(group, 1, True), earlier(group, 2, True)
    two, three = small(three_kernel, True, spot, rates, group, *offs)
    offs = earlier(three, 3, True), earlier(three, 6, True)

    s_side, s_ahead, s_behind = call(
        second_kernel,
        [(BLOCK, BF16)] * 3,
        [],
        3.0,
        4,
        g_along,
        g_over,
        side,
        ahead_part,
        behind_part,
        group,
    )
    g_side, g_ahead, g_behind = along_y(s_side, 1), along_y(s_ahead, 1), along_y(s_behind, -1)
    (s_across,) = call(third_kernel, [(BLOCK, BF16)], [], 0.5, 4, across_part, g_side, three)
    (mixed,) = call(
        last_kernel, [(BLOCK, BF16)], [], 0.5, 4, own_part, g_ahead, g_behind, shift_x(s_across)
    )
    grad_key, grad_value = call(
        back_kernel,
        [(BLOCK, BF16)] * 2,
        [deep, deep, table],
        4.5,
        8,
        spot,
        rates,
        two,
        *offs,
        before,
        grad_conv,
        back_starts,
        keep,
        keep_piece,
        gain,
        skip,
        key,
        value,
    )
    return mixed, grad_query, grad_key, grad_value


def solution(mesh):
    split, rows = P("ctx", "tp"), P("tp", None)
    return jax.shard_map(
        per_device,
        mesh=mesh,
        in_specs=(split, split, split, split, rows, rows, rows, P("tp")),
        out_specs=(split, split, split, split),
        check_vma=False,
    )
```

time: 102 us -> 95.4 us (0.935)
  the two profiles are of different devices: /device:TPU:2 before, /device:TPU:64 now
where the time goes in v2:
time: 95.4 us; the launch traced here: 95.1 us
  starting transfers between devices  44.6 us (47%)
  Pallas kernels  24.8 us (26%)
  waiting for transfers between devices  21.8 us (23%)
  other arithmetic  2.21 us (2%)
    pallas_call x18, Pallas kernels, call(): pl.pallas_call(kernel, out_shape=[jax.ShapeDtypeStruct(shape, kind) for s...  24.8 us
    ppermute x8, starting transfers between devices, earlier(): lax.ppermute(value, 'ctx', ctx_perm(lambda z, h, c: (z + move, h, c)))  22.4 us
    ppermute x8, waiting for transfers between devices, earlier(): lax.ppermute(value, 'ctx', ctx_perm(lambda z, h, c: (z + move, h, c)))  12.9 us
    ppermute x8, starting transfers between devices, along_y(): return lax.ppermute(value, ('ctx', 'tp'), pairs)  9.62 us
    ppermute x2, starting transfers between devices, other_half(): return lax.ppermute(value, 'ctx', ctx_perm(lambda z, h, c: (z, h + 1, c)))  6.51 us
    ppermute x4, starting transfers between devices, shift_x(): return lax.ppermute(value, 'tp', [(at, (at + 4) % 8) for at in range(8)])  5.97 us
    ppermute x8, waiting for transfers between devices, along_y(): return lax.ppermute(value, ('ctx', 'tp'), pairs)  2.88 us
    ppermute x2, waiting for transfers between devices, other_half(): return lax.ppermute(value, 'ctx', ctx_perm(lambda z, h, c: (z, h + 1, c)))  2.6 us
  transfers between devices with their start and end apart: 24, of which 14 were waited for; matrix products, arithmetic and copies ran while one was open for 2% of the time, Pallas kernels for 23%

profile of v2, /device:TPU:64, one launch (start us, length us, event | category | flops | bytes accessed | tf_op | source)
XLA Modules:
  0.0 95.1 jit_solution(12961553779641647956)
XLA Ops:
  0.6 1.7 %collective-permute-start.6 = (bf16[512,512]{1,0:T(8,128)(2,1)}, bf16[512,512]{1,0:T(8,128)(2,1)S(1)}, u32[]{:S(2)}, u32[]{:S(2)}) collective-permute-start(bf16[512,512]{1,0:T(8,128)(2,1)} %own.1), channel_id=1, source_target_pairs={{0,1},{1,2},{2,3},{3,0},{4,5},{5,6},{6,7},{7,4},{8,11},{9,8},{10,9... | collective-permute-start | bytes 1572872 | tf_op jit(solution)/shard_map/ppermute | solution.py:323
  3.8 1.7 %collective-permute-start.7 = (bf16[512,512]{1,0:T(8,128)(2,1)}, bf16[512,512]{1,0:T(8,128)(2,1)S(1)}, u32[]{:S(2)}, u32[]{:S(2)}) collective-permute-start(bf16[512,512]{1,0:T(8,128)(2,1)} %own.1), channel_id=1, source_target_pairs={{0,3},{1,0},{2,1},{3,2},{4,7},{5,4},{6,5},{7,6},{8,9},{9,10},{10,1... | collective-permute-start | bytes 1572872 | tf_op jit(solution)/shard_map/ppermute | solution.py:323
  8.5 1.9 %shard_map.111 = (f32[4,16,128]{2,1,0:T(8,128)S(1)}, f32[4,16,128]{2,1,0:T(8,128)S(1)}, f32[4,16,128]{2,1,0:T(8,128)S(1)}, f32[4,16,128]{2,1,0:T(8,128)S(1)}, f3...) custom-call(s32[3]{0:T(128)S(1)} %pad_add_fusion.spot, s32[8]{0:T(128)S(1)} %stack.47.place, ...), custom_call_target="tpu_custom_call" | custom-call | flops 2640000000 | bytes 7200000 | tf_op jit(solution)/shard_map/pallas_call | solution.py:290
  12.3 2.0 %collective-permute-start.1 = (f32[4,16,128]{2,1,0:T(8,128)S(1)}, f32[4,16,128]{2,1,0:T(8,128)S(1)}, u32[]{:S(2)}, u32[]{:S(2)}) collective-permute-start(f32[4,16,128]{2,1,0:T(8,128)S(1)} %get-tuple-element.42.pair), channel_id=1, source_target_pairs={{0,32},{8,40},{16,48},{24,56},{32,64},{40,72},{48,80},{56,88},{64,... | collective-permute-start | bytes 98312 | tf_op jit(solution)/shard_map/ppermute | solution.py:341
  14.3 2.0 %collective-permute-done.1.one_off.after = f32[4,16,128]{2,1,0:T(8,128)S(1)} collective-permute-done((f32[4,16,128]{2,1,0:T(8,128)S(1)}, f32[4,16,128]{2,1,0:T(8,128)S(1)}, u32[]{:S(2)}, u32[]{:S(2)}) %collective-permute-start.1) | collective-permute-done | bytes 32800 | tf_op jit(solution)/shard_map/ppermute | solution.py:341
  19.0 4.5 %collective-permute-start.2 = (f32[4,16,128]{2,1,0:T(8,128)S(1)}, f32[4,16,128]{2,1,0:T(8,128)S(1)}, u32[]{:S(2)}, u32[]{:S(2)}) collective-permute-start(f32[4,16,128]{2,1,0:T(8,128)S(1)} %get-tuple-element.42.pair), channel_id=1, source_target_pairs={{0,64},{8,72},{16,80},{24,88},{32,96},{40,104},{48,112},{56,120},{... | collective-permute-start | bytes 98312 | tf_op jit(solution)/shard_map/ppermute | solution.py:341
  25.7 1.9 %collective-permute-start.4 = (f32[4,16,128]{2,1,0:T(8,128)S(1)}, f32[4,16,128]{2,1,0:T(8,128)S(1)}, u32[]{:S(2)}, u32[]{:S(2)}) collective-permute-start(f32[4,16,128]{2,1,0:T(8,128)S(1)} %get-tuple-element.44), channel_id=1, source_target_pairs={{0,192},{8,200},{16,208},{24,216},{32,224},{40,232},{48,240},{56,2... | collective-permute-start | bytes 98312 | tf_op jit(solution)/shard_map/ppermute | solution.py:341
  27.5 3.2 %collective-permute-start.3 = (f32[4,16,128]{2,1,0:T(8,128)S(1)}, f32[4,16,128]{2,1,0:T(8,128)S(1)}, u32[]{:S(2)}, u32[]{:S(2)}) collective-permute-start(f32[4,16,128]{2,1,0:T(8,128)S(1)} %get-tuple-element.44), channel_id=1, source_target_pairs={{0,96},{8,104},{16,112},{24,120},{32,128},{40,136},{48,144},{56,15... | collective-permute-start | bytes 98312 | tf_op jit(solution)/shard_map/ppermute | solution.py:341
  30.7 1.8 %shard_map.115.after.acc = f32[512,512]{1,0:T(8,128)S(1)} custom-call(s32[8]{0:T(128)S(1)} %stack.47.place, bf16[512,4096]{1,0:T(8,128)(2,1)S(1)} %copy-done, bf16[512,512]{1,0:T(8,128)(2,1)S(1)} %copy-done.1, bf16[512,512]{1,0:T(8,128)(2,1)S(1)} %collective-permute-done.5.across, bf16[512,512]{1,0:T(8,128)(2,1)S(1)} %collective-permute-done.6.behind, ...), custom_call_target="tpu_custom_call" | custom-call | flops 2200000000 | bytes 6000000 | tf_op jit(solution)/shard_map/pallas_call | solution.py:290
  35.6 3.6 %collective-permute-start.8 = (f32[4,16,128]{2,1,0:T(8,128)S(1)}, f32[4,16,128]{2,1,0:T(8,128)S(1)}, u32[]{:S(2)}, u32[]{:S(2)}) collective-permute-start(f32[4,16,128]{2,1,0:T(8,128)S(1)} %get-tuple-element.45), channel_id=1, source_target_pairs={{0,16},{8,24},{16,0},{24,8},{32,48},{40,56},{48,32},{56,40},{64,80... | collective-permute-start | bytes 98312 | tf_op jit(solution)/shard_map/ppermute | solution.py:336
  39.1 2.1 %collective-permute-done.8.other = f32[4,16,128]{2,1,0:T(8,128)S(1)} collective-permute-done((f32[4,16,128]{2,1,0:T(8,128)S(1)}, f32[4,16,128]{2,1,0:T(8,128)S(1)}, u32[]{:S(2)}, u32[]{:S(2)}) %collective-permute-start.8) | collective-permute-done | bytes 32800 | tf_op jit(solution)/shard_map/ppermute | solution.py:336
  41.3 3.5 %shard_map.118 = (f32[512,512]{1,0:T(8,128)S(1)}, bf16[512,512]{1,0:T(8,128)(2,1)S(1)}) custom-call(s32[3]{0:T(128)S(1)} %pad_add_fusion.spot, f32[4,16,128]{2,1,0:T(8,128)S(1)} %get-tuple-element.40.rates, f32[4,16,128]{2,1,0:T(8,128)S(1)} %collective-permute-done.8.other, f32[4,16,128]{2,1,0:T(8,128)S(1)} %get-tuple-element.46.over, ...), custom_call_target="tpu_custom_call" | custom-call | flops 4950000128 | bytes 13500000 | tf_op jit(solution)/shard_map/pallas_call | solution.py:290
  47.3 1.8 %collective-permute-start.13 = (bf16[1024,512]{1,0:T(8,128)(2,1)S(1)}, bf16[1024,512]{1,0:T(8,128)(2,1)S(1)}, u32[]{:S(2)}, u32[]{:S(2)}) collective-permute-start(bf16[1024,512]{1,0:T(8,128)(2,1)S(1)} %get-tuple-element.54.after), channel_id=1, source_target_pairs={{0,1},{1,2},{2,3},{3,0},{4,5},{5,6},{6,7},{7,4},{8,11},{9,8},{10,9... | collective-permute-start | bytes 3145736 | tf_op jit(solution)/shard_map/ppermute | solution.py:323
  49.1 4.3 %shard_map.120 = (bf16[512,512]{1,0:T(8,128)(2,1)}, bf16[512,512]{1,0:T(8,128)(2,1)S(1)}, f32[4,128,128]{2,1,0:T(8,128)S(1)}, f32[4,16,128]{2,1,0:T(8,128)S(1)}) custom-call(s32[8]{0:T(128)S(1)} %stack.47.place, bf16[512,4096]{1,0:T(8,128)(2,1)S(1)} %copy-done, f32[512,512]{1,0:T(8,128)S(1)} %shard_map.115.after.acc, ...), custom_call_target="tpu_custom_call" | custom-call | flops 6600000000 | bytes 18000000 | tf_op jit(solution)/shard_map/pallas_call | solution.py:290
  55.2 3.0 %collective-permute-start.15 = (f32[4,16,128]{2,1,0:T(8,128)S(1)}, f32[4,16,128]{2,1,0:T(8,128)S(1)}, u32[]{:S(2)}, u32[]{:S(2)}) collective-permute-start(f32[4,16,128]{2,1,0:T(8,128)S(1)} %get-tuple-element.56.after.pair), channel_id=1, source_target_pairs={{0,16},{8,24},{16,0},{24,8},{32,48},{40,56},{48,32},{56,40},{64,80... | collective-permute-start | bytes 98312 | tf_op jit(solution)/shard_map/ppermute | solution.py:336
  58.2 2.1 %shard_map.122 = (bf16[512,512]{1,0:T(8,128)(2,1)S(1)}, bf16[512,512]{1,0:T(8,128)(2,1)S(1)}, bf16[512,512]{1,0:T(8,128)(2,1)S(1)}, bf16[512,512]{1,0:T(8,128)(2,1)S(1)}, bf16[512,512]{1,0:T(8,128)(2,1)S(1)}) custom-call(s32[8]{0:T(128)S(1)} %stack.47.place, bf16[512,512]{1,0:T(8,128)(2,1)S(1)} %get-tuple-element.52.mixed_in, bf16[512,4096]{1,0:T(8,128)(2,1)S(1)} %copy-done, ...), custom_call_target="tpu_custom_call" | custom-call | flops 2200000000 | bytes 6000000 | tf_op jit(solution)/shard_map/pallas_call | solution.py:290
  61.3 2.0 %collective-permute-done.13.along = bf16[1024,512]{1,0:T(8,128)(2,1)S(1)} collective-permute-done((bf16[1024,512]{1,0:T(8,128)(2,1)S(1)}, bf16[1024,512]{1,0:T(8,128)(2,1)S(1)}, u32[]{:S(2)}, u32[]{:S(2)}) %collective-permute-start.13) | collective-permute-done | bytes 1048608 | tf_op jit(solution)/shard_map/ppermute | solution.py:323
  64.4 2.1 %collective-permute-start.20 = (f32[4,16,128]{2,1,0:T(8,128)S(1)}, f32[4,16,128]{2,1,0:T(8,128)S(1)}, u32[]{:S(2)}, u32[]{:S(2)}) collective-permute-start(f32[4,16,128]{2,1,0:T(8,128)S(1)} %get-tuple-element.63.after.pair), channel_id=1, source_target_pairs={{0,192},{8,200},{16,208},{24,216},{32,224},{40,232},{48,240},{56,2... | collective-permute-start | bytes 98312 | tf_op jit(solution)/shard_map/ppermute | solution.py:341
  66.5 2.6 %collective-permute-start.19 = (f32[4,16,128]{2,1,0:T(8,128)S(1)}, f32[4,16,128]{2,1,0:T(8,128)S(1)}, u32[]{:S(2)}, u32[]{:S(2)}) collective-permute-start(f32[4,16,128]{2,1,0:T(8,128)S(1)} %get-tuple-element.63.after.pair), channel_id=1, source_target_pairs={{0,224},{8,232},{16,240},{24,248},{32,0},{40,8},{48,16},{56,24},{6... | collective-permute-start | bytes 98312 | tf_op jit(solution)/shard_map/ppermute | solution.py:341
  72.3 2.3 %collective-permute-start.17 = (bf16[512,512]{1,0:T(8,128)(2,1)S(1)}, bf16[512,512]{1,0:T(8,128)(2,1)S(1)}, u32[]{:S(2)}, u32[]{:S(2)}) collective-permute-start(bf16[512,512]{1,0:T(8,128)(2,1)S(1)} %get-tuple-element.65), channel_id=1, source_target_pairs={{0,3},{1,0},{2,1},{3,2},{4,7},{5,4},{6,5},{7,6},{8,9},{9,10},{10,1... | collective-permute-start | bytes 1572872 | tf_op jit(solution)/shard_map/ppermute | solution.py:323
  74.8 1.9 %collective-permute-start.21 = (bf16[512,512]{1,0:T(8,128)(2,1)S(1)}, bf16[512,512]{1,0:T(8,128)(2,1)S(1)}, u32[]{:S(2)}, u32[]{:S(2)}) collective-permute-start(bf16[512,512]{1,0:T(8,128)(2,1)S(1)} %shard_map.126), channel_id=1, source_target_pairs={{0,4},{1,5},{2,6},{3,7},{4,0},{5,1},{6,2},{7,3},{8,12},{9,13},{10,... | collective-permute-start | bytes 1572872 | tf_op jit(solution)/shard_map/ppermute | solution.py:314
  76.6 5.5 %collective-permute-start.23 = (f32[4,16,128]{2,1,0:T(8,128)S(1)}, f32[4,16,128]{2,1,0:T(8,128)S(1)}, u32[]{:S(2)}, u32[]{:S(2)}) collective-permute-start(f32[4,16,128]{2,1,0:T(8,128)S(1)} %get-tuple-element.68.after), channel_id=1, source_target_pairs={{0,64},{8,72},{16,80},{24,88},{32,96},{40,104},{48,112},{56,120},{... | collective-permute-start | bytes 98312 | tf_op jit(solution)/shard_map/ppermute | solution.py:341
  83.8 5.7 %collective-permute-done.22.three_off = f32[4,16,128]{2,1,0:T(8,128)S(1)} collective-permute-done((f32[4,16,128]{2,1,0:T(8,128)S(1)}, f32[4,16,128]{2,1,0:T(8,128)S(1)}, u32[]{:S(2)}, u32[]{:S(2)}) %collective-permute-start.22) | collective-permute-done | bytes 32800 | tf_op jit(solution)/shard_map/ppermute | solution.py:341
  89.5 4.6 %shard_map.128 = (bf16[512,512]{1,0:T(8,128)(2,1)}, bf16[512,512]{1,0:T(8,128)(2,1)}) custom-call(s32[3]{0:T(128)S(1)} %pad_add_fusion.spot, f32[4,16,128]{2,1,0:T(8,128)S(1)} %get-tuple-element.40.rates, f32[4,16,128]{2,1,0:T(8,128)S(1)} %get-tuple-element.70.two, f32[4,16,128]{2,1,0:T(8,128)S(1)} %collective-permute-done.22.three_off, ...), custom_call_target="tpu_custom_call" | custom-call | flops 4950000128 | bytes 13500000 | tf_op jit(solution)/shard_map/pallas_call | solution.py:290
  (60 shorter events, 26.6 us)
Async XLA Ops:
  0.6 15.7 %collective-permute-start.6 = (bf16[512,512]{1,0:T(8,128)(2,1)}, bf16[512,512]{1,0:T(8,128)(2,1)S(1)}, u32[]{:S(2)}, u32[]{:S(2)}) collective-permute-start(bf16[512,512]{1,0:T(8,128)(2,1)} %own.1), channel_id=1, source_target_pairs={{0,1},{1,2},{2,3},{3,0},{4,5},{5,6},{6,7},{7,4},{8,11},{9,8},{10,9... | collective-permute-start | bytes 1572872 | tf_op jit(solution)/shard_map/ppermute | solution.py:323
  2.3 15.0 %collective-permute-start.5 = (bf16[512,512]{1,0:T(8,128)(2,1)}, bf16[512,512]{1,0:T(8,128)(2,1)S(1)}, u32[]{:S(2)}, u32[]{:S(2)}) collective-permute-start(bf16[512,512]{1,0:T(8,128)(2,1)} %own.1), channel_id=1, source_target_pairs={{0,4},{1,5},{2,6},{3,7},{4,0},{5,1},{6,2},{7,3},{8,12},{9,13},{10,... | collective-permute-start | bytes 1572872 | tf_op jit(solution)/shard_map/ppermute | solution.py:314
  3.8 13.5 %collective-permute-start.7 = (bf16[512,512]{1,0:T(8,128)(2,1)}, bf16[512,512]{1,0:T(8,128)(2,1)S(1)}, u32[]{:S(2)}, u32[]{:S(2)}) collective-permute-start(bf16[512,512]{1,0:T(8,128)(2,1)} %own.1), channel_id=1, source_target_pairs={{0,3},{1,0},{2,1},{3,2},{4,7},{5,4},{6,5},{7,6},{8,9},{9,10},{10,1... | collective-permute-start | bytes 1572872 | tf_op jit(solution)/shard_map/ppermute | solution.py:323
  10.4 1.3 %collective-permute-start = (f32[4,16,128]{2,1,0:T(8,128)S(1)}, f32[4,16,128]{2,1,0:T(8,128)S(1)}, u32[]{:S(2)}, u32[]{:S(2)}) collective-permute-start(f32[4,16,128]{2,1,0:T(8,128)S(1)} %get-tuple-element.41.own), channel_id=1, source_target_pairs={{0,8},{8,0},{16,24},{24,16},{32,40},{40,32},{48,56},{56,48},{64,72... | collective-permute-start | bytes 98312 | tf_op jit(solution)/shard_map/ppermute | solution.py:332
  12.3 4.0 %collective-permute-start.1 = (f32[4,16,128]{2,1,0:T(8,128)S(1)}, f32[4,16,128]{2,1,0:T(8,128)S(1)}, u32[]{:S(2)}, u32[]{:S(2)}) collective-permute-start(f32[4,16,128]{2,1,0:T(8,128)S(1)} %get-tuple-element.42.pair), channel_id=1, source_target_pairs={{0,32},{8,40},{16,48},{24,56},{32,64},{40,72},{48,80},{56,88},{64,... | collective-permute-start | bytes 98312 | tf_op jit(solution)/shard_map/ppermute | solution.py:341
  17.3 16.1 %collective-permute-start.9 = (bf16[1024,512]{1,0:T(8,128)(2,1)S(1)}, bf16[1024,512]{1,0:T(8,128)(2,1)S(1)}, u32[]{:S(2)}, u32[]{:S(2)}) collective-permute-start(bf16[1024,512]{1,0:T(8,128)(2,1)S(1)} %shard_map.114.after), channel_id=1, source_target_pairs={{0,1},{1,2},{2,3},{3,0},{4,5},{5,6},{6,7},{7,4},{8,11},{9,8},{10,9... | collective-permute-start | bytes 3145736 | tf_op jit(solution)/shard_map/ppermute | solution.py:323
  17.4 15.1 %collective-permute-start.10 = (bf16[512,512]{1,0:T(8,128)(2,1)S(1)}, bf16[512,512]{1,0:T(8,128)(2,1)S(1)}, u32[]{:S(2)}, u32[]{:S(2)}) collective-permute-start(bf16[512,512]{1,0:T(8,128)(2,1)S(1)} %collective-permute-done.7.ahead), channel_id=1, source_target_pairs={{0,4},{1,5},{2,6},{3,7},{4,0},{5,1},{6,2},{7,3},{8,12},{9,13},{10,... | collective-permute-start | bytes 1572872 | tf_op jit(solution)/shard_map/ppermute | solution.py:314
  19.0 6.1 %collective-permute-start.2 = (f32[4,16,128]{2,1,0:T(8,128)S(1)}, f32[4,16,128]{2,1,0:T(8,128)S(1)}, u32[]{:S(2)}, u32[]{:S(2)}) collective-permute-start(f32[4,16,128]{2,1,0:T(8,128)S(1)} %get-tuple-element.42.pair), channel_id=1, source_target_pairs={{0,64},{8,72},{16,80},{24,88},{32,96},{40,104},{48,112},{56,120},{... | collective-permute-start | bytes 98312 | tf_op jit(solution)/shard_map/ppermute | solution.py:341
  25.7 8.3 %collective-permute-start.4 = (f32[4,16,128]{2,1,0:T(8,128)S(1)}, f32[4,16,128]{2,1,0:T(8,128)S(1)}, u32[]{:S(2)}, u32[]{:S(2)}) collective-permute-start(f32[4,16,128]{2,1,0:T(8,128)S(1)} %get-tuple-element.44), channel_id=1, source_target_pairs={{0,192},{8,200},{16,208},{24,216},{32,224},{40,232},{48,240},{56,2... | collective-permute-start | bytes 98312 | tf_op jit(solution)/shard_map/ppermute | solution.py:341
  27.5 7.5 %collective-permute-start.3 = (f32[4,16,128]{2,1,0:T(8,128)S(1)}, f32[4,16,128]{2,1,0:T(8,128)S(1)}, u32[]{:S(2)}, u32[]{:S(2)}) collective-permute-start(f32[4,16,128]{2,1,0:T(8,128)S(1)} %get-tuple-element.44), channel_id=1, source_target_pairs={{0,96},{8,104},{16,112},{24,120},{32,128},{40,136},{48,144},{56,15... | collective-permute-start | bytes 98312 | tf_op jit(solution)/shard_map/ppermute | solution.py:341
  33.5 11.3 %collective-permute-start.11 = (bf16[512,512]{1,0:T(8,128)(2,1)S(1)}, bf16[512,512]{1,0:T(8,128)(2,1)S(1)}, u32[]{:S(2)}, u32[]{:S(2)}) collective-permute-start(bf16[512,512]{1,0:T(8,128)(2,1)S(1)} %shard_map.117.after), channel_id=1, source_target_pairs={{0,1},{1,2},{2,3},{3,0},{4,5},{5,6},{6,7},{7,4},{8,11},{9,8},{10,9... | collective-permute-start | bytes 1572872 | tf_op jit(solution)/shard_map/ppermute | solution.py:323
  35.6 5.7 %collective-permute-start.8 = (f32[4,16,128]{2,1,0:T(8,128)S(1)}, f32[4,16,128]{2,1,0:T(8,128)S(1)}, u32[]{:S(2)}, u32[]{:S(2)}) collective-permute-start(f32[4,16,128]{2,1,0:T(8,128)S(1)} %get-tuple-element.45), channel_id=1, source_target_pairs={{0,16},{8,24},{16,0},{24,8},{32,48},{40,56},{48,32},{56,40},{64,80... | collective-permute-start | bytes 98312 | tf_op jit(solution)/shard_map/ppermute | solution.py:336
  46.3 15.0 %collective-permute-start.14 = (bf16[512,512]{1,0:T(8,128)(2,1)S(1)}, bf16[512,512]{1,0:T(8,128)(2,1)S(1)}, u32[]{:S(2)}, u32[]{:S(2)}) collective-permute-start(bf16[512,512]{1,0:T(8,128)(2,1)S(1)} %get-tuple-element.58), channel_id=1, source_target_pairs={{0,4},{1,5},{2,6},{3,7},{4,0},{5,1},{6,2},{7,3},{8,12},{9,13},{10,... | collective-permute-start | bytes 1572872 | tf_op jit(solution)/shard_map/ppermute | solution.py:314
  47.3 16.0 %collective-permute-start.13 = (bf16[1024,512]{1,0:T(8,128)(2,1)S(1)}, bf16[1024,512]{1,0:T(8,128)(2,1)S(1)}, u32[]{:S(2)}, u32[]{:S(2)}) collective-permute-start(bf16[1024,512]{1,0:T(8,128)(2,1)S(1)} %get-tuple-element.54.after), channel_id=1, source_target_pairs={{0,1},{1,2},{2,3},{3,0},{4,5},{5,6},{6,7},{7,4},{8,11},{9,8},{10,9... | collective-permute-start | bytes 3145736 | tf_op jit(solution)/shard_map/ppermute | solution.py:323
  53.5 1.2 %collective-permute-start.12 = (f32[4,16,128]{2,1,0:T(8,128)S(1)}, f32[4,16,128]{2,1,0:T(8,128)S(1)}, u32[]{:S(2)}, u32[]{:S(2)}) collective-permute-start(f32[4,16,128]{2,1,0:T(8,128)S(1)} %get-tuple-element.55.own), channel_id=1, source_target_pairs={{0,8},{8,0},{16,24},{24,16},{32,40},{40,32},{48,56},{56,48},{64,72... | collective-permute-start | bytes 98312 | tf_op jit(solution)/shard_map/ppermute | solution.py:332
  55.2 5.5 %collective-permute-start.15 = (f32[4,16,128]{2,1,0:T(8,128)S(1)}, f32[4,16,128]{2,1,0:T(8,128)S(1)}, u32[]{:S(2)}, u32[]{:S(2)}) collective-permute-start(f32[4,16,128]{2,1,0:T(8,128)S(1)} %get-tuple-element.56.after.pair), channel_id=1, source_target_pairs={{0,16},{8,24},{16,0},{24,8},{32,48},{40,56},{48,32},{56,40},{64,80... | collective-permute-start | bytes 98312 | tf_op jit(solution)/shard_map/ppermute | solution.py:336
  63.7 10.9 %collective-permute-start.18 = (bf16[512,512]{1,0:T(8,128)(2,1)S(1)}, bf16[512,512]{1,0:T(8,128)(2,1)S(1)}, u32[]{:S(2)}, u32[]{:S(2)}) collective-permute-start(bf16[512,512]{1,0:T(8,128)(2,1)S(1)} %get-tuple-element.67), channel_id=1, source_target_pairs={{0,1},{1,2},{2,3},{3,0},{4,5},{5,6},{6,7},{7,4},{8,11},{9,8},{10,9... | collective-permute-start | bytes 1572872 | tf_op jit(solution)/shard_map/ppermute | solution.py:323
  64.4 6.3 %collective-permute-start.20 = (f32[4,16,128]{2,1,0:T(8,128)S(1)}, f32[4,16,128]{2,1,0:T(8,128)S(1)}, u32[]{:S(2)}, u32[]{:S(2)}) collective-permute-start(f32[4,16,128]{2,1,0:T(8,128)S(1)} %get-tuple-element.63.after.pair), channel_id=1, source_target_pairs={{0,192},{8,200},{16,208},{24,216},{32,224},{40,232},{48,240},{56,2... | collective-permute-start | bytes 98312 | tf_op jit(solution)/shard_map/ppermute | solution.py:341
  66.5 4.3 %collective-permute-start.19 = (f32[4,16,128]{2,1,0:T(8,128)S(1)}, f32[4,16,128]{2,1,0:T(8,128)S(1)}, u32[]{:S(2)}, u32[]{:S(2)}) collective-permute-start(f32[4,16,128]{2,1,0:T(8,128)S(1)} %get-tuple-element.63.after.pair), channel_id=1, source_target_pairs={{0,224},{8,232},{16,240},{24,248},{32,0},{40,8},{48,16},{56,24},{6... | collective-permute-start | bytes 98312 | tf_op jit(solution)/shard_map/ppermute | solution.py:341
  71.3 22.7 %collective-permute-start.16 = (bf16[512,512]{1,0:T(8,128)(2,1)S(1)}, bf16[512,512]{1,0:T(8,128)(2,1)S(1)}, u32[]{:S(2)}, u32[]{:S(2)}) collective-permute-start(bf16[512,512]{1,0:T(8,128)(2,1)S(1)} %get-tuple-element.64), channel_id=1, source_target_pairs={{0,1},{1,2},{2,3},{3,0},{4,5},{5,6},{6,7},{7,4},{8,11},{9,8},{10,9... | collective-permute-start | bytes 1572872 | tf_op jit(solution)/shard_map/ppermute | solution.py:323
  72.3 21.7 %collective-permute-start.17 = (bf16[512,512]{1,0:T(8,128)(2,1)S(1)}, bf16[512,512]{1,0:T(8,128)(2,1)S(1)}, u32[]{:S(2)}, u32[]{:S(2)}) collective-permute-start(bf16[512,512]{1,0:T(8,128)(2,1)S(1)} %get-tuple-element.65), channel_id=1, source_target_pairs={{0,3},{1,0},{2,1},{3,2},{4,7},{5,4},{6,5},{7,6},{8,9},{9,10},{10,1... | collective-permute-start | bytes 1572872 | tf_op jit(solution)/shard_map/ppermute | solution.py:323
  74.8 19.3 %collective-permute-start.21 = (bf16[512,512]{1,0:T(8,128)(2,1)S(1)}, bf16[512,512]{1,0:T(8,128)(2,1)S(1)}, u32[]{:S(2)}, u32[]{:S(2)}) collective-permute-start(bf16[512,512]{1,0:T(8,128)(2,1)S(1)} %shard_map.126), channel_id=1, source_target_pairs={{0,4},{1,5},{2,6},{3,7},{4,0},{5,1},{6,2},{7,3},{8,12},{9,13},{10,... | collective-permute-start | bytes 1572872 | tf_op jit(solution)/shard_map/ppermute | solution.py:314
  76.6 7.1 %collective-permute-start.23 = (f32[4,16,128]{2,1,0:T(8,128)S(1)}, f32[4,16,128]{2,1,0:T(8,128)S(1)}, u32[]{:S(2)}, u32[]{:S(2)}) collective-permute-start(f32[4,16,128]{2,1,0:T(8,128)S(1)} %get-tuple-element.68.after), channel_id=1, source_target_pairs={{0,64},{8,72},{16,80},{24,88},{32,96},{40,104},{48,112},{56,120},{... | collective-permute-start | bytes 98312 | tf_op jit(solution)/shard_map/ppermute | solution.py:341
  82.2 7.3 %collective-permute-start.22 = (f32[4,16,128]{2,1,0:T(8,128)S(1)}, f32[4,16,128]{2,1,0:T(8,128)S(1)}, u32[]{:S(2)}, u32[]{:S(2)}) collective-permute-start(f32[4,16,128]{2,1,0:T(8,128)S(1)} %get-tuple-element.68.after), channel_id=1, source_target_pairs={{0,160},{8,168},{16,176},{24,184},{32,192},{40,200},{48,208},{56,2... | collective-permute-start | bytes 98312 | tf_op jit(solution)/shard_map/ppermute | solution.py:341
  (7 other events, 106.5 us)

commit v3 on v2

--- a/solution.py
+++ b/solution.py
@@ -15,7 +15,6 @@
 STEP = ROWS // PARTS
 APART = STEP + 8
 VMEM = pl.BlockSpec(memory_space=pltpu.VMEM)
-SMEM = pl.BlockSpec(memory_space=pltpu.SMEM)
 
 
 def tile_of(tile):
@@ -102,10 +101,6 @@
     return value.astype(F32)
 
 
-def columns(weight, place, which):
-    return weight[:, pl.ds(pl.multiple_of(place[which] * COLS, COLS), COLS)]
-
-
 NEAR = [(0, 0), (1, 0), (0, -1), (0, 1), (1, -1), (1, 1), (0, 2), (1, 2)]
 OWN, ACROSS, BEHIND, AHEAD, ACROSS_BEHIND, ACROSS_AHEAD, FAR, ACROSS_FAR = range(8)
 TOP, BOTTOM = slice(0, HALF), slice(HALF, ROWS)
@@ -113,12 +108,20 @@
 PER_TILE = range(TILES)
 
 
+def columns(weight, which):
+    at, step = lax.axis_index("tp"), 1 - 2 * lax.rem(lax.axis_index("ctx"), 2)
+    dx, dy = NEAR[which]
+    x = lax.rem(lax.div(at, 4) + dx, 2)
+    y = lax.rem(lax.rem(at, 4) + step * dy + 4, 4)
+    return weight[:, pl.ds(pl.multiple_of((x * 4 + y) * COLS, COLS), COLS)]
+
+
 def gate_kernel(
-    spot, place, gated, decay_rates, amplitude, rates, keep, keep_piece, gain, starts, total, signal, ends,
+    gated, fading, amplitude, rates, keep, keep_piece, gain, starts, total, signal, ends,
 ):
     for tile in PER_TILE:
         at = tile_of(tile)
-        rates[tile] = decay_rates[:, at]
+        rates[tile] = -fading[:, at]
         gain[tile] = amplitude[:, at]
         keep[tile] = jnp.exp(-rates[tile])
         keep_piece[tile] = jnp.exp(rates[tile] * -float(STEP))
@@ -131,19 +134,20 @@
     return jnp.exp(rates * (-float(ROWS) * jnp.asarray(n).astype(F32)))
 
 
-def spot_of(spot, flipped):
-    core, high, z = spot[0], spot[1], spot[2]
+def spot_of(flipped):
+    line = lax.axis_index("ctx")
+    core, high, z = lax.rem(line, 2), lax.rem(lax.div(line, 2), 2), lax.div(line, 4)
     return (1 - core, 1 - high, 7 - z) if flipped else (core, high, z)
 
 
-def pair_kernel(flipped, spot, rates, own, other, pair, before):
-    core, _, _ = spot_of(spot, flipped)
+def pair_kernel(flipped, rates, own, other, pair, before):
+    core, _, _ = spot_of(flipped)
     pair[...] = power(rates[...], 1 - core) * own[...] + power(rates[...], core) * other[...]
     before[...] = core.astype(F32) * other[...]
 
 
-def three_kernel(flipped, spot, rates, pair, one_off, two_off, two, three):
-    _, _, z = spot_of(spot, flipped)
+def three_kernel(flipped, rates, pair, one_off, two_off, two, three):
+    _, _, z = spot_of(flipped)
     here = (z >= 1).astype(F32) * one_off[...]
     here += (z >= 2).astype(F32) * (power(rates[...], 4) * two_off[...])
     two[...] = here
@@ -155,32 +159,28 @@
     return here + (z >= 6).astype(F32) * (power(rates, 20) * six_off)
 
 
-def sent_kernel(flipped, spot, rates, pair, two, three_off, six_off, after, over, sent):
-    _, high, z = spot_of(spot, flipped)
+def sent_kernel(flipped, rates, pair, two, three_off, six_off, after, after_too, over, sent):
+    _, high, z = spot_of(flipped)
     here = over_of(rates[...], z, two[...], three_off[...], six_off[...])
     over[...] = here
     later = high.astype(F32)
     sent[...] = later * here + (1.0 - later) * (pair[...] + power(rates[...], 4) * here)
 
 
-def group_kernel(flipped, spot, rates, pair, before, other, group, before_all):
-    core, high, _ = spot_of(spot, flipped)
+def group_kernel(flipped, rates, pair, before, other, group, before_all):
+    core, high, _ = spot_of(flipped)
     early, late = power(rates[...], 2 - 2 * high), power(rates[...], 2 * high)
     group[...] = early * pair[...] + late * other[...]
     before_all[...] = before[...] + high.astype(F32) * (power(rates[...], core) * other[...])
 
 
-def pack_kernel(across, behind, ahead, after, out):
-    out[FIRST, :] = across[...]
-    out[SECOND, :] = behind[...]
-
-
-def halve_kernel(got, after, out):
-    out[...] = got[FIRST, :]
+def relay_kernel(across, behind, ahead, after, after_too, across_out, behind_out):
+    across_out[...] = across[...]
+    behind_out[...] = behind[...]
 
 
 def mix_kernel(
-    spot, rates, other, over, before,
+    rates, other, over, before,
     gated, starts, keep, keep_piece, gain, skip, query, after,
     summed, mixed_in,
     signal, result, begin,
@@ -188,7 +188,7 @@
     for tile in PER_TILE:
         at = tile_of(tile)
         lay(signal, tile, wide(gated[:, at]))
-        core, _, _ = spot_of(spot, False)
+        core, _, _ = spot_of(False)
         initial = other[tile] + power(rates[tile], 2) * over[tile]
         initial = power(rates[tile], core) * initial + before[tile]
         whole_starts(starts, initial, begin, keep_piece, tile, False)
@@ -199,26 +199,28 @@
         mixed_in[:, at] = (wide(query[:, at]) * total).astype(BF16)
 
 
-def products(mixed_in, weight, place, outs):
+def products(mixed_in, weight, outs):
     for out, start, which in outs:
         for rows in (TOP, BOTTOM):
-            part = dot(mixed_in[rows, :], columns(weight, place, which))
+            part = dot(mixed_in[rows, :], columns(weight, which))
             out[start + rows.start : start + rows.stop, :] = part.astype(BF16)
 
 
-def first_kernel(place, mixed_in, weight, after, along, over):
-    outs = ((along, 0, ACROSS_FAR), (along, ROWS, FAR), (over, 0, ACROSS_BEHIND))
-    products(mixed_in, weight, place, outs)
-
-
-def rest_kernel(place, mixed_in, weight, after, side, ahead, behind, across, own):
-    outs = ((side, 0, ACROSS_AHEAD), (ahead, 0, AHEAD), (behind, 0, BEHIND))
-    products(mixed_in, weight, place, outs + ((across, 0, ACROSS), (own, 0, OWN)))
-
-
-def second_kernel(along, over, side, ahead, behind, after, side_out, ahead_out, behind_out):
-    side_out[...] = (wide(side[...]) + wide(along[FIRST, :])).astype(BF16)
-    ahead_out[...] = (wide(ahead[...]) + wide(along[SECOND, :])).astype(BF16)
+def first_kernel(mixed_in, weight, across_far, far):
+    products(mixed_in, weight, ((across_far, 0, ACROSS_FAR), (far, 0, FAR)))
+
+
+def rest_kernel(mixed_in, weight, after, over, side, ahead, behind, across, own):
+    outs = ((over, 0, ACROSS_BEHIND), (side, 0, ACROSS_AHEAD), (ahead, 0, AHEAD))
+    products(mixed_in, weight, outs + ((behind, 0, BEHIND), (across, 0, ACROSS), (own, 0, OWN)))
+
+
+def side_kernel(got, side, after, out):
+    out[...] = (wide(side[...]) + wide(got[...])).astype(BF16)
+
+
+def second_kernel(along, over, ahead, behind, after, ahead_out, behind_out):
+    ahead_out[...] = (wide(ahead[...]) + wide(along[...])).astype(BF16)
     behind_out[...] = (wide(behind[...]) + wide(over[...])).astype(BF16)
 
 
@@ -231,26 +233,31 @@
     out[...] = (inner + (wide(behind[...]) + wide(across[...]))).astype(BF16)
 
 
-def early_kernel(place, weight, own, across, behind, ahead, after, acc):
+def early_kernel(weight, own, across, behind, ahead, after, acc):
     blocks = ((own, OWN), (across, ACROSS), (behind, BEHIND), (ahead, AHEAD))
     for rows in (TOP, BOTTOM):
         grad = jnp.zeros((HALF, COLS), F32)
         for ref, which in blocks:
-            grad += turned(ref[rows, :], columns(weight, place, which))
+            grad += turned(ref[rows, :], columns(weight, which))
         acc[rows, :] = grad
 
 
+def later_kernel(weight, acc, got_across, got_behind, over, total):
+    parts = ((got_across, ACROSS_BEHIND), (got_behind, FAR), (over, ACROSS_AHEAD))
+    for rows in (TOP, BOTTOM):
+        grad = acc[rows, :]
+        for ref, which in parts:
+            grad += turned(ref[rows, :], columns(weight, which))
+        total[rows, :] = grad
+
+
 def grad_kernel(
-    place, weight, acc, got, over, far, query, summed, keep, keep_piece, after,
+    weight, acc, far, query, summed, keep, keep_piece, after,
     grad_query, grad_conv, starts, total,
     full, signal, ends,
 ):
-    parts = ((got, 0, ACROSS_BEHIND), (got, ROWS, FAR), (over, 0, ACROSS_AHEAD), (far, 0, ACROSS_FAR))
     for rows in (TOP, BOTTOM):
-        grad = acc[rows, :]
-        for ref, start, which in parts:
-            block = ref[start + rows.start : start + rows.stop, :]
-            grad += turned(block, columns(weight, place, which))
+        grad = acc[rows, :] + turned(far[rows, :], columns(weight, ACROSS_FAR))
         full[rows, :] = grad
     for tile in PER_TILE:
         at = tile_of(tile)
@@ -263,7 +270,7 @@
 
 
 def back_kernel(
-    spot, rates, two, three_off, six_off, before,
+    rates, two, three_off, six_off, before,
     grad_conv, starts, keep, keep_piece, gain, skip, key, value,
     grad_key, grad_value,
     signal, result, begin,
@@ -271,7 +278,7 @@
     for tile in PER_TILE:
         at = tile_of(tile)
         lay(signal, tile, wide(grad_conv[:, at]))
-        core, high, z = spot_of(spot, True)
+        core, high, z = spot_of(True)
         over = over_of(rates[tile], z, two[tile], three_off[tile], six_off[tile])
         initial = power(rates[tile], 2 * high + core) * over + before[tile]
         whole_starts(starts, initial, begin, keep_piece, tile, True)
@@ -290,7 +297,7 @@
     return pl.pallas_call(
         kernel,
         out_shape=[jax.ShapeDtypeStruct(shape, kind) for shape, kind in outs],
-        in_specs=[SMEM if arg.dtype == jnp.int32 else VMEM for arg in args],
+        in_specs=[VMEM] * len(args),
         out_specs=[VMEM] * len(outs),
         scratch_shapes=[pltpu.VMEM(shape, kind) for shape, kind in scratch],
         cost_estimate=pl.CostEstimate(
@@ -342,14 +349,9 @@
 
 
 def per_device(query, key, value, cotangent, weight, decay_rates, residues, skip_gain):
-    at, line = lax.axis_index("tp"), lax.axis_index("ctx")
-    x, y = at // 4, at % 4
-    step = 1 - 2 * (line % 2)
-    place = [(x + dx) % 2 * 4 + (y + step * dy + 4) % 4 for dx, dy in NEAR]
-    place = jnp.stack(place).astype(jnp.int32)
-    spot = jnp.stack([line % 2, line // 2 % 2, line // 4]).astype(jnp.int32)
     decay_rates, residues = decay_rates.T, residues.T
     amplitude = residues * jnp.sqrt(-jnp.expm1(-2.0 * decay_rates))
+    fading = -decay_rates
     skip = skip_gain.reshape(1, COLS)
 
     across = shift_x(cotangent)
@@ -359,32 +361,35 @@
     deep, table, state = (DEEP, F32), (TABLE, F32), (STATE_SHAPE, F32)
     gated = (key.astype(F32) * value.astype(F32)).astype(BF16)
     rates, keep, keep_piece, gain, starts, total = call(
-        gate_kernel, [state] * 4 + [table, state], [deep, table], 2.4, 6, spot, place, gated, decay_rates, amplitude
-    )
-    pair, before = small(pair_kernel, False, spot, rates, total, other_core(total))
+        gate_kernel, [state] * 4 + [table, state], [deep, table], 2.4, 6, gated, fading, amplitude
+    )
+    pair, before = small(pair_kernel, False, rates, total, other_core(total))
     offs = earlier(pair, 1, False), earlier(pair, 2, False)
-    (packed,) = call(pack_kernel, [(TWICE, BF16)], [], 1.0, 4, across, behind, ahead, offs[0])
-    got, over = along_y(packed, 1), shift_x(ahead)
-    (s_far,) = call(halve_kernel, [(BLOCK, BF16)], [], 1.0, 4, got, over)
-    far = along_y(s_far, 1)
+    s_across, s_behind = call(
+        relay_kernel, [(BLOCK, BF16)] * 2, [], 1.0, 4, across, behind, ahead, *offs
+    )
+    got_across, got_behind, over = along_y(s_across, 1), along_y(s_behind, 1), shift_x(ahead)
+    far = along_y(got_across, 1)
     (acc,) = call(
         early_kernel,
         [(BLOCK, F32)],
         [],
         2.0,
         6,
-        place,
         weight,
         cotangent,
         across,
         behind,
         ahead,
-        packed,
-    )
-
-    two, three = small(three_kernel, False, spot, rates, pair, *offs)
+        s_across,
+    )
+
+    two, three = small(three_kernel, False, rates, pair, *offs)
     offs = earlier(three, 3, False), earlier(three, 6, False)
-    over_state, sent = small(sent_kernel, False, spot, rates, pair, two, *offs, acc)
+    over_state, sent = small(sent_kernel, False, rates, pair, two, *offs, acc, got_across)
+    (acc,) = call(
+        later_kernel, [(BLOCK, F32)], [], 1.5, 6, weight, acc, got_across, got_behind, over
+    )
     carried = other_half(sent), over_state, before
     summed, mixed_in = call(
         mix_kernel,
@@ -392,7 +397,6 @@
         [deep, deep, table],
         4.5,
         8,
-        spot,
         rates,
         *carried,
         gated,
@@ -402,31 +406,20 @@
         gain,
         skip,
         query,
-        s_far,
-    )
-    s_along, s_over = call(
-        first_kernel,
-        [(TWICE, BF16), (BLOCK, BF16)],
-        [],
-        1.5,
-        6,
-        place,
-        mixed_in,
-        weight,
-        far,
-    )
-    g_along, g_over = along_y(s_along, 1), shift_x(s_over)
+        got_across,
+    )
+    s_across_far, s_along = call(
+        first_kernel, [(BLOCK, BF16)] * 2, [], 1.0, 6, mixed_in, weight
+    )
+    g_across_far, g_along = along_y(s_across_far, 1), along_y(s_along, 1)
     grad_query, grad_conv, back_starts, back_total = call(
         grad_kernel,
         [(BLOCK, BF16), (BLOCK, BF16), table, state],
         [(BLOCK, F32), deep, table],
         6.0,
         8,
-        place,
         weight,
         acc,
-        got,
-        over,
         far,
         query,
         summed,
@@ -434,28 +427,29 @@
         keep_piece,
         s_along,
     )
-    pair, before = small(pair_kernel, True, spot, rates, back_total, other_core(back_total))
+    pair, before = small(pair_kernel, True, rates, back_total, other_core(back_total))
     half_other = other_half(pair)
-    side, ahead_part, behind_part, across_part, own_part = call(
-        rest_kernel, [(BLOCK, BF16)] * 5, [], 2.0, 6, place, mixed_in, weight, pair
-    )
-    group, before = small(group_kernel, True, spot, rates, pair, before, half_other)
+    s_over, side, ahead_part, behind_part, across_part, own_part = call(
+        rest_kernel, [(BLOCK, BF16)] * 6, [], 2.0, 6, mixed_in, weight, pair
+    )
+    group, before = small(group_kernel, True, rates, pair, before, half_other)
     offs = earlier(group, 1, True), earlier(group, 2, True)
-    two, three = small(three_kernel, True, spot, rates, group, *offs)
+    two, three = small(three_kernel, True, rates, group, *offs)
     offs = earlier(three, 3, True), earlier(three, 6, True)
 
-    s_side, s_ahead, s_behind = call(
+    g_over = shift_x(s_over)
+    (s_side,) = call(side_kernel, [(BLOCK, BF16)], [], 0.5, 4, g_across_far, side, group)
+    s_ahead, s_behind = call(
         second_kernel,
-        [(BLOCK, BF16)] * 3,
+        [(BLOCK, BF16)] * 2,
         [],
-        3.0,
+        1.0,
         4,
         g_along,
         g_over,
-        side,
         ahead_part,
         behind_part,
-        group,
+        three,
     )
     g_side, g_ahead, g_behind = along_y(s_side, 1), along_y(s_ahead, 1), along_y(s_behind, -1)
     (s_across,) = call(third_kernel, [(BLOCK, BF16)], [], 0.5, 4, across_part, g_side, three)
@@ -468,7 +462,6 @@
         [deep, deep, table],
         4.5,
         8,
-        spot,
         rates,
         two,
         *offs,

time: 95.4 us -> 84.5 us (0.89)
  the two profiles are of different devices: /device:TPU:64 before, /device:TPU:2 now
where the time goes in v3:
time: 84.5 us; the launch traced here: 83.2 us
  starting transfers between devices  35.3 us (42%)
  waiting for transfers between devices  26.9 us (32%)
  Pallas kernels  17.9 us (21%)
  other arithmetic  2.14 us (3%)
    pallas_call x19, Pallas kernels, call(): pl.pallas_call(kernel, out_shape=[jax.ShapeDtypeStruct(shape, kind) for s...  17.9 us
    ppermute x8, waiting for transfers between devices, earlier(): lax.ppermute(value, 'ctx', ctx_perm(lambda z, h, c: (z + move, h, c)))  16.3 us
    ppermute x10, starting transfers between devices, along_y(): return lax.ppermute(value, ('ctx', 'tp'), pairs)  13.9 us
    ppermute x8, starting transfers between devices, earlier(): lax.ppermute(value, 'ctx', ctx_perm(lambda z, h, c: (z + move, h, c)))  12.7 us
    ppermute x4, starting transfers between devices, shift_x(): return lax.ppermute(value, 'tp', [(at, (at + 4) % 8) for at in range(8)])  4.92 us
    ppermute x4, waiting for transfers between devices, shift_x(): return lax.ppermute(value, 'tp', [(at, (at + 4) % 8) for at in range(8)])  4.49 us
    ppermute x2, starting transfers between devices, other_half(): return lax.ppermute(value, 'ctx', ctx_perm(lambda z, h, c: (z, h + 1, c)))  3.71 us
    ppermute x2, waiting for transfers between devices, other_core(): return lax.ppermute(value, 'ctx', ctx_perm(lambda z, h, c: (z, h, c + 1)))  2.23 us
  transfers between devices with their start and end apart: 26, of which 13 were waited for; matrix products, arithmetic and copies ran while one was open for 3% of the time, Pallas kernels for 20%

profile of v3, /device:TPU:2, one launch (start us, length us, event | category | flops | bytes accessed | tf_op | source)
XLA Modules:
  0.0 83.2 jit_solution(15261993806083003494)
XLA Ops:
  0.6 1.7 %collective-permute-start.6 = (bf16[512,512]{1,0:T(8,128)(2,1)}, bf16[512,512]{1,0:T(8,128)(2,1)S(1)}, u32[]{:S(2)}, u32[]{:S(2)}) collective-permute-start(bf16[512,512]{1,0:T(8,128)(2,1)} %own.1), channel_id=1, source_target_pairs={{0,1},{1,2},{2,3},{3,0},{4,5},{5,6},{6,7},{7,4},{8,11},{9,8},{10,9... | collective-permute-start | bytes 1572872 | tf_op jit(solution)/shard_map/ppermute | solution.py:330
  3.1 3.1 %collective-permute-start.7 = (bf16[512,512]{1,0:T(8,128)(2,1)}, bf16[512,512]{1,0:T(8,128)(2,1)S(1)}, u32[]{:S(2)}, u32[]{:S(2)}) collective-permute-start(bf16[512,512]{1,0:T(8,128)(2,1)} %own.1), channel_id=1, source_target_pairs={{0,3},{1,0},{2,1},{3,2},{4,7},{5,4},{6,5},{7,6},{8,9},{9,10},{10,1... | collective-permute-start | bytes 1572872 | tf_op jit(solution)/shard_map/ppermute | solution.py:330
  8.4 1.4 %shard_map.111 = (f32[4,16,128]{2,1,0:T(8,128)S(1)}, f32[4,16,128]{2,1,0:T(8,128)S(1)}, f32[4,16,128]{2,1,0:T(8,128)S(1)}, f32[4,16,128]{2,1,0:T(8,128)S(1)}, f3...) custom-call(bf16[512,512]{1,0:T(8,128)(2,1)S(1)} %multiply_convert_fusion.gated, ...), custom_call_target="tpu_custom_call" | custom-call | flops 2640000000 | bytes 7200000 | tf_op jit(solution)/shard_map/pallas_call | solution.py:297
  11.1 1.6 %collective-permute-start.2 = (f32[4,16,128]{2,1,0:T(8,128)S(1)}, f32[4,16,128]{2,1,0:T(8,128)S(1)}, u32[]{:S(2)}, u32[]{:S(2)}) collective-permute-start(f32[4,16,128]{2,1,0:T(8,128)S(1)} %get-tuple-element.44.pair), channel_id=1, source_target_pairs={{0,64},{8,72},{16,80},{24,88},{32,96},{40,104},{48,112},{56,120},{... | collective-permute-start | bytes 98312 | tf_op jit(solution)/shard_map/ppermute | solution.py:348
  12.7 1.9 %collective-permute-start.1 = (f32[4,16,128]{2,1,0:T(8,128)S(1)}, f32[4,16,128]{2,1,0:T(8,128)S(1)}, u32[]{:S(2)}, u32[]{:S(2)}) collective-permute-start(f32[4,16,128]{2,1,0:T(8,128)S(1)} %get-tuple-element.44.pair), channel_id=1, source_target_pairs={{0,32},{8,40},{16,48},{24,56},{32,64},{40,72},{48,80},{56,88},{64,... | collective-permute-start | bytes 98312 | tf_op jit(solution)/shard_map/ppermute | solution.py:348
  14.6 3.1 %collective-permute-done.2.two_off.after_too = f32[4,16,128]{2,1,0:T(8,128)S(1)} collective-permute-done((f32[4,16,128]{2,1,0:T(8,128)S(1)}, f32[4,16,128]{2,1,0:T(8,128)S(1)}, u32[]{:S(2)}, u32[]{:S(2)}) %collective-permute-start.2) | collective-permute-done | bytes 32800 | tf_op jit(solution)/shard_map/ppermute | solution.py:348
  18.9 1.5 %collective-permute-start.11 = (bf16[512,512]{1,0:T(8,128)(2,1)S(1)}, bf16[512,512]{1,0:T(8,128)(2,1)S(1)}, u32[]{:S(2)}, u32[]{:S(2)}) collective-permute-start(bf16[512,512]{1,0:T(8,128)(2,1)S(1)} %collective-permute-done.7.ahead), channel_id=1, source_target_pairs={{0,4},{1,5},{2,6},{3,7},{4,0},{5,1},{6,2},{7,3},{8,12},{9,13},{10,... | collective-permute-start | bytes 1572872 | tf_op jit(solution)/shard_map/ppermute | solution.py:321
  20.4 1.6 %collective-permute-start.10 = (bf16[512,512]{1,0:T(8,128)(2,1)S(1)}, bf16[512,512]{1,0:T(8,128)(2,1)S(1)}, u32[]{:S(2)}, u32[]{:S(2)}) collective-permute-start(bf16[512,512]{1,0:T(8,128)(2,1)S(1)} %get-tuple-element.56), channel_id=1, source_target_pairs={{0,1},{1,2},{2,3},{3,0},{4,5},{5,6},{6,7},{7,4},{8,11},{9,8},{10,9... | collective-permute-start | bytes 1572872 | tf_op jit(solution)/shard_map/ppermute | solution.py:330
  22.0 3.7 %collective-permute-start.4 = (f32[4,16,128]{2,1,0:T(8,128)S(1)}, f32[4,16,128]{2,1,0:T(8,128)S(1)}, u32[]{:S(2)}, u32[]{:S(2)}) collective-permute-start(f32[4,16,128]{2,1,0:T(8,128)S(1)} %get-tuple-element.46), channel_id=1, source_target_pairs={{0,192},{8,200},{16,208},{24,216},{32,224},{40,232},{48,240},{56,2... | collective-permute-start | bytes 98312 | tf_op jit(solution)/shard_map/ppermute | solution.py:348
  27.3 5.7 %collective-permute-done.3.three_off = f32[4,16,128]{2,1,0:T(8,128)S(1)} collective-permute-done((f32[4,16,128]{2,1,0:T(8,128)S(1)}, f32[4,16,128]{2,1,0:T(8,128)S(1)}, u32[]{:S(2)}, u32[]{:S(2)}) %collective-permute-start.3) | collective-permute-done | bytes 32800 | tf_op jit(solution)/shard_map/ppermute | solution.py:348
  33.0 2.4 %collective-permute-start.9 = (f32[4,16,128]{2,1,0:T(8,128)S(1)}, f32[4,16,128]{2,1,0:T(8,128)S(1)}, u32[]{:S(2)}, u32[]{:S(2)}) collective-permute-start(f32[4,16,128]{2,1,0:T(8,128)S(1)} %get-tuple-element.48), channel_id=1, source_target_pairs={{0,16},{8,24},{16,0},{24,8},{32,48},{40,56},{48,32},{56,40},{64,80... | collective-permute-start | bytes 98312 | tf_op jit(solution)/shard_map/ppermute | solution.py:343
  35.5 1.4 %collective-permute-start.12 = (bf16[512,512]{1,0:T(8,128)(2,1)S(1)}, bf16[512,512]{1,0:T(8,128)(2,1)S(1)}, u32[]{:S(2)}, u32[]{:S(2)}) collective-permute-start(bf16[512,512]{1,0:T(8,128)(2,1)S(1)} %collective-permute-done.8.after_too.after.got_across), channel_id=1, source_target_pairs={{0,1},{1,2},{2,3},{3,0},{4,5},{5,6},{6,7},{7,4},{8,11},{9,8},{10,9... | collective-permute-start | bytes 1572872 | tf_op jit(solution)/shard_map/ppermute | solution.py:330
  38.5 2.9 %shard_map.117 = (f32[512,512]{1,0:T(8,128)S(1)}, bf16[512,512]{1,0:T(8,128)(2,1)S(1)}) custom-call(f32[4,16,128]{2,1,0:T(8,128)S(1)} %get-tuple-element.42.rates, f32[4,16,128]{2,1,0:T(8,128)S(1)} %collective-permute-done.9.other, f32[4,16,128]{2,1,0:T(8,128)S(1)} %get-tuple-element.49.over, f32[4,16,128]{2,1,0:T(8,128)S(1)} %get-tuple-element.50.before, ...), custom_call_target="tpu_custom_call" | custom-call | flops 4950000128 | bytes 13500000 | tf_op jit(solution)/shard_map/pallas_call | solution.py:297
  42.2 1.5 %collective-permute-start.21 = (bf16[512,512]{1,0:T(8,128)(2,1)S(1)}, bf16[512,512]{1,0:T(8,128)(2,1)S(1)}, u32[]{:S(2)}, u32[]{:S(2)}) collective-permute-start(bf16[512,512]{1,0:T(8,128)(2,1)S(1)} %get-tuple-element.71), channel_id=1, source_target_pairs={{0,1},{1,2},{2,3},{3,0},{4,5},{5,6},{6,7},{7,4},{8,11},{9,8},{10,9... | collective-permute-start | bytes 1572872 | tf_op jit(solution)/shard_map/ppermute | solution.py:330
  43.8 2.1 %collective-permute-done.12.far = bf16[512,512]{1,0:T(8,128)(2,1)S(1)} collective-permute-done((bf16[512,512]{1,0:T(8,128)(2,1)S(1)}, bf16[512,512]{1,0:T(8,128)(2,1)S(1)}, u32[]{:S(2)}, u32[]{:S(2)}) %collective-permute-start.12) | collective-permute-done | bytes 524320 | tf_op jit(solution)/shard_map/ppermute | solution.py:330
  45.9 3.0 %shard_map.120 = (bf16[512,512]{1,0:T(8,128)(2,1)}, bf16[512,512]{1,0:T(8,128)(2,1)S(1)}, f32[4,128,128]{2,1,0:T(8,128)S(1)}, f32[4,16,128]{2,1,0:T(8,128)S(1)}) custom-call(bf16[512,4096]{1,0:T(8,128)(2,1)S(1)} %copy-done, f32[512,512]{1,0:T(8,128)S(1)} %shard_map.118.acc, bf16[512,512]{1,0:T(8,128)(2,1)S(1)} %collective-permute-done.12.far, ...), custom_call_target="tpu_custom_call" | custom-call | flops 6600000000 | bytes 18000000 | tf_op jit(solution)/shard_map/pallas_call | solution.py:297
  51.3 1.8 %shard_map.122 = (bf16[512,512]{1,0:T(8,128)(2,1)S(1)}, bf16[512,512]{1,0:T(8,128)(2,1)S(1)}, bf16[512,512]{1,0:T(8,128)(2,1)S(1)}, bf16[512,512]{1,0:T(8,128)(2...) custom-call(bf16[512,512]{1,0:T(8,128)(2,1)S(1)} %get-tuple-element.55.mixed_in, ...), custom_call_target="tpu_custom_call" | custom-call | flops 2200000000 | bytes 6000000 | tf_op jit(solution)/shard_map/pallas_call | solution.py:297
  56.5 2.0 %collective-permute-start.18 = (f32[4,16,128]{2,1,0:T(8,128)S(1)}, f32[4,16,128]{2,1,0:T(8,128)S(1)}, u32[]{:S(2)}, u32[]{:S(2)}) collective-permute-start(f32[4,16,128]{2,1,0:T(8,128)S(1)} %get-tuple-element.66.pair.after), channel_id=1, source_target_pairs={{0,192},{8,200},{16,208},{24,216},{32,224},{40,232},{48,240},{56,2... | collective-permute-start | bytes 98312 | tf_op jit(solution)/shard_map/ppermute | solution.py:348
  58.5 2.8 %collective-permute-done.18.two_off = f32[4,16,128]{2,1,0:T(8,128)S(1)} collective-permute-done((f32[4,16,128]{2,1,0:T(8,128)S(1)}, f32[4,16,128]{2,1,0:T(8,128)S(1)}, u32[]{:S(2)}, u32[]{:S(2)}) %collective-permute-start.18) | collective-permute-done | bytes 32800 | tf_op jit(solution)/shard_map/ppermute | solution.py:348
  62.5 4.5 %collective-permute-done.15.over = bf16[512,512]{1,0:T(8,128)(2,1)S(1)} collective-permute-done((bf16[512,512]{1,0:T(8,128)(2,1)S(1)}, bf16[512,512]{1,0:T(8,128)(2,1)S(1)}, u32[]{:S(2)}, u32[]{:S(2)}) %collective-permute-start.15) | collective-permute-done | bytes 524320 | tf_op jit(solution)/shard_map/ppermute | solution.py:321
  68.2 2.3 %collective-permute-start.20 = (bf16[512,512]{1,0:T(8,128)(2,1)S(1)}, bf16[512,512]{1,0:T(8,128)(2,1)S(1)}, u32[]{:S(2)}, u32[]{:S(2)}) collective-permute-start(bf16[512,512]{1,0:T(8,128)(2,1)S(1)} %get-tuple-element.69), channel_id=1, source_target_pairs={{0,3},{1,0},{2,1},{3,2},{4,7},{5,4},{6,5},{7,6},{8,9},{9,10},{10,1... | collective-permute-start | bytes 1572872 | tf_op jit(solution)/shard_map/ppermute | solution.py:330
  71.9 3.4 %collective-permute-start.24 = (f32[4,16,128]{2,1,0:T(8,128)S(1)}, f32[4,16,128]{2,1,0:T(8,128)S(1)}, u32[]{:S(2)}, u32[]{:S(2)}) collective-permute-start(f32[4,16,128]{2,1,0:T(8,128)S(1)} %get-tuple-element.67.after), channel_id=1, source_target_pairs={{0,160},{8,168},{16,176},{24,184},{32,192},{40,200},{48,208},{56,2... | collective-permute-start | bytes 98312 | tf_op jit(solution)/shard_map/ppermute | solution.py:348
  75.4 2.7 %collective-permute-done.25.six_off = f32[4,16,128]{2,1,0:T(8,128)S(1)} collective-permute-done((f32[4,16,128]{2,1,0:T(8,128)S(1)}, f32[4,16,128]{2,1,0:T(8,128)S(1)}, u32[]{:S(2)}, u32[]{:S(2)}) %collective-permute-start.25) | collective-permute-done | bytes 32800 | tf_op jit(solution)/shard_map/ppermute | solution.py:348
  78.1 4.0 %shard_map.129 = (bf16[512,512]{1,0:T(8,128)(2,1)}, bf16[512,512]{1,0:T(8,128)(2,1)}) custom-call(f32[4,16,128]{2,1,0:T(8,128)S(1)} %get-tuple-element.42.rates, f32[4,16,128]{2,1,0:T(8,128)S(1)} %get-tuple-element.74.two, f32[4,16,128]{2,1,0:T(8,128)S(1)} %collective-permute-done.24.three_off, f32[4,16,128]{2,1,0:T(8,128)S(1)} %collective-permute-done.25.six_off, ...), custom_call_target="tpu_custom_call" | custom-call | flops 4950000128 | bytes 13500000 | tf_op jit(solution)/shard_map/pallas_call | solution.py:297
  (61 shorter events, 20.2 us)
Async XLA Ops:
  0.6 17.8 %collective-permute-start.6 = (bf16[512,512]{1,0:T(8,128)(2,1)}, bf16[512,512]{1,0:T(8,128)(2,1)S(1)}, u32[]{:S(2)}, u32[]{:S(2)}) collective-permute-start(bf16[512,512]{1,0:T(8,128)(2,1)} %own.1), channel_id=1, source_target_pairs={{0,1},{1,2},{2,3},{3,0},{4,5},{5,6},{6,7},{7,4},{8,11},{9,8},{10,9... | collective-permute-start | bytes 1572872 | tf_op jit(solution)/shard_map/ppermute | solution.py:330
  2.3 16.1 %collective-permute-start.5 = (bf16[512,512]{1,0:T(8,128)(2,1)}, bf16[512,512]{1,0:T(8,128)(2,1)S(1)}, u32[]{:S(2)}, u32[]{:S(2)}) collective-permute-start(bf16[512,512]{1,0:T(8,128)(2,1)} %own.1), channel_id=1, source_target_pairs={{0,4},{1,5},{2,6},{3,7},{4,0},{5,1},{6,2},{7,3},{8,12},{9,13},{10,... | collective-permute-start | bytes 1572872 | tf_op jit(solution)/shard_map/ppermute | solution.py:321
  3.1 15.3 %collective-permute-start.7 = (bf16[512,512]{1,0:T(8,128)(2,1)}, bf16[512,512]{1,0:T(8,128)(2,1)S(1)}, u32[]{:S(2)}, u32[]{:S(2)}) collective-permute-start(bf16[512,512]{1,0:T(8,128)(2,1)} %own.1), channel_id=1, source_target_pairs={{0,3},{1,0},{2,1},{3,2},{4,7},{5,4},{6,5},{7,6},{8,9},{9,10},{10,1... | collective-permute-start | bytes 1572872 | tf_op jit(solution)/shard_map/ppermute | solution.py:330
  11.1 6.6 %collective-permute-start.2 = (f32[4,16,128]{2,1,0:T(8,128)S(1)}, f32[4,16,128]{2,1,0:T(8,128)S(1)}, u32[]{:S(2)}, u32[]{:S(2)}) collective-permute-start(f32[4,16,128]{2,1,0:T(8,128)S(1)} %get-tuple-element.44.pair), channel_id=1, source_target_pairs={{0,64},{8,72},{16,80},{24,88},{32,96},{40,104},{48,112},{56,120},{... | collective-permute-start | bytes 98312 | tf_op jit(solution)/shard_map/ppermute | solution.py:348
  12.7 5.7 %collective-permute-start.1 = (f32[4,16,128]{2,1,0:T(8,128)S(1)}, f32[4,16,128]{2,1,0:T(8,128)S(1)}, u32[]{:S(2)}, u32[]{:S(2)}) collective-permute-start(f32[4,16,128]{2,1,0:T(8,128)S(1)} %get-tuple-element.44.pair), channel_id=1, source_target_pairs={{0,32},{8,40},{16,48},{24,56},{32,64},{40,72},{48,80},{56,88},{64,... | collective-permute-start | bytes 98312 | tf_op jit(solution)/shard_map/ppermute | solution.py:348
  18.5 14.5 %collective-permute-start.8 = (bf16[512,512]{1,0:T(8,128)(2,1)S(1)}, bf16[512,512]{1,0:T(8,128)(2,1)S(1)}, u32[]{:S(2)}, u32[]{:S(2)}) collective-permute-start(bf16[512,512]{1,0:T(8,128)(2,1)S(1)} %get-tuple-element.47.after), channel_id=1, source_target_pairs={{0,1},{1,2},{2,3},{3,0},{4,5},{5,6},{6,7},{7,4},{8,11},{9,8},{10,9... | collective-permute-start | bytes 1572872 | tf_op jit(solution)/shard_map/ppermute | solution.py:330
  18.9 17.9 %collective-permute-start.11 = (bf16[512,512]{1,0:T(8,128)(2,1)S(1)}, bf16[512,512]{1,0:T(8,128)(2,1)S(1)}, u32[]{:S(2)}, u32[]{:S(2)}) collective-permute-start(bf16[512,512]{1,0:T(8,128)(2,1)S(1)} %collective-permute-done.7.ahead), channel_id=1, source_target_pairs={{0,4},{1,5},{2,6},{3,7},{4,0},{5,1},{6,2},{7,3},{8,12},{9,13},{10,... | collective-permute-start | bytes 1572872 | tf_op jit(solution)/shard_map/ppermute | solution.py:321
  20.4 16.4 %collective-permute-start.10 = (bf16[512,512]{1,0:T(8,128)(2,1)S(1)}, bf16[512,512]{1,0:T(8,128)(2,1)S(1)}, u32[]{:S(2)}, u32[]{:S(2)}) collective-permute-start(bf16[512,512]{1,0:T(8,128)(2,1)S(1)} %get-tuple-element.56), channel_id=1, source_target_pairs={{0,1},{1,2},{2,3},{3,0},{4,5},{5,6},{6,7},{7,4},{8,11},{9,8},{10,9... | collective-permute-start | bytes 1572872 | tf_op jit(solution)/shard_map/ppermute | solution.py:330
  22.0 5.3 %collective-permute-start.4 = (f32[4,16,128]{2,1,0:T(8,128)S(1)}, f32[4,16,128]{2,1,0:T(8,128)S(1)}, u32[]{:S(2)}, u32[]{:S(2)}) collective-permute-start(f32[4,16,128]{2,1,0:T(8,128)S(1)} %get-tuple-element.46), channel_id=1, source_target_pairs={{0,192},{8,200},{16,208},{24,216},{32,224},{40,232},{48,240},{56,2... | collective-permute-start | bytes 98312 | tf_op jit(solution)/shard_map/ppermute | solution.py:348
  25.7 7.3 %collective-permute-start.3 = (f32[4,16,128]{2,1,0:T(8,128)S(1)}, f32[4,16,128]{2,1,0:T(8,128)S(1)}, u32[]{:S(2)}, u32[]{:S(2)}) collective-permute-start(f32[4,16,128]{2,1,0:T(8,128)S(1)} %get-tuple-element.46), channel_id=1, source_target_pairs={{0,96},{8,104},{16,112},{24,120},{32,128},{40,136},{48,144},{56,15... | collective-permute-start | bytes 98312 | tf_op jit(solution)/shard_map/ppermute | solution.py:348
  33.0 5.5 %collective-permute-start.9 = (f32[4,16,128]{2,1,0:T(8,128)S(1)}, f32[4,16,128]{2,1,0:T(8,128)S(1)}, u32[]{:S(2)}, u32[]{:S(2)}) collective-permute-start(f32[4,16,128]{2,1,0:T(8,128)S(1)} %get-tuple-element.48), channel_id=1, source_target_pairs={{0,16},{8,24},{16,0},{24,8},{32,48},{40,56},{48,32},{56,40},{64,80... | collective-permute-start | bytes 98312 | tf_op jit(solution)/shard_map/ppermute | solution.py:343
  35.5 10.4 %collective-permute-start.12 = (bf16[512,512]{1,0:T(8,128)(2,1)S(1)}, bf16[512,512]{1,0:T(8,128)(2,1)S(1)}, u32[]{:S(2)}, u32[]{:S(2)}) collective-permute-start(bf16[512,512]{1,0:T(8,128)(2,1)S(1)} %collective-permute-done.8.after_too.after.got_across), channel_id=1, source_target_pairs={{0,1},{1,2},{2,3},{3,0},{4,5},{5,6},{6,7},{7,4},{8,11},{9,8},{10,9... | collective-permute-start | bytes 1572872 | tf_op jit(solution)/shard_map/ppermute | solution.py:330
  42.2 13.4 %collective-permute-start.21 = (bf16[512,512]{1,0:T(8,128)(2,1)S(1)}, bf16[512,512]{1,0:T(8,128)(2,1)S(1)}, u32[]{:S(2)}, u32[]{:S(2)}) collective-permute-start(bf16[512,512]{1,0:T(8,128)(2,1)S(1)} %get-tuple-element.71), channel_id=1, source_target_pairs={{0,1},{1,2},{2,3},{3,0},{4,5},{5,6},{6,7},{7,4},{8,11},{9,8},{10,9... | collective-permute-start | bytes 1572872 | tf_op jit(solution)/shard_map/ppermute | solution.py:330
  48.8 13.6 %collective-permute-start.14 = (bf16[512,512]{1,0:T(8,128)(2,1)S(1)}, bf16[512,512]{1,0:T(8,128)(2,1)S(1)}, u32[]{:S(2)}, u32[]{:S(2)}) collective-permute-start(bf16[512,512]{1,0:T(8,128)(2,1)S(1)} %get-tuple-element.58.after), channel_id=1, source_target_pairs={{0,1},{1,2},{2,3},{3,0},{4,5},{5,6},{6,7},{7,4},{8,11},{9,8},{10,9... | collective-permute-start | bytes 1572872 | tf_op jit(solution)/shard_map/ppermute | solution.py:330
  50.1 5.5 %collective-permute-start.16 = (f32[4,16,128]{2,1,0:T(8,128)S(1)}, f32[4,16,128]{2,1,0:T(8,128)S(1)}, u32[]{:S(2)}, u32[]{:S(2)}) collective-permute-start(f32[4,16,128]{2,1,0:T(8,128)S(1)} %get-tuple-element.60.after.pair), channel_id=1, source_target_pairs={{0,16},{8,24},{16,0},{24,8},{32,48},{40,56},{48,32},{56,40},{64,80... | collective-permute-start | bytes 98312 | tf_op jit(solution)/shard_map/ppermute | solution.py:343
  53.1 13.8 %collective-permute-start.15 = (bf16[512,512]{1,0:T(8,128)(2,1)S(1)}, bf16[512,512]{1,0:T(8,128)(2,1)S(1)}, u32[]{:S(2)}, u32[]{:S(2)}) collective-permute-start(bf16[512,512]{1,0:T(8,128)(2,1)S(1)} %get-tuple-element.62), channel_id=1, source_target_pairs={{0,4},{1,5},{2,6},{3,7},{4,0},{5,1},{6,2},{7,3},{8,12},{9,13},{10,... | collective-permute-start | bytes 1572872 | tf_op jit(solution)/shard_map/ppermute | solution.py:321
  55.8 14.7 %collective-permute-start.22 = (bf16[512,512]{1,0:T(8,128)(2,1)S(1)}, bf16[512,512]{1,0:T(8,128)(2,1)S(1)}, u32[]{:S(2)}, u32[]{:S(2)}) collective-permute-start(bf16[512,512]{1,0:T(8,128)(2,1)S(1)} %shard_map.126), channel_id=1, source_target_pairs={{0,1},{1,2},{2,3},{3,0},{4,5},{5,6},{6,7},{7,4},{8,11},{9,8},{10,9... | collective-permute-start | bytes 1572872 | tf_op jit(solution)/shard_map/ppermute | solution.py:330
  56.5 4.8 %collective-permute-start.18 = (f32[4,16,128]{2,1,0:T(8,128)S(1)}, f32[4,16,128]{2,1,0:T(8,128)S(1)}, u32[]{:S(2)}, u32[]{:S(2)}) collective-permute-start(f32[4,16,128]{2,1,0:T(8,128)S(1)} %get-tuple-element.66.pair.after), channel_id=1, source_target_pairs={{0,192},{8,200},{16,208},{24,216},{32,224},{40,232},{48,240},{56,2... | collective-permute-start | bytes 98312 | tf_op jit(solution)/shard_map/ppermute | solution.py:348
  58.5 3.9 %collective-permute-start.17 = (f32[4,16,128]{2,1,0:T(8,128)S(1)}, f32[4,16,128]{2,1,0:T(8,128)S(1)}, u32[]{:S(2)}, u32[]{:S(2)}) collective-permute-start(f32[4,16,128]{2,1,0:T(8,128)S(1)} %get-tuple-element.66.pair.after), channel_id=1, source_target_pairs={{0,224},{8,232},{16,240},{24,248},{32,0},{40,8},{48,16},{56,24},{6... | collective-permute-start | bytes 98312 | tf_op jit(solution)/shard_map/ppermute | solution.py:348
  67.2 14.9 %collective-permute-start.19 = (bf16[512,512]{1,0:T(8,128)(2,1)S(1)}, bf16[512,512]{1,0:T(8,128)(2,1)S(1)}, u32[]{:S(2)}, u32[]{:S(2)}) collective-permute-start(bf16[512,512]{1,0:T(8,128)(2,1)S(1)} %get-tuple-element.68), channel_id=1, source_target_pairs={{0,1},{1,2},{2,3},{3,0},{4,5},{5,6},{6,7},{7,4},{8,11},{9,8},{10,9... | collective-permute-start | bytes 1572872 | tf_op jit(solution)/shard_map/ppermute | solution.py:330
  68.2 14.0 %collective-permute-start.20 = (bf16[512,512]{1,0:T(8,128)(2,1)S(1)}, bf16[512,512]{1,0:T(8,128)(2,1)S(1)}, u32[]{:S(2)}, u32[]{:S(2)}) collective-permute-start(bf16[512,512]{1,0:T(8,128)(2,1)S(1)} %get-tuple-element.69), channel_id=1, source_target_pairs={{0,3},{1,0},{2,1},{3,2},{4,7},{5,4},{6,5},{7,6},{8,9},{9,10},{10,1... | collective-permute-start | bytes 1572872 | tf_op jit(solution)/shard_map/ppermute | solution.py:330
  70.6 11.5 %collective-permute-start.23 = (bf16[512,512]{1,0:T(8,128)(2,1)S(1)}, bf16[512,512]{1,0:T(8,128)(2,1)S(1)}, u32[]{:S(2)}, u32[]{:S(2)}) collective-permute-start(bf16[512,512]{1,0:T(8,128)(2,1)S(1)} %shard_map.127), channel_id=1, source_target_pairs={{0,4},{1,5},{2,6},{3,7},{4,0},{5,1},{6,2},{7,3},{8,12},{9,13},{10,... | collective-permute-start | bytes 1572872 | tf_op jit(solution)/shard_map/ppermute | solution.py:321
  71.9 6.1 %collective-permute-start.25 = (f32[4,16,128]{2,1,0:T(8,128)S(1)}, f32[4,16,128]{2,1,0:T(8,128)S(1)}, u32[]{:S(2)}, u32[]{:S(2)}) collective-permute-start(f32[4,16,128]{2,1,0:T(8,128)S(1)} %get-tuple-element.67.after), channel_id=1, source_target_pairs={{0,64},{8,72},{16,80},{24,88},{32,96},{40,104},{48,112},{56,120},{... | collective-permute-start | bytes 98312 | tf_op jit(solution)/shard_map/ppermute | solution.py:348
  71.9 6.1 %collective-permute-start.24 = (f32[4,16,128]{2,1,0:T(8,128)S(1)}, f32[4,16,128]{2,1,0:T(8,128)S(1)}, u32[]{:S(2)}, u32[]{:S(2)}) collective-permute-start(f32[4,16,128]{2,1,0:T(8,128)S(1)} %get-tuple-element.67.after), channel_id=1, source_target_pairs={{0,160},{8,168},{16,176},{24,184},{32,192},{40,200},{48,208},{56,2... | collective-permute-start | bytes 98312 | tf_op jit(solution)/shard_map/ppermute | solution.py:348
  (8 other events, 87.5 us)

commit v4 on v3

--- a/solution.py
+++ b/solution.py
@@ -210,22 +210,17 @@
     products(mixed_in, weight, ((across_far, 0, ACROSS_FAR), (far, 0, FAR)))
 
 
-def rest_kernel(mixed_in, weight, after, over, side, ahead, behind, across, own):
-    outs = ((over, 0, ACROSS_BEHIND), (side, 0, ACROSS_AHEAD), (ahead, 0, AHEAD))
+def over_kernel(mixed_in, weight, after, over, side):
+    products(mixed_in, weight, ((over, 0, ACROSS_BEHIND), (side, 0, ACROSS_AHEAD)))
+
+
+def rest_kernel(mixed_in, weight, after, ahead, behind, across, own):
+    outs = ((ahead, 0, AHEAD),)
     products(mixed_in, weight, outs + ((behind, 0, BEHIND), (across, 0, ACROSS), (own, 0, OWN)))
 
 
-def side_kernel(got, side, after, out):
-    out[...] = (wide(side[...]) + wide(got[...])).astype(BF16)
-
-
-def second_kernel(along, over, ahead, behind, after, ahead_out, behind_out):
-    ahead_out[...] = (wide(ahead[...]) + wide(along[...])).astype(BF16)
-    behind_out[...] = (wide(behind[...]) + wide(over[...])).astype(BF16)
-
-
-def third_kernel(across, got, after, out):
-    out[...] = (wide(across[...]) + wide(got[...])).astype(BF16)
+def sum_kernel(got, part, after, out):
+    out[...] = (wide(part[...]) + wide(got[...])).astype(BF16)
 
 
 def last_kernel(own, ahead, behind, across, out):
@@ -429,30 +424,21 @@
     )
     pair, before = small(pair_kernel, True, rates, back_total, other_core(back_total))
     half_other = other_half(pair)
-    s_over, side, ahead_part, behind_part, across_part, own_part = call(
-        rest_kernel, [(BLOCK, BF16)] * 6, [], 2.0, 6, mixed_in, weight, pair
-    )
+    s_over, side = call(over_kernel, [(BLOCK, BF16)] * 2, [], 0.7, 6, mixed_in, weight, pair)
     group, before = small(group_kernel, True, rates, pair, before, half_other)
+    ahead_part, behind_part, across_part, own_part = call(
+        rest_kernel, [(BLOCK, BF16)] * 4, [], 2.0, 6, mixed_in, weight, group
+    )
     offs = earlier(group, 1, True), earlier(group, 2, True)
     two, three = small(three_kernel, True, rates, group, *offs)
     offs = earlier(three, 3, True), earlier(three, 6, True)
 
     g_over = shift_x(s_over)
-    (s_side,) = call(side_kernel, [(BLOCK, BF16)], [], 0.5, 4, g_across_far, side, group)
-    s_ahead, s_behind = call(
-        second_kernel,
-        [(BLOCK, BF16)] * 2,
-        [],
-        1.0,
-        4,
-        g_along,
-        g_over,
-        ahead_part,
-        behind_part,
-        three,
-    )
+    (s_side,) = call(sum_kernel, [(BLOCK, BF16)], [], 0.5, 4, g_across_far, side, group)
+    (s_ahead,) = call(sum_kernel, [(BLOCK, BF16)], [], 0.5, 4, g_along, ahead_part, three)
+    (s_behind,) = call(sum_kernel, [(BLOCK, BF16)], [], 0.5, 4, g_over, behind_part, three)
     g_side, g_ahead, g_behind = along_y(s_side, 1), along_y(s_ahead, 1), along_y(s_behind, -1)
-    (s_across,) = call(third_kernel, [(BLOCK, BF16)], [], 0.5, 4, across_part, g_side, three)
+    (s_across,) = call(sum_kernel, [(BLOCK, BF16)], [], 0.5, 4, g_side, across_part, three)
     (mixed,) = call(
         last_kernel, [(BLOCK, BF16)], [], 0.5, 4, own_part, g_ahead, g_behind, shift_x(s_across)
     )

time: 84.5 us -> 82.5 us (0.976); the launches traced: 83.2 us -> 82.3 us
  waiting for transfers between devices: 26.9 us -> 23.2 us
  starting transfers between devices: 35.3 us -> 37.9 us
    ppermute x8, starting transfers between devices: 12.7 us -> 15.8 us  [earlier(): lax.ppermute(value, 'ctx', ctx_perm(lambda z, h, c: (z + move, h, c)))]
    ppermute x4, waiting for transfers between devices: 4.49 us -> 1.78 us  [shift_x(): return lax.ppermute(value, 'tp', [(at, (at + 4) % 8) for at in range(8)])]
    ppermute x10, starting transfers between devices: 13.9 us -> 11.7 us  [along_y(): return lax.ppermute(value, ('ctx', 'tp'), pairs)]
    ppermute x4, starting transfers between devices: 4.92 us -> 6.63 us  [shift_x(): return lax.ppermute(value, 'tp', [(at, (at + 4) % 8) for at in range(8)])]
    ppermute x8, waiting for transfers between devices: 16.3 us -> 14.8 us  [earlier(): lax.ppermute(value, 'ctx', ctx_perm(lambda z, h, c: (z + move, h, c)))]
    pallas_call x19 -> x21, Pallas kernels: 17.9 us -> 18.1 us  [call(): pl.pallas_call(kernel, out_shape=[jax.ShapeDtypeStruct(shape, kind) for s...]
  transfers between devices with their start and end apart: 26 -> 26, of which waited for: 13 -> 13; matrix products, arithmetic and copies ran while one was open for 3% -> 3% of each run, Pallas kernels for 20% -> 21%
where the time goes in v4:
time: 82.5 us; the launch traced here: 82.3 us
  starting transfers between devices  37.9 us (46%)
  waiting for transfers between devices  23.2 us (28%)
  Pallas kernels  18.1 us (22%)
  other arithmetic  2.14 us (3%)
  between operations  0.87 us (1%)
    pallas_call x21, Pallas kernels, call(): pl.pallas_call(kernel, out_shape=[jax.ShapeDtypeStruct(shape, kind) for s...  18.1 us
    ppermute x8, starting transfers between devices, earlier(): lax.ppermute(value, 'ctx', ctx_perm(lambda z, h, c: (z + move, h, c)))  15.8 us
    ppermute x8, waiting for transfers between devices, earlier(): lax.ppermute(value, 'ctx', ctx_perm(lambda z, h, c: (z + move, h, c)))  14.8 us
    ppermute x10, starting transfers between devices, along_y(): return lax.ppermute(value, ('ctx', 'tp'), pairs)  11.7 us
    ppermute x4, starting transfers between devices, shift_x(): return lax.ppermute(value, 'tp', [(at, (at + 4) % 8) for at in range(8)])  6.63 us
    ppermute x2, starting transfers between devices, other_half(): return lax.ppermute(value, 'ctx', ctx_perm(lambda z, h, c: (z, h + 1, c)))  3.71 us
    ppermute x10, waiting for transfers between devices, along_y(): return lax.ppermute(value, ('ctx', 'tp'), pairs)  2.8 us
    ppermute x2, waiting for transfers between devices, other_half(): return lax.ppermute(value, 'ctx', ctx_perm(lambda z, h, c: (z, h + 1, c)))  2.01 us
  transfers between devices with their start and end apart: 26, of which 13 were waited for; matrix products, arithmetic and copies ran while one was open for 3% of the time, Pallas kernels for 21%

profile of v4, /device:TPU:2, one launch (start us, length us, event | category | flops | bytes accessed | tf_op | source)
XLA Modules:
  0.0 82.3 jit_solution(18374371257214954438)
XLA Ops:
  0.6 2.4 %collective-permute-start.5 = (bf16[512,512]{1,0:T(8,128)(2,1)}, bf16[512,512]{1,0:T(8,128)(2,1)S(1)}, u32[]{:S(2)}, u32[]{:S(2)}) collective-permute-start(bf16[512,512]{1,0:T(8,128)(2,1)} %own.1), channel_id=1, source_target_pairs={{0,4},{1,5},{2,6},{3,7},{4,0},{5,1},{6,2},{7,3},{8,12},{9,13},{10,... | collective-permute-start | bytes 1572872 | tf_op jit(solution)/shard_map/ppermute | solution.py:316
  3.0 3.2 %collective-permute-start.7 = (bf16[512,512]{1,0:T(8,128)(2,1)}, bf16[512,512]{1,0:T(8,128)(2,1)S(1)}, u32[]{:S(2)}, u32[]{:S(2)}) collective-permute-start(bf16[512,512]{1,0:T(8,128)(2,1)} %own.1), channel_id=1, source_target_pairs={{0,3},{1,0},{2,1},{3,2},{4,7},{5,4},{6,5},{7,6},{8,9},{9,10},{10,1... | collective-permute-start | bytes 1572872 | tf_op jit(solution)/shard_map/ppermute | solution.py:325
  11.3 3.3 %collective-permute-start.2 = (f32[4,16,128]{2,1,0:T(8,128)S(1)}, f32[4,16,128]{2,1,0:T(8,128)S(1)}, u32[]{:S(2)}, u32[]{:S(2)}) collective-permute-start(f32[4,16,128]{2,1,0:T(8,128)S(1)} %get-tuple-element.42.pair), channel_id=1, source_target_pairs={{0,64},{8,72},{16,80},{24,88},{32,96},{40,104},{48,112},{56,120},{... | collective-permute-start | bytes 98312 | tf_op jit(solution)/shard_map/ppermute | solution.py:343
  14.6 2.7 %collective-permute-done.1.one_off.after = f32[4,16,128]{2,1,0:T(8,128)S(1)} collective-permute-done((f32[4,16,128]{2,1,0:T(8,128)S(1)}, f32[4,16,128]{2,1,0:T(8,128)S(1)}, u32[]{:S(2)}, u32[]{:S(2)}) %collective-permute-start.1) | collective-permute-done | bytes 32800 | tf_op jit(solution)/shard_map/ppermute | solution.py:343
  17.4 2.3 %collective-permute-done.2.two_off.after_too = f32[4,16,128]{2,1,0:T(8,128)S(1)} collective-permute-done((f32[4,16,128]{2,1,0:T(8,128)S(1)}, f32[4,16,128]{2,1,0:T(8,128)S(1)}, u32[]{:S(2)}, u32[]{:S(2)}) %collective-permute-start.2) | collective-permute-done | bytes 32800 | tf_op jit(solution)/shard_map/ppermute | solution.py:343
  20.2 1.6 %collective-permute-start.10 = (bf16[512,512]{1,0:T(8,128)(2,1)S(1)}, bf16[512,512]{1,0:T(8,128)(2,1)S(1)}, u32[]{:S(2)}, u32[]{:S(2)}) collective-permute-start(bf16[512,512]{1,0:T(8,128)(2,1)S(1)} %get-tuple-element.54), channel_id=1, source_target_pairs={{0,1},{1,2},{2,3},{3,0},{4,5},{5,6},{6,7},{7,4},{8,11},{9,8},{10,9... | collective-permute-start | bytes 1572872 | tf_op jit(solution)/shard_map/ppermute | solution.py:325
  21.8 1.5 %collective-permute-start.11 = (bf16[512,512]{1,0:T(8,128)(2,1)S(1)}, bf16[512,512]{1,0:T(8,128)(2,1)S(1)}, u32[]{:S(2)}, u32[]{:S(2)}) collective-permute-start(bf16[512,512]{1,0:T(8,128)(2,1)S(1)} %collective-permute-done.7.ahead), channel_id=1, source_target_pairs={{0,4},{1,5},{2,6},{3,7},{4,0},{5,1},{6,2},{7,3},{8,12},{9,13},{10,... | collective-permute-start | bytes 1572872 | tf_op jit(solution)/shard_map/ppermute | solution.py:316
  23.3 2.4 %collective-permute-start.3 = (f32[4,16,128]{2,1,0:T(8,128)S(1)}, f32[4,16,128]{2,1,0:T(8,128)S(1)}, u32[]{:S(2)}, u32[]{:S(2)}) collective-permute-start(f32[4,16,128]{2,1,0:T(8,128)S(1)} %get-tuple-element.44), channel_id=1, source_target_pairs={{0,96},{8,104},{16,112},{24,120},{32,128},{40,136},{48,144},{56,15... | collective-permute-start | bytes 98312 | tf_op jit(solution)/shard_map/ppermute | solution.py:343
  27.9 2.4 %collective-permute-done.3.three_off = f32[4,16,128]{2,1,0:T(8,128)S(1)} collective-permute-done((f32[4,16,128]{2,1,0:T(8,128)S(1)}, f32[4,16,128]{2,1,0:T(8,128)S(1)}, u32[]{:S(2)}, u32[]{:S(2)}) %collective-permute-start.3) | collective-permute-done | bytes 32800 | tf_op jit(solution)/shard_map/ppermute | solution.py:343
  30.6 2.2 %collective-permute-start.9 = (f32[4,16,128]{2,1,0:T(8,128)S(1)}, f32[4,16,128]{2,1,0:T(8,128)S(1)}, u32[]{:S(2)}, u32[]{:S(2)}) collective-permute-start(f32[4,16,128]{2,1,0:T(8,128)S(1)} %get-tuple-element.46), channel_id=1, source_target_pairs={{0,16},{8,24},{16,0},{24,8},{32,48},{40,56},{48,32},{56,40},{64,80... | collective-permute-start | bytes 98312 | tf_op jit(solution)/shard_map/ppermute | solution.py:338
  32.8 1.8 %collective-permute-start.12 = (bf16[512,512]{1,0:T(8,128)(2,1)S(1)}, bf16[512,512]{1,0:T(8,128)(2,1)S(1)}, u32[]{:S(2)}, u32[]{:S(2)}) collective-permute-start(bf16[512,512]{1,0:T(8,128)(2,1)S(1)} %collective-permute-done.8.after_too.after.got_across), channel_id=1, source_target_pairs={{0,1},{1,2},{2,3},{3,0},{4,5},{5,6},{6,7},{7,4},{8,11},{9,8},{10,9... | collective-permute-start | bytes 1572872 | tf_op jit(solution)/shard_map/ppermute | solution.py:325
  36.9 3.0 %shard_map.117 = (f32[512,512]{1,0:T(8,128)S(1)}, bf16[512,512]{1,0:T(8,128)(2,1)S(1)}) custom-call(f32[4,16,128]{2,1,0:T(8,128)S(1)} %get-tuple-element.40.rates, f32[4,16,128]{2,1,0:T(8,128)S(1)} %collective-permute-done.9.other, f32[4,16,128]{2,1,0:T(8,128)S(1)} %get-tuple-element.47.over, f32[4,16,128]{2,1,0:T(8,128)S(1)} %get-tuple-element.48.before, ...), custom_call_target="tpu_custom_call" | custom-call | flops 4950000128 | bytes 13500000 | tf_op jit(solution)/shard_map/pallas_call | solution.py:292
  41.7 1.5 %collective-permute-done.12.far = bf16[512,512]{1,0:T(8,128)(2,1)S(1)} collective-permute-done((bf16[512,512]{1,0:T(8,128)(2,1)S(1)}, bf16[512,512]{1,0:T(8,128)(2,1)S(1)}, u32[]{:S(2)}, u32[]{:S(2)}) %collective-permute-start.12) | collective-permute-done | bytes 524320 | tf_op jit(solution)/shard_map/ppermute | solution.py:325
  43.2 3.0 %shard_map.120 = (bf16[512,512]{1,0:T(8,128)(2,1)}, bf16[512,512]{1,0:T(8,128)(2,1)S(1)}, f32[4,128,128]{2,1,0:T(8,128)S(1)}, f32[4,16,128]{2,1,0:T(8,128)S(1)}) custom-call(bf16[512,4096]{1,0:T(8,128)(2,1)S(1)} %copy-done, f32[512,512]{1,0:T(8,128)S(1)} %shard_map.118.acc, bf16[512,512]{1,0:T(8,128)(2,1)S(1)} %collective-permute-done.12.far, ...), custom_call_target="tpu_custom_call" | custom-call | flops 6600000000 | bytes 18000000 | tf_op jit(solution)/shard_map/pallas_call | solution.py:292
  47.4 1.5 %collective-permute-start.14 = (f32[4,16,128]{2,1,0:T(8,128)S(1)}, f32[4,16,128]{2,1,0:T(8,128)S(1)}, u32[]{:S(2)}, u32[]{:S(2)}) collective-permute-start(f32[4,16,128]{2,1,0:T(8,128)S(1)} %get-tuple-element.58.pair.after), channel_id=1, source_target_pairs={{0,16},{8,24},{16,0},{24,8},{32,48},{40,56},{48,32},{56,40},{64,80... | collective-permute-start | bytes 98312 | tf_op jit(solution)/shard_map/ppermute | solution.py:338
  50.9 2.0 %collective-permute-done.14.other = f32[4,16,128]{2,1,0:T(8,128)S(1)} collective-permute-done((f32[4,16,128]{2,1,0:T(8,128)S(1)}, f32[4,16,128]{2,1,0:T(8,128)S(1)}, u32[]{:S(2)}, u32[]{:S(2)}) %collective-permute-start.14) | collective-permute-done | bytes 32800 | tf_op jit(solution)/shard_map/ppermute | solution.py:338
  53.8 2.9 %collective-permute-start.16 = (f32[4,16,128]{2,1,0:T(8,128)S(1)}, f32[4,16,128]{2,1,0:T(8,128)S(1)}, u32[]{:S(2)}, u32[]{:S(2)}) collective-permute-start(f32[4,16,128]{2,1,0:T(8,128)S(1)} %get-tuple-element.60.after.pair), channel_id=1, source_target_pairs={{0,224},{8,232},{16,240},{24,248},{32,0},{40,8},{48,16},{56,24},{6... | collective-permute-start | bytes 98312 | tf_op jit(solution)/shard_map/ppermute | solution.py:343
  59.4 2.2 %collective-permute-done.17.two_off = f32[4,16,128]{2,1,0:T(8,128)S(1)} collective-permute-done((f32[4,16,128]{2,1,0:T(8,128)S(1)}, f32[4,16,128]{2,1,0:T(8,128)S(1)}, u32[]{:S(2)}, u32[]{:S(2)}) %collective-permute-start.17) | collective-permute-done | bytes 32800 | tf_op jit(solution)/shard_map/ppermute | solution.py:343
  62.3 1.8 %collective-permute-done.19.got = bf16[512,512]{1,0:T(8,128)(2,1)S(1)} collective-permute-done((bf16[512,512]{1,0:T(8,128)(2,1)S(1)}, bf16[512,512]{1,0:T(8,128)(2,1)S(1)}, u32[]{:S(2)}, u32[]{:S(2)}) %collective-permute-start.19) | collective-permute-done | bytes 524320 | tf_op jit(solution)/shard_map/ppermute | solution.py:316
  64.2 1.8 %collective-permute-start.20 = (bf16[512,512]{1,0:T(8,128)(2,1)S(1)}, bf16[512,512]{1,0:T(8,128)(2,1)S(1)}, u32[]{:S(2)}, u32[]{:S(2)}) collective-permute-start(bf16[512,512]{1,0:T(8,128)(2,1)S(1)} %shard_map.127), channel_id=1, source_target_pairs={{0,3},{1,0},{2,1},{3,2},{4,7},{5,4},{6,5},{7,6},{8,9},{9,10},{10,1... | collective-permute-start | bytes 1572872 | tf_op jit(solution)/shard_map/ppermute | solution.py:325
  66.1 1.5 %collective-permute-start.23 = (bf16[512,512]{1,0:T(8,128)(2,1)S(1)}, bf16[512,512]{1,0:T(8,128)(2,1)S(1)}, u32[]{:S(2)}, u32[]{:S(2)}) collective-permute-start(bf16[512,512]{1,0:T(8,128)(2,1)S(1)} %shard_map.129), channel_id=1, source_target_pairs={{0,4},{1,5},{2,6},{3,7},{4,0},{5,1},{6,2},{7,3},{8,12},{9,13},{10,... | collective-permute-start | bytes 1572872 | tf_op jit(solution)/shard_map/ppermute | solution.py:316
  67.6 3.5 %collective-permute-start.24 = (f32[4,16,128]{2,1,0:T(8,128)S(1)}, f32[4,16,128]{2,1,0:T(8,128)S(1)}, u32[]{:S(2)}, u32[]{:S(2)}) collective-permute-start(f32[4,16,128]{2,1,0:T(8,128)S(1)} %get-tuple-element.63.after), channel_id=1, source_target_pairs={{0,160},{8,168},{16,176},{24,184},{32,192},{40,200},{48,208},{56,2... | collective-permute-start | bytes 98312 | tf_op jit(solution)/shard_map/ppermute | solution.py:343
  73.3 3.8 %collective-permute-done.25.six_off = f32[4,16,128]{2,1,0:T(8,128)S(1)} collective-permute-done((f32[4,16,128]{2,1,0:T(8,128)S(1)}, f32[4,16,128]{2,1,0:T(8,128)S(1)}, u32[]{:S(2)}, u32[]{:S(2)}) %collective-permute-start.25) | collective-permute-done | bytes 32800 | tf_op jit(solution)/shard_map/ppermute | solution.py:343
  77.2 4.0 %shard_map.131 = (bf16[512,512]{1,0:T(8,128)(2,1)}, bf16[512,512]{1,0:T(8,128)(2,1)}) custom-call(f32[4,16,128]{2,1,0:T(8,128)S(1)} %get-tuple-element.40.rates, f32[4,16,128]{2,1,0:T(8,128)S(1)} %get-tuple-element.70.two, f32[4,16,128]{2,1,0:T(8,128)S(1)} %collective-permute-done.24.three_off, f32[4,16,128]{2,1,0:T(8,128)S(1)} %collective-permute-done.25.six_off, ...), custom_call_target="tpu_custom_call" | custom-call | flops 4950000128 | bytes 13500000 | tf_op jit(solution)/shard_map/pallas_call | solution.py:292
  (63 shorter events, 23.1 us)
Async XLA Ops:
  0.6 19.1 %collective-permute-start.5 = (bf16[512,512]{1,0:T(8,128)(2,1)}, bf16[512,512]{1,0:T(8,128)(2,1)S(1)}, u32[]{:S(2)}, u32[]{:S(2)}) collective-permute-start(bf16[512,512]{1,0:T(8,128)(2,1)} %own.1), channel_id=1, source_target_pairs={{0,4},{1,5},{2,6},{3,7},{4,0},{5,1},{6,2},{7,3},{8,12},{9,13},{10,... | collective-permute-start | bytes 1572872 | tf_op jit(solution)/shard_map/ppermute | solution.py:316
  3.0 16.7 %collective-permute-start.6 = (bf16[512,512]{1,0:T(8,128)(2,1)}, bf16[512,512]{1,0:T(8,128)(2,1)S(1)}, u32[]{:S(2)}, u32[]{:S(2)}) collective-permute-start(bf16[512,512]{1,0:T(8,128)(2,1)} %own.1), channel_id=1, source_target_pairs={{0,1},{1,2},{2,3},{3,0},{4,5},{5,6},{6,7},{7,4},{8,11},{9,8},{10,9... | collective-permute-start | bytes 1572872 | tf_op jit(solution)/shard_map/ppermute | solution.py:325
  3.0 16.7 %collective-permute-start.7 = (bf16[512,512]{1,0:T(8,128)(2,1)}, bf16[512,512]{1,0:T(8,128)(2,1)S(1)}, u32[]{:S(2)}, u32[]{:S(2)}) collective-permute-start(bf16[512,512]{1,0:T(8,128)(2,1)} %own.1), channel_id=1, source_target_pairs={{0,3},{1,0},{2,1},{3,2},{4,7},{5,4},{6,5},{7,6},{8,9},{9,10},{10,1... | collective-permute-start | bytes 1572872 | tf_op jit(solution)/shard_map/ppermute | solution.py:325
  11.1 6.3 %collective-permute-start.1 = (f32[4,16,128]{2,1,0:T(8,128)S(1)}, f32[4,16,128]{2,1,0:T(8,128)S(1)}, u32[]{:S(2)}, u32[]{:S(2)}) collective-permute-start(f32[4,16,128]{2,1,0:T(8,128)S(1)} %get-tuple-element.42.pair), channel_id=1, source_target_pairs={{0,32},{8,40},{16,48},{24,56},{32,64},{40,72},{48,80},{56,88},{64,... | collective-permute-start | bytes 98312 | tf_op jit(solution)/shard_map/ppermute | solution.py:343
  11.3 8.3 %collective-permute-start.2 = (f32[4,16,128]{2,1,0:T(8,128)S(1)}, f32[4,16,128]{2,1,0:T(8,128)S(1)}, u32[]{:S(2)}, u32[]{:S(2)}) collective-permute-start(f32[4,16,128]{2,1,0:T(8,128)S(1)} %get-tuple-element.42.pair), channel_id=1, source_target_pairs={{0,64},{8,72},{16,80},{24,88},{32,96},{40,104},{48,112},{56,120},{... | collective-permute-start | bytes 98312 | tf_op jit(solution)/shard_map/ppermute | solution.py:343
  19.8 10.7 %collective-permute-start.8 = (bf16[512,512]{1,0:T(8,128)(2,1)S(1)}, bf16[512,512]{1,0:T(8,128)(2,1)S(1)}, u32[]{:S(2)}, u32[]{:S(2)}) collective-permute-start(bf16[512,512]{1,0:T(8,128)(2,1)S(1)} %get-tuple-element.45.after), channel_id=1, source_target_pairs={{0,1},{1,2},{2,3},{3,0},{4,5},{5,6},{6,7},{7,4},{8,11},{9,8},{10,9... | collective-permute-start | bytes 1572872 | tf_op jit(solution)/shard_map/ppermute | solution.py:325
  20.2 15.6 %collective-permute-start.10 = (bf16[512,512]{1,0:T(8,128)(2,1)S(1)}, bf16[512,512]{1,0:T(8,128)(2,1)S(1)}, u32[]{:S(2)}, u32[]{:S(2)}) collective-permute-start(bf16[512,512]{1,0:T(8,128)(2,1)S(1)} %get-tuple-element.54), channel_id=1, source_target_pairs={{0,1},{1,2},{2,3},{3,0},{4,5},{5,6},{6,7},{7,4},{8,11},{9,8},{10,9... | collective-permute-start | bytes 1572872 | tf_op jit(solution)/shard_map/ppermute | solution.py:325
  21.8 14.1 %collective-permute-start.11 = (bf16[512,512]{1,0:T(8,128)(2,1)S(1)}, bf16[512,512]{1,0:T(8,128)(2,1)S(1)}, u32[]{:S(2)}, u32[]{:S(2)}) collective-permute-start(bf16[512,512]{1,0:T(8,128)(2,1)S(1)} %collective-permute-done.7.ahead), channel_id=1, source_target_pairs={{0,4},{1,5},{2,6},{3,7},{4,0},{5,1},{6,2},{7,3},{8,12},{9,13},{10,... | collective-permute-start | bytes 1572872 | tf_op jit(solution)/shard_map/ppermute | solution.py:316
  23.3 7.0 %collective-permute-start.3 = (f32[4,16,128]{2,1,0:T(8,128)S(1)}, f32[4,16,128]{2,1,0:T(8,128)S(1)}, u32[]{:S(2)}, u32[]{:S(2)}) collective-permute-start(f32[4,16,128]{2,1,0:T(8,128)S(1)} %get-tuple-element.44), channel_id=1, source_target_pairs={{0,96},{8,104},{16,112},{24,120},{32,128},{40,136},{48,144},{56,15... | collective-permute-start | bytes 98312 | tf_op jit(solution)/shard_map/ppermute | solution.py:343
  25.7 4.8 %collective-permute-start.4 = (f32[4,16,128]{2,1,0:T(8,128)S(1)}, f32[4,16,128]{2,1,0:T(8,128)S(1)}, u32[]{:S(2)}, u32[]{:S(2)}) collective-permute-start(f32[4,16,128]{2,1,0:T(8,128)S(1)} %get-tuple-element.44), channel_id=1, source_target_pairs={{0,192},{8,200},{16,208},{24,216},{32,224},{40,232},{48,240},{56,2... | collective-permute-start | bytes 98312 | tf_op jit(solution)/shard_map/ppermute | solution.py:343
  30.6 6.3 %collective-permute-start.9 = (f32[4,16,128]{2,1,0:T(8,128)S(1)}, f32[4,16,128]{2,1,0:T(8,128)S(1)}, u32[]{:S(2)}, u32[]{:S(2)}) collective-permute-start(f32[4,16,128]{2,1,0:T(8,128)S(1)} %get-tuple-element.46), channel_id=1, source_target_pairs={{0,16},{8,24},{16,0},{24,8},{32,48},{40,56},{48,32},{56,40},{64,80... | collective-permute-start | bytes 98312 | tf_op jit(solution)/shard_map/ppermute | solution.py:338
  32.8 10.4 %collective-permute-start.12 = (bf16[512,512]{1,0:T(8,128)(2,1)S(1)}, bf16[512,512]{1,0:T(8,128)(2,1)S(1)}, u32[]{:S(2)}, u32[]{:S(2)}) collective-permute-start(bf16[512,512]{1,0:T(8,128)(2,1)S(1)} %collective-permute-done.8.after_too.after.got_across), channel_id=1, source_target_pairs={{0,1},{1,2},{2,3},{3,0},{4,5},{5,6},{6,7},{7,4},{8,11},{9,8},{10,9... | collective-permute-start | bytes 1572872 | tf_op jit(solution)/shard_map/ppermute | solution.py:325
  40.6 12.3 %collective-permute-start.21 = (bf16[512,512]{1,0:T(8,128)(2,1)S(1)}, bf16[512,512]{1,0:T(8,128)(2,1)S(1)}, u32[]{:S(2)}, u32[]{:S(2)}) collective-permute-start(bf16[512,512]{1,0:T(8,128)(2,1)S(1)} %get-tuple-element.66), channel_id=1, source_target_pairs={{0,1},{1,2},{2,3},{3,0},{4,5},{5,6},{6,7},{7,4},{8,11},{9,8},{10,9... | collective-permute-start | bytes 1572872 | tf_op jit(solution)/shard_map/ppermute | solution.py:325
  46.2 15.5 %collective-permute-start.15 = (bf16[512,512]{1,0:T(8,128)(2,1)S(1)}, bf16[512,512]{1,0:T(8,128)(2,1)S(1)}, u32[]{:S(2)}, u32[]{:S(2)}) collective-permute-start(bf16[512,512]{1,0:T(8,128)(2,1)S(1)} %get-tuple-element.56.after), channel_id=1, source_target_pairs={{0,1},{1,2},{2,3},{3,0},{4,5},{5,6},{6,7},{7,4},{8,11},{9,8},{10,9... | collective-permute-start | bytes 1572872 | tf_op jit(solution)/shard_map/ppermute | solution.py:325
  47.4 5.5 %collective-permute-start.14 = (f32[4,16,128]{2,1,0:T(8,128)S(1)}, f32[4,16,128]{2,1,0:T(8,128)S(1)}, u32[]{:S(2)}, u32[]{:S(2)}) collective-permute-start(f32[4,16,128]{2,1,0:T(8,128)S(1)} %get-tuple-element.58.pair.after), channel_id=1, source_target_pairs={{0,16},{8,24},{16,0},{24,8},{32,48},{40,56},{48,32},{56,40},{64,80... | collective-permute-start | bytes 98312 | tf_op jit(solution)/shard_map/ppermute | solution.py:338
  49.6 14.5 %collective-permute-start.19 = (bf16[512,512]{1,0:T(8,128)(2,1)S(1)}, bf16[512,512]{1,0:T(8,128)(2,1)S(1)}, u32[]{:S(2)}, u32[]{:S(2)}) collective-permute-start(bf16[512,512]{1,0:T(8,128)(2,1)S(1)} %get-tuple-element.64), channel_id=1, source_target_pairs={{0,4},{1,5},{2,6},{3,7},{4,0},{5,1},{6,2},{7,3},{8,12},{9,13},{10,... | collective-permute-start | bytes 1572872 | tf_op jit(solution)/shard_map/ppermute | solution.py:316
  53.1 12.9 %collective-permute-start.22 = (bf16[512,512]{1,0:T(8,128)(2,1)S(1)}, bf16[512,512]{1,0:T(8,128)(2,1)S(1)}, u32[]{:S(2)}, u32[]{:S(2)}) collective-permute-start(bf16[512,512]{1,0:T(8,128)(2,1)S(1)} %shard_map.128), channel_id=1, source_target_pairs={{0,1},{1,2},{2,3},{3,0},{4,5},{5,6},{6,7},{7,4},{8,11},{9,8},{10,9... | collective-permute-start | bytes 1572872 | tf_op jit(solution)/shard_map/ppermute | solution.py:325
  53.8 5.6 %collective-permute-start.16 = (f32[4,16,128]{2,1,0:T(8,128)S(1)}, f32[4,16,128]{2,1,0:T(8,128)S(1)}, u32[]{:S(2)}, u32[]{:S(2)}) collective-permute-start(f32[4,16,128]{2,1,0:T(8,128)S(1)} %get-tuple-element.60.after.pair), channel_id=1, source_target_pairs={{0,224},{8,232},{16,240},{24,248},{32,0},{40,8},{48,16},{56,24},{6... | collective-permute-start | bytes 98312 | tf_op jit(solution)/shard_map/ppermute | solution.py:343
  56.7 5.0 %collective-permute-start.17 = (f32[4,16,128]{2,1,0:T(8,128)S(1)}, f32[4,16,128]{2,1,0:T(8,128)S(1)}, u32[]{:S(2)}, u32[]{:S(2)}) collective-permute-start(f32[4,16,128]{2,1,0:T(8,128)S(1)} %get-tuple-element.60.after.pair), channel_id=1, source_target_pairs={{0,192},{8,200},{16,208},{24,216},{32,224},{40,232},{48,240},{56,2... | collective-permute-start | bytes 98312 | tf_op jit(solution)/shard_map/ppermute | solution.py:343
  61.8 19.4 %collective-permute-start.18 = (bf16[512,512]{1,0:T(8,128)(2,1)S(1)}, bf16[512,512]{1,0:T(8,128)(2,1)S(1)}, u32[]{:S(2)}, u32[]{:S(2)}) collective-permute-start(bf16[512,512]{1,0:T(8,128)(2,1)S(1)} %shard_map.125), channel_id=1, source_target_pairs={{0,1},{1,2},{2,3},{3,0},{4,5},{5,6},{6,7},{7,4},{8,11},{9,8},{10,9... | collective-permute-start | bytes 1572872 | tf_op jit(solution)/shard_map/ppermute | solution.py:325
  64.2 17.0 %collective-permute-start.20 = (bf16[512,512]{1,0:T(8,128)(2,1)S(1)}, bf16[512,512]{1,0:T(8,128)(2,1)S(1)}, u32[]{:S(2)}, u32[]{:S(2)}) collective-permute-start(bf16[512,512]{1,0:T(8,128)(2,1)S(1)} %shard_map.127), channel_id=1, source_target_pairs={{0,3},{1,0},{2,1},{3,2},{4,7},{5,4},{6,5},{7,6},{8,9},{9,10},{10,1... | collective-permute-start | bytes 1572872 | tf_op jit(solution)/shard_map/ppermute | solution.py:325
  66.1 15.1 %collective-permute-start.23 = (bf16[512,512]{1,0:T(8,128)(2,1)S(1)}, bf16[512,512]{1,0:T(8,128)(2,1)S(1)}, u32[]{:S(2)}, u32[]{:S(2)}) collective-permute-start(bf16[512,512]{1,0:T(8,128)(2,1)S(1)} %shard_map.129), channel_id=1, source_target_pairs={{0,4},{1,5},{2,6},{3,7},{4,0},{5,1},{6,2},{7,3},{8,12},{9,13},{10,... | collective-permute-start | bytes 1572872 | tf_op jit(solution)/shard_map/ppermute | solution.py:316
  67.6 5.7 %collective-permute-start.24 = (f32[4,16,128]{2,1,0:T(8,128)S(1)}, f32[4,16,128]{2,1,0:T(8,128)S(1)}, u32[]{:S(2)}, u32[]{:S(2)}) collective-permute-start(f32[4,16,128]{2,1,0:T(8,128)S(1)} %get-tuple-element.63.after), channel_id=1, source_target_pairs={{0,160},{8,168},{16,176},{24,184},{32,192},{40,200},{48,208},{56,2... | collective-permute-start | bytes 98312 | tf_op jit(solution)/shard_map/ppermute | solution.py:343
  71.1 6.0 %collective-permute-start.25 = (f32[4,16,128]{2,1,0:T(8,128)S(1)}, f32[4,16,128]{2,1,0:T(8,128)S(1)}, u32[]{:S(2)}, u32[]{:S(2)}) collective-permute-start(f32[4,16,128]{2,1,0:T(8,128)S(1)} %get-tuple-element.63.after), channel_id=1, source_target_pairs={{0,64},{8,72},{16,80},{24,88},{32,96},{40,104},{48,112},{56,120},{... | collective-permute-start | bytes 98312 | tf_op jit(solution)/shard_map/ppermute | solution.py:343
  (8 other events, 81.9 us)

commit v5 on v4

--- a/solution.py
+++ b/solution.py
@@ -351,7 +351,6 @@
 
     across = shift_x(cotangent)
     behind = along_y(cotangent, 1)
-    ahead = along_y(cotangent, -1)
 
     deep, table, state = (DEEP, F32), (TABLE, F32), (STATE_SHAPE, F32)
     gated = (key.astype(F32) * value.astype(F32)).astype(BF16)
@@ -359,6 +358,8 @@
         gate_kernel, [state] * 4 + [table, state], [deep, table], 2.4, 6, gated, fading, amplitude
     )
     pair, before = small(pair_kernel, False, rates, total, other_core(total))
+    late, _ = lax.optimization_barrier((cotangent, pair))
+    ahead = along_y(late, -1)
     offs = earlier(pair, 1, False), earlier(pair, 2, False)
     s_across, s_behind = call(
         relay_kernel, [(BLOCK, BF16)] * 2, [], 1.0, 4, across, behind, ahead, *offs

time: 82.5 us -> 86.3 us (1.046)
  starting transfers between devices: 37.9 us -> 41.8 us
    ppermute x8, starting transfers between devices: 15.8 us -> 20.2 us  [earlier(): lax.ppermute(value, 'ctx', ctx_perm(lambda z, h, c: (z + move, h, c)))]
    ppermute x10, waiting for transfers between devices: 2.8 us -> 4.69 us  [along_y(): return lax.ppermute(value, ('ctx', 'tp'), pairs)]
    ppermute x8, waiting for transfers between devices: 14.8 us -> 13.5 us  [earlier(): lax.ppermute(value, 'ctx', ctx_perm(lambda z, h, c: (z + move, h, c)))]
    ppermute x2, waiting for transfers between devices: 1.81 us -> 0.55 us  [other_core(): return lax.ppermute(value, 'ctx', ctx_perm(lambda z, h, c: (z, h, c + 1)))]
    ppermute x4, starting transfers between devices: 6.63 us -> 5.71 us  [shift_x(): return lax.ppermute(value, 'tp', [(at, (at + 4) % 8) for at in range(8)])]
    ppermute x2, waiting for transfers between devices: 2.01 us -> 2.9 us  [other_half(): return lax.ppermute(value, 'ctx', ctx_perm(lambda z, h, c: (z, h + 1, c)))]
  transfers between devices with their start and end apart: 26 -> 26, of which waited for: 13 -> 14; matrix products, arithmetic and copies ran while one was open for 3% -> 0% of each run, Pallas kernels for 21% -> 18%
where the time goes in v5:
time: 86.3 us; the launch traced here: 86.1 us
  starting transfers between devices  41.8 us (48%)
  waiting for transfers between devices  23.2 us (27%)
  Pallas kernels  18.1 us (21%)
  other arithmetic  2.14 us (2%)
    ppermute x8, starting transfers between devices, earlier(): lax.ppermute(value, 'ctx', ctx_perm(lambda z, h, c: (z + move, h, c)))  20.2 us
    pallas_call x21, Pallas kernels, call(): pl.pallas_call(kernel, out_shape=[jax.ShapeDtypeStruct(shape, kind) for s...  18.1 us
    ppermute x8, waiting for transfers between devices, earlier(): lax.ppermute(value, 'ctx', ctx_perm(lambda z, h, c: (z + move, h, c)))  13.5 us
    ppermute x10, starting transfers between devices, along_y(): return lax.ppermute(value, ('ctx', 'tp'), pairs)  12.1 us
    ppermute x4, starting transfers between devices, shift_x(): return lax.ppermute(value, 'tp', [(at, (at + 4) % 8) for at in range(8)])  5.71 us
    ppermute x10, waiting for transfers between devices, along_y(): return lax.ppermute(value, ('ctx', 'tp'), pairs)  4.69 us
    ppermute x2, starting transfers between devices, other_half(): return lax.ppermute(value, 'ctx', ctx_perm(lambda z, h, c: (z, h + 1, c)))  3.71 us
    ppermute x2, waiting for transfers between devices, other_half(): return lax.ppermute(value, 'ctx', ctx_perm(lambda z, h, c: (z, h + 1, c)))  2.9 us
  transfers between devices with their start and end apart: 26, of which 14 were waited for; matrix products, arithmetic and copies ran while one was open for 0% of the time, Pallas kernels for 18%

profile of v5, /device:TPU:2, one launch (start us, length us, event | category | flops | bytes accessed | tf_op | source)
XLA Modules:
  0.0 86.1 jit_solution(11897012368516637255)
XLA Ops:
  4.3 2.4 %collective-permute-start.5 = (bf16[512,512]{1,0:T(8,128)(2,1)S(1)}, bf16[512,512]{1,0:T(8,128)(2,1)S(1)}, u32[]{:S(2)}, u32[]{:S(2)}) collective-permute-start(bf16[512,512]{1,0:T(8,128)(2,1)S(1)} %copy-done.3), channel_id=1, source_target_pairs={{0,4},{1,5},{2,6},{3,7},{4,0},{5,1},{6,2},{7,3},{8,12},{9,13},{10,... | collective-permute-start | bytes 1572872 | tf_op jit(solution)/shard_map/ppermute | solution.py:316
  6.7 3.3 %collective-permute-start.7 = (bf16[512,512]{1,0:T(8,128)(2,1)S(1)}, bf16[512,512]{1,0:T(8,128)(2,1)S(1)}, u32[]{:S(2)}, u32[]{:S(2)}) collective-permute-start(bf16[512,512]{1,0:T(8,128)(2,1)S(1)} %copy-done.3), channel_id=1, source_target_pairs={{0,3},{1,0},{2,1},{3,2},{4,7},{5,4},{6,5},{7,6},{8,9},{9,10},{10,1... | collective-permute-start | bytes 1572872 | tf_op jit(solution)/shard_map/ppermute | solution.py:325
  10.5 3.3 %collective-permute-start.2 = (f32[4,16,128]{2,1,0:T(8,128)S(1)}, f32[4,16,128]{2,1,0:T(8,128)S(1)}, u32[]{:S(2)}, u32[]{:S(2)}) collective-permute-start(f32[4,16,128]{2,1,0:T(8,128)S(1)} %get-tuple-element.43.pair), channel_id=1, source_target_pairs={{0,64},{8,72},{16,80},{24,88},{32,96},{40,104},{48,112},{56,120},{... | collective-permute-start | bytes 98312 | tf_op jit(solution)/shard_map/ppermute | solution.py:343
  13.8 2.9 %collective-permute-done.1.one_off.after = f32[4,16,128]{2,1,0:T(8,128)S(1)} collective-permute-done((f32[4,16,128]{2,1,0:T(8,128)S(1)}, f32[4,16,128]{2,1,0:T(8,128)S(1)}, u32[]{:S(2)}, u32[]{:S(2)}) %collective-permute-start.1) | collective-permute-done | bytes 32800 | tf_op jit(solution)/shard_map/ppermute | solution.py:343
  19.1 3.2 %collective-permute-done.6.behind = bf16[512,512]{1,0:T(8,128)(2,1)S(1)} collective-permute-done((bf16[512,512]{1,0:T(8,128)(2,1)S(1)}, bf16[512,512]{1,0:T(8,128)(2,1)S(1)}, u32[]{:S(2)}, u32[]{:S(2)}) %collective-permute-start.6) | collective-permute-done | bytes 524320 | tf_op jit(solution)/shard_map/ppermute | solution.py:325
  24.0 4.7 %collective-permute-start.3 = (f32[4,16,128]{2,1,0:T(8,128)S(1)}, f32[4,16,128]{2,1,0:T(8,128)S(1)}, u32[]{:S(2)}, u32[]{:S(2)}) collective-permute-start(f32[4,16,128]{2,1,0:T(8,128)S(1)} %get-tuple-element.45), channel_id=1, source_target_pairs={{0,96},{8,104},{16,112},{24,120},{32,128},{40,136},{48,144},{56,15... | collective-permute-start | bytes 98312 | tf_op jit(solution)/shard_map/ppermute | solution.py:343
  28.7 1.8 %collective-permute-start.4 = (f32[4,16,128]{2,1,0:T(8,128)S(1)}, f32[4,16,128]{2,1,0:T(8,128)S(1)}, u32[]{:S(2)}, u32[]{:S(2)}) collective-permute-start(f32[4,16,128]{2,1,0:T(8,128)S(1)} %get-tuple-element.45), channel_id=1, source_target_pairs={{0,192},{8,200},{16,208},{24,216},{32,224},{40,232},{48,240},{56,2... | collective-permute-start | bytes 98312 | tf_op jit(solution)/shard_map/ppermute | solution.py:343
  32.7 1.8 %collective-permute-done.4.six_off = f32[4,16,128]{2,1,0:T(8,128)S(1)} collective-permute-done((f32[4,16,128]{2,1,0:T(8,128)S(1)}, f32[4,16,128]{2,1,0:T(8,128)S(1)}, u32[]{:S(2)}, u32[]{:S(2)}) %collective-permute-start.4) | collective-permute-done | bytes 32800 | tf_op jit(solution)/shard_map/ppermute | solution.py:343
  34.6 2.2 %collective-permute-start.9 = (f32[4,16,128]{2,1,0:T(8,128)S(1)}, f32[4,16,128]{2,1,0:T(8,128)S(1)}, u32[]{:S(2)}, u32[]{:S(2)}) collective-permute-start(f32[4,16,128]{2,1,0:T(8,128)S(1)} %get-tuple-element.48), channel_id=1, source_target_pairs={{0,16},{8,24},{16,0},{24,8},{32,48},{40,56},{48,32},{56,40},{64,80... | collective-permute-start | bytes 98312 | tf_op jit(solution)/shard_map/ppermute | solution.py:338
  36.8 1.9 %collective-permute-start.12 = (bf16[512,512]{1,0:T(8,128)(2,1)S(1)}, bf16[512,512]{1,0:T(8,128)(2,1)S(1)}, u32[]{:S(2)}, u32[]{:S(2)}) collective-permute-start(bf16[512,512]{1,0:T(8,128)(2,1)S(1)} %collective-permute-done.8.after_too.after.got_across), channel_id=1, source_target_pairs={{0,1},{1,2},{2,3},{3,0},{4,5},{5,6},{6,7},{7,4},{8,11},{9,8},{10,9... | collective-permute-start | bytes 1572872 | tf_op jit(solution)/shard_map/ppermute | solution.py:325
  40.1 3.0 %shard_map.117 = (f32[512,512]{1,0:T(8,128)S(1)}, bf16[512,512]{1,0:T(8,128)(2,1)S(1)}) custom-call(f32[4,16,128]{2,1,0:T(8,128)S(1)} %get-tuple-element.41.rates, f32[4,16,128]{2,1,0:T(8,128)S(1)} %collective-permute-done.9.other, f32[4,16,128]{2,1,0:T(8,128)S(1)} %get-tuple-element.49.over, f32[4,16,128]{2,1,0:T(8,128)S(1)} %get-tuple-element.50.before, ...), custom_call_target="tpu_custom_call" | custom-call | flops 4950000128 | bytes 13500000 | tf_op jit(solution)/shard_map/pallas_call | solution.py:292
  43.8 1.9 %collective-permute-start.21 = (bf16[512,512]{1,0:T(8,128)(2,1)S(1)}, bf16[512,512]{1,0:T(8,128)(2,1)S(1)}, u32[]{:S(2)}, u32[]{:S(2)}) collective-permute-start(bf16[512,512]{1,0:T(8,128)(2,1)S(1)} %get-tuple-element.68), channel_id=1, source_target_pairs={{0,1},{1,2},{2,3},{3,0},{4,5},{5,6},{6,7},{7,4},{8,11},{9,8},{10,9... | collective-permute-start | bytes 1572872 | tf_op jit(solution)/shard_map/ppermute | solution.py:325
  47.2 3.0 %shard_map.120 = (bf16[512,512]{1,0:T(8,128)(2,1)}, bf16[512,512]{1,0:T(8,128)(2,1)S(1)}, f32[4,128,128]{2,1,0:T(8,128)S(1)}, f32[4,16,128]{2,1,0:T(8,128)S(1)}) custom-call(bf16[512,4096]{1,0:T(8,128)(2,1)S(1)} %copy-done, f32[512,512]{1,0:T(8,128)S(1)} %shard_map.118.acc, bf16[512,512]{1,0:T(8,128)(2,1)S(1)} %collective-permute-done.12.far, ...), custom_call_target="tpu_custom_call" | custom-call | flops 6600000000 | bytes 18000000 | tf_op jit(solution)/shard_map/pallas_call | solution.py:292
  51.4 1.5 %collective-permute-start.14 = (f32[4,16,128]{2,1,0:T(8,128)S(1)}, f32[4,16,128]{2,1,0:T(8,128)S(1)}, u32[]{:S(2)}, u32[]{:S(2)}) collective-permute-start(f32[4,16,128]{2,1,0:T(8,128)S(1)} %get-tuple-element.60.pair.after), channel_id=1, source_target_pairs={{0,16},{8,24},{16,0},{24,8},{32,48},{40,56},{48,32},{56,40},{64,80... | collective-permute-start | bytes 98312 | tf_op jit(solution)/shard_map/ppermute | solution.py:338
  54.4 2.5 %collective-permute-done.14.other = f32[4,16,128]{2,1,0:T(8,128)S(1)} collective-permute-done((f32[4,16,128]{2,1,0:T(8,128)S(1)}, f32[4,16,128]{2,1,0:T(8,128)S(1)}, u32[]{:S(2)}, u32[]{:S(2)}) %collective-permute-start.14) | collective-permute-done | bytes 32800 | tf_op jit(solution)/shard_map/ppermute | solution.py:338
  57.8 2.3 %collective-permute-start.16 = (f32[4,16,128]{2,1,0:T(8,128)S(1)}, f32[4,16,128]{2,1,0:T(8,128)S(1)}, u32[]{:S(2)}, u32[]{:S(2)}) collective-permute-start(f32[4,16,128]{2,1,0:T(8,128)S(1)} %get-tuple-element.62.after.pair), channel_id=1, source_target_pairs={{0,224},{8,232},{16,240},{24,248},{32,0},{40,8},{48,16},{56,24},{6... | collective-permute-start | bytes 98312 | tf_op jit(solution)/shard_map/ppermute | solution.py:343
  60.1 1.8 %collective-permute-start.17 = (f32[4,16,128]{2,1,0:T(8,128)S(1)}, f32[4,16,128]{2,1,0:T(8,128)S(1)}, u32[]{:S(2)}, u32[]{:S(2)}) collective-permute-start(f32[4,16,128]{2,1,0:T(8,128)S(1)} %get-tuple-element.62.after.pair), channel_id=1, source_target_pairs={{0,192},{8,200},{16,208},{24,216},{32,224},{40,232},{48,240},{56,2... | collective-permute-start | bytes 98312 | tf_op jit(solution)/shard_map/ppermute | solution.py:343
  63.2 1.8 %collective-permute-done.17.two_off = f32[4,16,128]{2,1,0:T(8,128)S(1)} collective-permute-done((f32[4,16,128]{2,1,0:T(8,128)S(1)}, f32[4,16,128]{2,1,0:T(8,128)S(1)}, u32[]{:S(2)}, u32[]{:S(2)}) %collective-permute-start.17) | collective-permute-done | bytes 32800 | tf_op jit(solution)/shard_map/ppermute | solution.py:343
  65.2 1.7 %collective-permute-start.18 = (bf16[512,512]{1,0:T(8,128)(2,1)S(1)}, bf16[512,512]{1,0:T(8,128)(2,1)S(1)}, u32[]{:S(2)}, u32[]{:S(2)}) collective-permute-start(bf16[512,512]{1,0:T(8,128)(2,1)S(1)} %shard_map.125), channel_id=1, source_target_pairs={{0,1},{1,2},{2,3},{3,0},{4,5},{5,6},{6,7},{7,4},{8,11},{9,8},{10,9... | collective-permute-start | bytes 1572872 | tf_op jit(solution)/shard_map/ppermute | solution.py:325
  69.1 1.5 %collective-permute-start.23 = (bf16[512,512]{1,0:T(8,128)(2,1)S(1)}, bf16[512,512]{1,0:T(8,128)(2,1)S(1)}, u32[]{:S(2)}, u32[]{:S(2)}) collective-permute-start(bf16[512,512]{1,0:T(8,128)(2,1)S(1)} %shard_map.129), channel_id=1, source_target_pairs={{0,4},{1,5},{2,6},{3,7},{4,0},{5,1},{6,2},{7,3},{8,12},{9,13},{10,... | collective-permute-start | bytes 1572872 | tf_op jit(solution)/shard_map/ppermute | solution.py:316
  70.6 4.4 %collective-permute-start.24 = (f32[4,16,128]{2,1,0:T(8,128)S(1)}, f32[4,16,128]{2,1,0:T(8,128)S(1)}, u32[]{:S(2)}, u32[]{:S(2)}) collective-permute-start(f32[4,16,128]{2,1,0:T(8,128)S(1)} %get-tuple-element.65.after), channel_id=1, source_target_pairs={{0,160},{8,168},{16,176},{24,184},{32,192},{40,200},{48,208},{56,2... | collective-permute-start | bytes 98312 | tf_op jit(solution)/shard_map/ppermute | solution.py:343
  75.0 1.5 %collective-permute-start.25 = (f32[4,16,128]{2,1,0:T(8,128)S(1)}, f32[4,16,128]{2,1,0:T(8,128)S(1)}, u32[]{:S(2)}, u32[]{:S(2)}) collective-permute-start(f32[4,16,128]{2,1,0:T(8,128)S(1)} %get-tuple-element.65.after), channel_id=1, source_target_pairs={{0,64},{8,72},{16,80},{24,88},{32,96},{40,104},{48,112},{56,120},{... | collective-permute-start | bytes 98312 | tf_op jit(solution)/shard_map/ppermute | solution.py:343
  77.2 3.8 %collective-permute-done.25.six_off = f32[4,16,128]{2,1,0:T(8,128)S(1)} collective-permute-done((f32[4,16,128]{2,1,0:T(8,128)S(1)}, f32[4,16,128]{2,1,0:T(8,128)S(1)}, u32[]{:S(2)}, u32[]{:S(2)}) %collective-permute-start.25) | collective-permute-done | bytes 32800 | tf_op jit(solution)/shard_map/ppermute | solution.py:343
  81.0 4.0 %shard_map.131 = (bf16[512,512]{1,0:T(8,128)(2,1)}, bf16[512,512]{1,0:T(8,128)(2,1)}) custom-call(f32[4,16,128]{2,1,0:T(8,128)S(1)} %get-tuple-element.41.rates, f32[4,16,128]{2,1,0:T(8,128)S(1)} %get-tuple-element.72.two, f32[4,16,128]{2,1,0:T(8,128)S(1)} %collective-permute-done.24.three_off, f32[4,16,128]{2,1,0:T(8,128)S(1)} %collective-permute-done.25.six_off, ...), custom_call_target="tpu_custom_call" | custom-call | flops 4950000128 | bytes 13500000 | tf_op jit(solution)/shard_map/pallas_call | solution.py:292
  (63 shorter events, 23.2 us)
Async XLA Ops:
  4.3 14.8 %collective-permute-start.5 = (bf16[512,512]{1,0:T(8,128)(2,1)S(1)}, bf16[512,512]{1,0:T(8,128)(2,1)S(1)}, u32[]{:S(2)}, u32[]{:S(2)}) collective-permute-start(bf16[512,512]{1,0:T(8,128)(2,1)S(1)} %copy-done.3), channel_id=1, source_target_pairs={{0,4},{1,5},{2,6},{3,7},{4,0},{5,1},{6,2},{7,3},{8,12},{9,13},{10,... | collective-permute-start | bytes 1572872 | tf_op jit(solution)/shard_map/ppermute | solution.py:316
  6.6 15.7 %collective-permute-start.6 = (bf16[512,512]{1,0:T(8,128)(2,1)S(1)}, bf16[512,512]{1,0:T(8,128)(2,1)S(1)}, u32[]{:S(2)}, u32[]{:S(2)}) collective-permute-start(bf16[512,512]{1,0:T(8,128)(2,1)S(1)} %copy-done.3), channel_id=1, source_target_pairs={{0,1},{1,2},{2,3},{3,0},{4,5},{5,6},{6,7},{7,4},{8,11},{9,8},{10,9... | collective-permute-start | bytes 1572872 | tf_op jit(solution)/shard_map/ppermute | solution.py:325
  6.7 15.7 %collective-permute-start.7 = (bf16[512,512]{1,0:T(8,128)(2,1)S(1)}, bf16[512,512]{1,0:T(8,128)(2,1)S(1)}, u32[]{:S(2)}, u32[]{:S(2)}) collective-permute-start(bf16[512,512]{1,0:T(8,128)(2,1)S(1)} %copy-done.3), channel_id=1, source_target_pairs={{0,3},{1,0},{2,1},{3,2},{4,7},{5,4},{6,5},{7,6},{8,9},{9,10},{10,1... | collective-permute-start | bytes 1572872 | tf_op jit(solution)/shard_map/ppermute | solution.py:325
  10.0 6.7 %collective-permute-start.1 = (f32[4,16,128]{2,1,0:T(8,128)S(1)}, f32[4,16,128]{2,1,0:T(8,128)S(1)}, u32[]{:S(2)}, u32[]{:S(2)}) collective-permute-start(f32[4,16,128]{2,1,0:T(8,128)S(1)} %get-tuple-element.43.pair), channel_id=1, source_target_pairs={{0,32},{8,40},{16,48},{24,56},{32,64},{40,72},{48,80},{56,88},{64,... | collective-permute-start | bytes 98312 | tf_op jit(solution)/shard_map/ppermute | solution.py:343
  10.5 7.6 %collective-permute-start.2 = (f32[4,16,128]{2,1,0:T(8,128)S(1)}, f32[4,16,128]{2,1,0:T(8,128)S(1)}, u32[]{:S(2)}, u32[]{:S(2)}) collective-permute-start(f32[4,16,128]{2,1,0:T(8,128)S(1)} %get-tuple-element.43.pair), channel_id=1, source_target_pairs={{0,64},{8,72},{16,80},{24,88},{32,96},{40,104},{48,112},{56,120},{... | collective-permute-start | bytes 98312 | tf_op jit(solution)/shard_map/ppermute | solution.py:343
  22.4 12.1 %collective-permute-start.8 = (bf16[512,512]{1,0:T(8,128)(2,1)S(1)}, bf16[512,512]{1,0:T(8,128)(2,1)S(1)}, u32[]{:S(2)}, u32[]{:S(2)}) collective-permute-start(bf16[512,512]{1,0:T(8,128)(2,1)S(1)} %get-tuple-element.47.after), channel_id=1, source_target_pairs={{0,1},{1,2},{2,3},{3,0},{4,5},{5,6},{6,7},{7,4},{8,11},{9,8},{10,9... | collective-permute-start | bytes 1572872 | tf_op jit(solution)/shard_map/ppermute | solution.py:325
  22.5 16.2 %collective-permute-start.10 = (bf16[512,512]{1,0:T(8,128)(2,1)S(1)}, bf16[512,512]{1,0:T(8,128)(2,1)S(1)}, u32[]{:S(2)}, u32[]{:S(2)}) collective-permute-start(bf16[512,512]{1,0:T(8,128)(2,1)S(1)} %get-tuple-element.56), channel_id=1, source_target_pairs={{0,1},{1,2},{2,3},{3,0},{4,5},{5,6},{6,7},{7,4},{8,11},{9,8},{10,9... | collective-permute-start | bytes 1572872 | tf_op jit(solution)/shard_map/ppermute | solution.py:325
  22.9 15.7 %collective-permute-start.11 = (bf16[512,512]{1,0:T(8,128)(2,1)S(1)}, bf16[512,512]{1,0:T(8,128)(2,1)S(1)}, u32[]{:S(2)}, u32[]{:S(2)}) collective-permute-start(bf16[512,512]{1,0:T(8,128)(2,1)S(1)} %collective-permute-done.7.ahead), channel_id=1, source_target_pairs={{0,4},{1,5},{2,6},{3,7},{4,0},{5,1},{6,2},{7,3},{8,12},{9,13},{10,... | collective-permute-start | bytes 1572872 | tf_op jit(solution)/shard_map/ppermute | solution.py:316
  24.0 8.7 %collective-permute-start.3 = (f32[4,16,128]{2,1,0:T(8,128)S(1)}, f32[4,16,128]{2,1,0:T(8,128)S(1)}, u32[]{:S(2)}, u32[]{:S(2)}) collective-permute-start(f32[4,16,128]{2,1,0:T(8,128)S(1)} %get-tuple-element.45), channel_id=1, source_target_pairs={{0,96},{8,104},{16,112},{24,120},{32,128},{40,136},{48,144},{56,15... | collective-permute-start | bytes 98312 | tf_op jit(solution)/shard_map/ppermute | solution.py:343
  28.7 5.8 %collective-permute-start.4 = (f32[4,16,128]{2,1,0:T(8,128)S(1)}, f32[4,16,128]{2,1,0:T(8,128)S(1)}, u32[]{:S(2)}, u32[]{:S(2)}) collective-permute-start(f32[4,16,128]{2,1,0:T(8,128)S(1)} %get-tuple-element.45), channel_id=1, source_target_pairs={{0,192},{8,200},{16,208},{24,216},{32,224},{40,232},{48,240},{56,2... | collective-permute-start | bytes 98312 | tf_op jit(solution)/shard_map/ppermute | solution.py:343
  34.6 5.5 %collective-permute-start.9 = (f32[4,16,128]{2,1,0:T(8,128)S(1)}, f32[4,16,128]{2,1,0:T(8,128)S(1)}, u32[]{:S(2)}, u32[]{:S(2)}) collective-permute-start(f32[4,16,128]{2,1,0:T(8,128)S(1)} %get-tuple-element.48), channel_id=1, source_target_pairs={{0,16},{8,24},{16,0},{24,8},{32,48},{40,56},{48,32},{56,40},{64,80... | collective-permute-start | bytes 98312 | tf_op jit(solution)/shard_map/ppermute | solution.py:338
  36.8 10.4 %collective-permute-start.12 = (bf16[512,512]{1,0:T(8,128)(2,1)S(1)}, bf16[512,512]{1,0:T(8,128)(2,1)S(1)}, u32[]{:S(2)}, u32[]{:S(2)}) collective-permute-start(bf16[512,512]{1,0:T(8,128)(2,1)S(1)} %collective-permute-done.8.after_too.after.got_across), channel_id=1, source_target_pairs={{0,1},{1,2},{2,3},{3,0},{4,5},{5,6},{6,7},{7,4},{8,11},{9,8},{10,9... | collective-permute-start | bytes 1572872 | tf_op jit(solution)/shard_map/ppermute | solution.py:325
  43.8 13.1 %collective-permute-start.21 = (bf16[512,512]{1,0:T(8,128)(2,1)S(1)}, bf16[512,512]{1,0:T(8,128)(2,1)S(1)}, u32[]{:S(2)}, u32[]{:S(2)}) collective-permute-start(bf16[512,512]{1,0:T(8,128)(2,1)S(1)} %get-tuple-element.68), channel_id=1, source_target_pairs={{0,1},{1,2},{2,3},{3,0},{4,5},{5,6},{6,7},{7,4},{8,11},{9,8},{10,9... | collective-permute-start | bytes 1572872 | tf_op jit(solution)/shard_map/ppermute | solution.py:325
  50.2 14.9 %collective-permute-start.15 = (bf16[512,512]{1,0:T(8,128)(2,1)S(1)}, bf16[512,512]{1,0:T(8,128)(2,1)S(1)}, u32[]{:S(2)}, u32[]{:S(2)}) collective-permute-start(bf16[512,512]{1,0:T(8,128)(2,1)S(1)} %get-tuple-element.58.after), channel_id=1, source_target_pairs={{0,1},{1,2},{2,3},{3,0},{4,5},{5,6},{6,7},{7,4},{8,11},{9,8},{10,9... | collective-permute-start | bytes 1572872 | tf_op jit(solution)/shard_map/ppermute | solution.py:325
  51.4 5.5 %collective-permute-start.14 = (f32[4,16,128]{2,1,0:T(8,128)S(1)}, f32[4,16,128]{2,1,0:T(8,128)S(1)}, u32[]{:S(2)}, u32[]{:S(2)}) collective-permute-start(f32[4,16,128]{2,1,0:T(8,128)S(1)} %get-tuple-element.60.pair.after), channel_id=1, source_target_pairs={{0,16},{8,24},{16,0},{24,8},{32,48},{40,56},{48,32},{56,40},{64,80... | collective-permute-start | bytes 98312 | tf_op jit(solution)/shard_map/ppermute | solution.py:338
  53.6 13.8 %collective-permute-start.19 = (bf16[512,512]{1,0:T(8,128)(2,1)S(1)}, bf16[512,512]{1,0:T(8,128)(2,1)S(1)}, u32[]{:S(2)}, u32[]{:S(2)}) collective-permute-start(bf16[512,512]{1,0:T(8,128)(2,1)S(1)} %get-tuple-element.66), channel_id=1, source_target_pairs={{0,4},{1,5},{2,6},{3,7},{4,0},{5,1},{6,2},{7,3},{8,12},{9,13},{10,... | collective-permute-start | bytes 1572872 | tf_op jit(solution)/shard_map/ppermute | solution.py:316
  57.1 11.9 %collective-permute-start.22 = (bf16[512,512]{1,0:T(8,128)(2,1)S(1)}, bf16[512,512]{1,0:T(8,128)(2,1)S(1)}, u32[]{:S(2)}, u32[]{:S(2)}) collective-permute-start(bf16[512,512]{1,0:T(8,128)(2,1)S(1)} %shard_map.128), channel_id=1, source_target_pairs={{0,1},{1,2},{2,3},{3,0},{4,5},{5,6},{6,7},{7,4},{8,11},{9,8},{10,9... | collective-permute-start | bytes 1572872 | tf_op jit(solution)/shard_map/ppermute | solution.py:325
  57.8 5.4 %collective-permute-start.16 = (f32[4,16,128]{2,1,0:T(8,128)S(1)}, f32[4,16,128]{2,1,0:T(8,128)S(1)}, u32[]{:S(2)}, u32[]{:S(2)}) collective-permute-start(f32[4,16,128]{2,1,0:T(8,128)S(1)} %get-tuple-element.62.after.pair), channel_id=1, source_target_pairs={{0,224},{8,232},{16,240},{24,248},{32,0},{40,8},{48,16},{56,24},{6... | collective-permute-start | bytes 98312 | tf_op jit(solution)/shard_map/ppermute | solution.py:343
  60.1 4.9 %collective-permute-start.17 = (f32[4,16,128]{2,1,0:T(8,128)S(1)}, f32[4,16,128]{2,1,0:T(8,128)S(1)}, u32[]{:S(2)}, u32[]{:S(2)}) collective-permute-start(f32[4,16,128]{2,1,0:T(8,128)S(1)} %get-tuple-element.62.after.pair), channel_id=1, source_target_pairs={{0,192},{8,200},{16,208},{24,216},{32,224},{40,232},{48,240},{56,2... | collective-permute-start | bytes 98312 | tf_op jit(solution)/shard_map/ppermute | solution.py:343
  65.2 19.8 %collective-permute-start.18 = (bf16[512,512]{1,0:T(8,128)(2,1)S(1)}, bf16[512,512]{1,0:T(8,128)(2,1)S(1)}, u32[]{:S(2)}, u32[]{:S(2)}) collective-permute-start(bf16[512,512]{1,0:T(8,128)(2,1)S(1)} %shard_map.125), channel_id=1, source_target_pairs={{0,1},{1,2},{2,3},{3,0},{4,5},{5,6},{6,7},{7,4},{8,11},{9,8},{10,9... | collective-permute-start | bytes 1572872 | tf_op jit(solution)/shard_map/ppermute | solution.py:325
  67.5 17.5 %collective-permute-start.20 = (bf16[512,512]{1,0:T(8,128)(2,1)S(1)}, bf16[512,512]{1,0:T(8,128)(2,1)S(1)}, u32[]{:S(2)}, u32[]{:S(2)}) collective-permute-start(bf16[512,512]{1,0:T(8,128)(2,1)S(1)} %shard_map.127), channel_id=1, source_target_pairs={{0,3},{1,0},{2,1},{3,2},{4,7},{5,4},{6,5},{7,6},{8,9},{9,10},{10,1... | collective-permute-start | bytes 1572872 | tf_op jit(solution)/shard_map/ppermute | solution.py:325
  69.1 16.0 %collective-permute-start.23 = (bf16[512,512]{1,0:T(8,128)(2,1)S(1)}, bf16[512,512]{1,0:T(8,128)(2,1)S(1)}, u32[]{:S(2)}, u32[]{:S(2)}) collective-permute-start(bf16[512,512]{1,0:T(8,128)(2,1)S(1)} %shard_map.129), channel_id=1, source_target_pairs={{0,4},{1,5},{2,6},{3,7},{4,0},{5,1},{6,2},{7,3},{8,12},{9,13},{10,... | collective-permute-start | bytes 1572872 | tf_op jit(solution)/shard_map/ppermute | solution.py:316
  70.6 6.6 %collective-permute-start.24 = (f32[4,16,128]{2,1,0:T(8,128)S(1)}, f32[4,16,128]{2,1,0:T(8,128)S(1)}, u32[]{:S(2)}, u32[]{:S(2)}) collective-permute-start(f32[4,16,128]{2,1,0:T(8,128)S(1)} %get-tuple-element.65.after), channel_id=1, source_target_pairs={{0,160},{8,168},{16,176},{24,184},{32,192},{40,200},{48,208},{56,2... | collective-permute-start | bytes 98312 | tf_op jit(solution)/shard_map/ppermute | solution.py:343
  75.0 6.0 %collective-permute-start.25 = (f32[4,16,128]{2,1,0:T(8,128)S(1)}, f32[4,16,128]{2,1,0:T(8,128)S(1)}, u32[]{:S(2)}, u32[]{:S(2)}) collective-permute-start(f32[4,16,128]{2,1,0:T(8,128)S(1)} %get-tuple-element.65.after), channel_id=1, source_target_pairs={{0,64},{8,72},{16,80},{24,88},{32,96},{40,104},{48,112},{56,120},{... | collective-permute-start | bytes 98312 | tf_op jit(solution)/shard_map/ppermute | solution.py:343
  (8 other events, 75.6 us)
